TPU v7x, 512 devices: a whole 4x8x8 slice. The times are simulated.
512 devices in a mesh: tm: 16 (over x, z_hi, core), cell: 32 (over y, z_lo).
Axes of the slice: x: 4, y: 8, z: 8 (z_hi: 2, z_lo: 4; z = z_hi * 4 + z_lo), core: 2. Of those that a mesh axis runs over, the one named last changes fastest.
Arguments:
- sensitivity: bfloat16 [2048, 16, 16384], P(None, 'tm', 'cell'), may hold values from -0.25 to 0.25
- duals: bfloat16 [2048, 128], P(('tm', 'cell')), may hold values from -6 to 6
- time_cov: float32 [16, 16], replicated, may hold values from 0.05 to 0.5
- cell_coords: int32 [2, 16384], P(None, 'cell'), may hold values from 0 to 127, as said below
- obs_time: int32 [2048], replicated, may hold values from 0 to 15
- obs_owner: int32 [2048], replicated, may hold values from 0 to 2047, each once
Outputs:
- product: float32 [2048, 128], P(('tm', 'cell'))
Inputs may be any that keep to these rules, and one draw needn't show every extreme that they name: `cell_coords`: every cell has its own grid position; rows lie below 128 and columns below 128. `obs_owner`: every observation stands in exactly one slot.
All inputs are finite; a program needn't handle non-finite values.
Results may differ from a plain program's by a relative error of at most 0.0049.
Values may be sent and summed in bfloat16 or wider, within the bound.
No kernel may reach another device: no remote copies, remote signals or barrier semaphores. Data moves between devices by JAX's collectives and lax.ppermute only.
A program may use at most 64 MiB of HBM per device.

v0:
```python
import jax
import jax.numpy as jnp
from jax import lax
from jax.sharding import Mesh
from jax.sharding import PartitionSpec as P

LSCALE = 4
TM = ("tm_0", "tm_1", "tm_2")
TM_CELL = ("tm_0", "tm_1", "tm_2", "cell_0", "cell_1")
CELL = ("cell_0", "cell_1")


def laid_out(pieces, dim):
    pieces = jnp.moveaxis(pieces, 0, dim)
    shape = pieces.shape
    return pieces.reshape(*shape[:dim], shape[dim] * shape[dim + 1], *shape[dim + 2 :])


def sent_to_all(array, axis):
    copies = jnp.broadcast_to(array, (lax.axis_size(axis), *array.shape))
    return lax.all_to_all(copies, axis, split_axis=0, concat_axis=0, tiled=True)


def gathered_copies(array, axis, dim):
    return laid_out(sent_to_all(array, axis), dim)


def cut_along(array, dim, length):
    shape = array.shape
    pieces = array.reshape(*shape[:dim], length, shape[dim] // length, *shape[dim + 1 :])
    return jnp.moveaxis(pieces, dim, 0)


def edges_of(length, count):
    hop = length // count
    if hop >= 8:
        hop -= hop % 8
    return [hop * k for k in range(1, count)]


def own_block(pieces, axes, sequence):
    inside = pieces.shape[1:]
    pieces = pieces.reshape(*(lax.axis_size(a) for a in axes), *inside)
    pieces = jnp.moveaxis(pieces, sequence, range(len(axes))).reshape(-1, *inside)
    for k in sequence:
        pieces = lax.psum_scatter(pieces, axes[k], scatter_dimension=0, tiled=True)
    return pieces[0]


def sum_at_once(array, axes, dim):
    pieces = cut_along(array, dim, lax.axis_size(axes))
    widest = max(range(1, max(2, pieces.ndim - 1)), key=lambda d: pieces.shape[d])
    count, done = (len(axes), [])
    for first, slab in enumerate(
        jnp.split(pieces, edges_of(pieces.shape[widest], count), axis=widest)
    ):
        if slab.size:
            sequence = [(first + k) % count for k in range(count)]
            done.append(own_block(slab, axes, sequence))
    return jnp.concatenate(done, axis=widest - 1)


def covariance(left_coords, right_coords):
    row_gap = (left_coords[0][:, None] - right_coords[0][None, :]).astype(jnp.float32)
    col_gap = (left_coords[1][:, None] - right_coords[1][None, :]).astype(jnp.float32)
    distance = jnp.sqrt(row_gap * row_gap + col_gap * col_gap)
    return (jnp.exp(-distance / LSCALE) / (8.0 * LSCALE)).astype(jnp.bfloat16)


def per_device(sensitivity, duals, time_cov, cell_coords, obs_time, obs_owner):
    obs_count = sensitivity.shape[0]
    time_count = sensitivity.shape[1]
    cell_count = sensitivity.shape[2]
    real_count = duals.shape[1]
    first_time = lax.axis_index(TM) * time_count
    time_index = first_time + jnp.arange(time_count, dtype=jnp.int32)
    live = time_index[None, :, None] <= obs_time[:, None, None]
    masked = jnp.where(live, sensitivity, jnp.zeros((), jnp.bfloat16))
    flattened = masked.reshape(obs_count, time_count * cell_count)
    picked = flattened
    adjoint = lax.dot_general(
        picked,
        lax.all_gather(duals, TM_CELL, axis=0, tiled=True),
        (((0,), (0,)), ((), ())),
        preferred_element_type=jnp.float32,
    )
    local_adj = (
        adjoint.astype(jnp.bfloat16).reshape(time_count, cell_count, real_count).transpose(1, 0, 2)
    )
    all_coords = gathered_copies(cell_coords, CELL, 1)
    spread_adj = lax.all_to_all(local_adj, TM, split_axis=2, concat_axis=1, tiled=True)
    values = jnp.einsum(
        "st,ctr->csr", time_cov, spread_adj.astype(jnp.float32), precision=lax.Precision.HIGHEST
    ).astype(jnp.bfloat16)
    portion = lax.all_gather(values, CELL, axis=0, tiled=True)
    kernel = covariance(cell_coords, all_coords)
    summed = jnp.dot(
        kernel, portion.reshape(portion.shape[0], -1), preferred_element_type=jnp.float32
    )
    weighted = lax.all_to_all(
        summed.reshape(values.shape).astype(jnp.bfloat16),
        TM,
        split_axis=1,
        concat_axis=2,
        tiled=True,
    )
    weighted_flat = weighted.transpose(1, 0, 2).reshape(time_count * cell_count, real_count)
    picked = jnp.take(flattened, obs_owner, axis=0)
    return sum_at_once(
        jnp.dot(picked, weighted_flat, preferred_element_type=jnp.float32), TM_CELL, 0
    )


def solution(mesh):
    split = Mesh(mesh.devices.reshape(4, 2, 2, 8, 4), ("tm_0", "tm_1", "tm_2", "cell_0", "cell_1"))
    return jax.shard_map(
        per_device,
        mesh=split,
        in_specs=(P(None, TM, CELL), P(TM_CELL, None), P(), P(None, CELL), P(), P()),
        out_specs=P(TM_CELL, None),
        check_vma=False,
    )
```

profile of v0, /device:TPU:1, one launch (start us, length us, event | category | flops | bytes accessed | tf_op | source)
XLA Modules:
  0.0 1606.2 jit_solution(16433688849147574105)
XLA Ops:
  6.5 1192.5 %all-gather = bf16[512,4,128]{2,1,0:T(4,128)(2,1)S(1)} all-gather(bf16[1,4,128]{2,1,0:T(4,128)(2,1)} %bitcast.57), channel_id=1, replica_groups=mesh['tm_0'=4,'tm_1'=2,'tm_2'=2,'cell_0'=8,'cell_1'=4] {'tm_0','tm_1','t..., dimensions={0}, use_global_device_ids=true | all-gather | bytes 525312 | tf_op jit(solution)/shard_map/all_gather | solution.py:83
  1199.1 0.7 broadcast_compare_fusion
  1199.8 1.8 select_bitcast_fusion
  1201.6 0.8 fusion.14
  1202.4 0.2 copy.17
  1202.6 0.5 broadcast.41
  1203.1 1.4 reduce
  1204.6 74.2 %all_to_all.26 = bf16[16,2,2048]{2,1,0:T(2,128)(2,1)S(1)} all-to-all(bf16[16,2,2048]{2,1,0:T(2,128)(2,1)S(1)} %reshape.87), channel_id=1, replica_groups=mesh['tm_0'=4,'tm_1'=2,'tm_2'=2,'cell_0'=8,'cell_1'=4] {'tm_0','tm_1','t..., dimensions={0} | all-to-all | bytes 262144 | tf_op jit(solution)/shard_map/all_to_all | solution.py:91
  1278.7 0.1 reshape.88
  1278.9 0.9 fusion.15
  1279.9 0.7 broadcast_in_dim.33
  1280.5 3.9 all-to-all-start
  1284.4 9.2 gather_fusion
  1293.6 2.3 all-to-all-done
  1295.9 0.1 fusion.22
  1296.0 115.7 %all-gather.3.cloned.1.call-done = bf16[16384,16,8]{0,1,2:T(8,128)(2,1)} async-done(((bf16[512,16,8]{0,1,2:T(8,128)(2,1)}), bf16[16384,16,8]{0,1,2:T(8,128)(2,1)}) %all-gather.3.cloned.1.call-update) | async-done | bytes 4194320 | tf_op jit(solution)/shard_map/all_gather | solution.py:95
  1411.8 22.9 %fusion.9 = bf16[512,16,8]{0,1,2:T(8,128)(2,1)S(1)} fusion(bf16[16384,16,8]{0,1,2:T(8,128)(2,1)} %all-gather.3.cloned.1.call-done, s32[16384]{0:T(1024)S(1)} %bitcast.54, s32[512]{0:T(512)S(1)} %bitcast.56, s32[16384]{0:T(1024)S(1)} %bitcast.53, s32[512]{0:T(512)S(1)} %bitcast.55), kind=kOutput, calls=%fused_computation.12 | convolution fusion | flops 2239823872 | bytes 4460544 | tf_op jit(solution)/shard_map/dot_general | solution.py:97
  1434.7 0.7 copy.21
  1435.4 27.8 %all-to-all-start.2 = ((bf16[512,16,8]{0,2,1:T(8,128)(2,1)}), bf16[512,16,8]{0,2,1:T(8,128)(2,1)S(1)}, u32[]{:S(2)}, u32[]{:S(2)}) async-start(bf16[512,16,8]{0,2,1:T(8,128)(2,1)} %copy.21), calls=%async_computation.2 | async-start | bytes 262144 | tf_op jit(solution)/shard_map/all_to_all | solution.py:100
  1463.2 1.6 broadcast_select_fusion
  1464.8 2.5 select_n.30
  1467.4 5.9 all-to-all-done.2
  1473.2 1.3 fusion.6
  1474.6 1.1 copy.24
  1475.8 31.4 %reduce-scatter.5.cloned.1.call-done = f32[128,4,128]{2,0,1:T(8,128)} async-done(((f32[512,4,128]{2,0,1:T(8,128)}), f32[128,4,128]{2,0,1:T(8,128)}) %reduce-scatter.5.cloned.1.call-update) | async-done | bytes 262160 | tf_op jit(solution)/shard_map/reduce_scatter | solution.py:46
  1507.2 25.7 %reduce-scatter.7.cloned.1.call-done = f32[32,4,128]{2,0,1:T(8,128)} async-done(((f32[128,4,128]{2,0,1:T(8,128)}), f32[32,4,128]{2,0,1:T(8,128)}) %reduce-scatter.7.cloned.1.call-update) | async-done | bytes 65552 | tf_op jit(solution)/shard_map/reduce_scatter | solution.py:46
  1532.9 27.2 %reduce-scatter.9.cloned.1.call-done = f32[16,4,128]{2,0,1:T(8,128)} async-done(((f32[32,4,128]{2,0,1:T(8,128)}), f32[16,4,128]{2,0,1:T(8,128)}) %reduce-scatter.9.cloned.1.call-update) | async-done | bytes 32784 | tf_op jit(solution)/shard_map/reduce_scatter | solution.py:46
  1560.1 1.3 dynamic-slice
  1561.5 14.6 reduce-scatter.11.cloned.1.call-done
  1576.0 0.7 copy.25
  1576.8 21.6 %all-reduce = f32[8,4,128]{2,1,0:T(4,128)S(1)} all-reduce(f32[8,4,128]{2,1,0:T(4,128)S(1)} %copy.25), channel_id=6, replica_groups=mesh['tm_0'=4,'tm_1'=2,'tm_2'=2,'cell_0'=8,'cell_1'=4] {'cell_0'}, use_global_device_ids=true, to_apply=%region_4.5.clone | all-reduce | flops 4096 | bytes 32768
  1598.4 1.3 dynamic-slice_bitcast_fusion
  (23 shorter events, 0.4 us)
Async XLA Ops:
  6.5 1272.4 %copy-start = (f32[16,16]{1,0:T(8,128)S(1)}, f32[16,16]{1,0:T(8,128)}, u32[]{:S(2)}) copy-start(f32[16,16]{1,0:T(8,128)} %param.8) | copy-start | bytes 3076
  6.5 1405.2 %all-gather.3.cloned.1.call-start = ((), (), s32[]{:S(2)}) async-start(), calls=%async_computation.7 | async-start | bytes 4325376 | tf_op jit(solution)/shard_map/all_gather | solution.py:95
  1199.8 80.1 %copy-start.3 = (s32[2,512]{1,0:T(2,128)S(1)}, s32[2,512]{1,0:T(2,128)}, u32[]{:S(2)}) copy-start(s32[2,512]{1,0:T(2,128)} %param.9) | copy-start | bytes 12292
  1199.8 84.6 %copy-start.2 = (s32[2048]{0:T(1024)S(1)}, s32[2048]{0:T(1024)}, u32[]{:S(2)}) copy-start(s32[2048]{0:T(1024)} %param.11) | copy-start | bytes 24580
  1280.5 15.4 all-to-all-start
  1411.8 51.5 %copy-start.1 = (bf16[2048,512]{1,0:T(8,128)(2,1)S(1)}, bf16[2048,512]{1,0:T(8,128)(2,1)}, u32[]{:S(2)}) copy-start(bf16[2048,512]{1,0:T(8,128)(2,1)} %gather_fusion) | copy-start | bytes 6291460
  1435.4 37.8 %all-to-all-start.2 = ((bf16[512,16,8]{0,2,1:T(8,128)(2,1)}), bf16[512,16,8]{0,2,1:T(8,128)(2,1)S(1)}, u32[]{:S(2)}, u32[]{:S(2)}) async-start(bf16[512,16,8]{0,2,1:T(8,128)(2,1)} %copy.21), calls=%async_computation.2 | async-start | bytes 262144 | tf_op jit(solution)/shard_map/all_to_all | solution.py:100
  1463.2 43.9 %reduce-scatter.5.cloned.1.call-start = ((), (), s32[]{:S(2)}) async-start(), calls=%async_computation.8 | async-start | bytes 1310720 | tf_op jit(solution)/shard_map/reduce_scatter | solution.py:46
  1475.7 57.2 %reduce-scatter.7.cloned.1.call-start = ((), (), s32[]{:S(2)}) async-start(), calls=%async_computation.9 | async-start | bytes 327680 | tf_op jit(solution)/shard_map/reduce_scatter | solution.py:46
  1507.1 53.0 %reduce-scatter.9.cloned.1.call-start = ((), (), s32[]{:S(2)}) async-start(), calls=%async_computation.10 | async-start | bytes 98304 | tf_op jit(solution)/shard_map/reduce_scatter | solution.py:46
  1532.9 43.1 %reduce-scatter.11.cloned.1.call-start = ((), (), s32[]{:S(2)}) async-start(), calls=%async_computation.11 | async-start | bytes 49152 | tf_op jit(solution)/shard_map/reduce_scatter | solution.py:46
Sparse Core Ops, SparseCore 0:
  1280.0 131.7 all-gather.2
  1475.8 31.2 reduce-scatter.4
  1510.2 22.6 reduce-scatter.6
  1535.5 24.6 reduce-scatter.8
  1562.7 13.3 reduce-scatter.10
where the time goes:
time: 1610 us
  blocking collectives  1290 us (80%)
  waiting for transfers between devices  223 us (14%)
  starting transfers between devices  31.8 us (2%)
  matrix products  25.9 us (2%)
  local copies, waits for them, and re-layouts  18.6 us (1%)
    all_gather x1, blocking collectives, per_device(): lax.all_gather(duals, TM_CELL, axis=0, tiled=True)  1190 us
    all_gather x1, waiting for transfers between devices, per_device(): portion = lax.all_gather(values, CELL, axis=0, tiled=True)  116 us
    reduce_scatter x4, waiting for transfers between devices, own_block(): pieces = lax.psum_scatter(pieces, axes[k], scatter_dimension=0, tiled=True)  98.8 us
    all_to_all x1, blocking collectives, per_device(): lax.all_to_all(local_adj, TM, split_axis=2, concat_axis=1, tiled=True)  74.2 us
  transfers between devices with their start and end apart: 7, of which 7 were waited for; matrix products, arithmetic and copies ran while one was open for 1% of the time, Pallas kernels for 0%

commit v1 on v0

v1 whole, which is shorter than its diff:
```python
import functools

import jax
import jax.numpy as jnp
import ml_dtypes
import numpy as np
from jax import lax
from jax.experimental import pallas as pl
from jax.experimental.pallas import tpu as pltpu
from jax.sharding import Mesh
from jax.sharding import PartitionSpec as P

LSCALE = 4
GRID = 128
X, ZH, CO, Y, ZL = "tm_0", "tm_1", "tm_2", "cell_0", "cell_1"
CELL = (Y, ZL)
EVERY = (X, ZH, CO, Y, ZL)
BF16 = jnp.bfloat16
F32 = jnp.float32
EXACT = lax.Precision.HIGHEST


def spectrum():
    size = 2 * GRID
    gap = np.arange(GRID, dtype=np.float32)
    distance = np.sqrt(gap[:, None] * gap[:, None] + gap[None, :] * gap[None, :])
    table = (np.exp(-distance / np.float32(LSCALE)) / np.float32(8.0 * LSCALE)).astype(ml_dtypes.bfloat16)
    table = table.astype(np.float64)
    wave = np.concatenate([np.arange(GRID + 1), np.arange(1, GRID)])
    angle = 2.0 * np.pi * wave[:, None] * np.arange(GRID)[None, :] / size
    basis = np.where(np.arange(size)[:, None] <= GRID, np.cos(angle), np.sin(angle))
    edge = (wave == 0) | (wave == GRID)
    basis = basis * np.where(edge, np.sqrt(1.0 / size), np.sqrt(2.0 / size))[:, None]
    fold = np.cos(angle) * np.where(np.arange(GRID) == 0, 1.0, 2.0)[None, :]
    eigen = fold @ table @ fold.T
    return basis.astype(np.float32), eigen.astype(np.float32)


def spatial_kernel(group, weight_ref, field_ref, rows_ref, cols_ref, basis_ref, turned_ref, eigen_ref, out_ref,
                   mixed, on_row, on_col, grid):
    kept = weight_ref.shape[0]
    times = field_ref.shape[0]
    chunks = rows_ref.shape[0]
    for s in range(kept):
        total = jnp.zeros((chunks, GRID), F32)
        for t in range(times):
            total = total + weight_ref[s, t] * field_ref[t].astype(F32)
        mixed[s] = total.astype(BF16).astype(F32)
    place = lax.broadcasted_iota(jnp.int32, (GRID, GRID), 0)
    grid[...] = jnp.zeros_like(grid)

    def put(j, carry):
        first = pl.multiple_of(j * group, group)
        rows = rows_ref[pl.ds(first, group), :]
        cols = cols_ref[pl.ds(first, group), :]
        values = [mixed[s, pl.ds(first, group), :] for s in range(kept)]
        lefts = []
        rights = []
        for g in range(group):
            span = pl.ds(pl.multiple_of(first * GRID + g * GRID, GRID), GRID)
            row_hit = jnp.where(place == rows[g : g + 1, :], 1.0, 0.0).astype(BF16)
            col_hit = jnp.where(place == cols[g : g + 1, :], 1.0, 0.0).astype(BF16)
            on_row[:, span] = row_hit
            on_col[:, span] = col_hit
            lefts.append(
                jnp.concatenate([row_hit * values[s][g : g + 1, :].astype(BF16) for s in range(kept)], axis=0)
            )
            rights.append(col_hit)
        grid[...] += lax.dot_general(
            jnp.concatenate(lefts, axis=1),
            jnp.concatenate(rights, axis=1),
            (((1,), (1,)), ((), ())),
            preferred_element_type=F32,
        )
        return carry

    lax.fori_loop(0, chunks // group, put, 0)
    basis = basis_ref[...]
    turned = turned_ref[...]
    ahead = jnp.dot(grid[...], turned, precision=EXACT, preferred_element_type=F32)
    for s in range(kept):
        span = slice(s * GRID, (s + 1) * GRID)
        waves = jnp.dot(basis, ahead[span], precision=EXACT, preferred_element_type=F32) * eigen_ref[...]
        back = jnp.dot(turned, waves, precision=EXACT, preferred_element_type=F32)
        grid[span, :] = jnp.dot(back, basis, precision=EXACT, preferred_element_type=F32)
    smooth = grid[...].astype(BF16)

    def take(j, carry):
        first = pl.multiple_of(j * group, group)
        span = pl.ds(pl.multiple_of(first * GRID, group * GRID), group * GRID)
        picked = jnp.dot(smooth, on_col[:, span], preferred_element_type=F32)
        row_hit = on_row[:, span].astype(F32)
        for s in range(kept):
            line = jnp.sum(picked[s * GRID : (s + 1) * GRID] * row_hit, axis=0, keepdims=True)
            block = jnp.concatenate([line[:, g * GRID : (g + 1) * GRID] for g in range(group)], axis=0)
            out_ref[pl.ds(pl.multiple_of(s * chunks + first, group), group), :] = block.astype(BF16)
        return carry

    lax.fori_loop(0, chunks // group, take, 0)


def spatial(weight, field, rows, cols):
    kept = weight.shape[0]
    chunks = field.shape[1]
    cells = chunks * GRID
    basis, eigen = spectrum()
    vmem = pl.BlockSpec(memory_space=pltpu.VMEM)
    return pl.pallas_call(
        functools.partial(spatial_kernel, 16),
        out_shape=jax.ShapeDtypeStruct((kept * chunks, GRID), BF16),
        in_specs=[pl.BlockSpec(memory_space=pltpu.SMEM)] + [vmem] * 6,
        out_specs=vmem,
        scratch_shapes=[
            pltpu.VMEM((kept, chunks, GRID), F32),
            pltpu.VMEM((GRID, cells), BF16),
            pltpu.VMEM((GRID, cells), BF16),
            pltpu.VMEM((kept * GRID, GRID), F32),
        ],
        compiler_params=pltpu.CompilerParams(vmem_limit_bytes=40 << 20),
    )(weight, field, rows, cols, jnp.asarray(basis), jnp.asarray(basis.T.copy()), jnp.asarray(eigen))


def exchange(pieces, axes):
    return lax.all_to_all(pieces, axes, split_axis=0, concat_axis=0, tiled=True)


def copies(array, axes):
    return exchange(jnp.broadcast_to(array, (lax.axis_size(axes), *array.shape)), axes)


def per_device(sensitivity, duals, time_cov, cell_coords, obs_time, obs_owner):
    obs = sensitivity.shape[0]
    reals = duals.shape[1]
    flat = sensitivity.reshape(obs, -1)
    here = lax.axis_index((X, ZH, CO))
    live = here <= obs_time
    quarter = lax.axis_size(X)
    kept = time_cov.shape[0] // quarter
    weight = lax.dynamic_slice_in_dim(time_cov, lax.axis_index(X) * kept, kept, 0)

    own = duals.shape[0]
    places = cell_coords.astype(BF16).reshape(-1, GRID)
    half = places.shape[0] // 2
    first = copies(jnp.concatenate([duals, places], axis=0), CELL)
    rows = first[:, own : own + half].reshape(-1, GRID).astype(jnp.int32)
    cols = first[:, own + half :].reshape(-1, GRID).astype(jnp.int32)
    second = copies(first[:, :own].reshape(-1, reals), (X, ZH))
    third = lax.all_gather(second, CO, axis=0)
    all_duals = third.transpose(1, 0, 2, 3).reshape(obs, reals)

    seen = jnp.where(live[:, None], all_duals, jnp.zeros((), BF16))
    adjoint = lax.dot_general(seen, flat, (((0,), (0,)), ((), ())), preferred_element_type=F32).astype(BF16)
    pieces = jnp.broadcast_to(adjoint.reshape(1, reals, -1, GRID), (quarter, reals, flat.shape[1] // GRID, GRID))
    field = exchange(pieces.reshape(-1, *pieces.shape[2:]), EVERY)
    field = field.reshape(time_cov.shape[0], -1, GRID)

    weighted = spatial(weight, field, rows, cols)
    weighted = exchange(weighted.reshape(reals, -1, GRID), (ZH, CO, Y, ZL)).reshape(reals, -1)

    forward = lax.dot_general(flat, weighted, (((1,), (1,)), ((), ())), preferred_element_type=F32).astype(BF16)
    pair = lax.axis_size(CO)
    groups = lax.axis_size((X, ZH))
    slots = obs_owner.reshape(groups, pair, -1).transpose(1, 0, 2).reshape(-1)
    chosen = (slots[:, None] == jnp.arange(obs, dtype=jnp.int32)[None, :]) & live[None, :]
    product = jnp.dot(chosen.astype(BF16), forward, preferred_element_type=F32).astype(BF16)
    product = exchange(product.reshape(pair, -1, reals), CO)
    product = jnp.sum(product.astype(F32), axis=0).astype(BF16)
    product = exchange(product.reshape(-1, own, reals), (X, ZH, Y, ZL))
    return jnp.sum(product.astype(F32), axis=0)


def solution(mesh):
    split = Mesh(mesh.devices.reshape(4, 2, 2, 8, 4), EVERY)
    every = P(EVERY, None)
    return jax.shard_map(
        per_device,
        mesh=split,
        in_specs=(P(None, (X, ZH, CO), CELL), every, P(), P(None, CELL), P(), P()),
        out_specs=every,
        check_vma=False,
    )
```

time: 1610 us -> 155 us (0.10)
  blocking collectives: 1290 us -> 55.7 us
  waiting for transfers between devices: 223 us -> 45.6 us
  matrix products: 25.9 us -> 4.61 us
  Pallas kernels: 0 us -> 18.1 us
    all_gather x1, blocking collectives: 1190 us -> 5.23 us  [per_device(): third = lax.all_gather(second, CO, axis=0)]
    all_gather x1 -> x0, waiting for transfers between devices: 116 us -> none  [per_device(): portion = lax.all_gather(values, CELL, axis=0, tiled=True)]
    reduce_scatter x4 -> x0, waiting for transfers between devices: 98.8 us -> none  [own_block(): pieces = lax.psum_scatter(pieces, axes[k], scatter_dimension=0, tiled=True)]
    all_to_all x2 -> x3, waiting for transfers between devices: 8.17 us -> 45.6 us  [exchange(): return lax.all_to_all(pieces, axes, split_axis=0, concat_axis=0, tiled=True)]
    all_to_all x1 -> x3, blocking collectives: 74.2 us -> 50.5 us  [exchange(): return lax.all_to_all(pieces, axes, split_axis=0, concat_axis=0, tiled=True)]
    unnamed x1 -> x0, blocking collectives: 21.6 us -> none
    dot_general x4 -> x2, matrix products: 25.9 us -> 4.61 us  [the longest x1 4.15 us: per_device(): jnp.dot(chosen.astype(BF16), forward, preferred_element_type=F32)]
    pallas_call x0 -> x1, Pallas kernels: none -> 18.1 us  [spatial(): pl.pallas_call(functools.partial(spatial_kernel, 16), out_shape=jax.Shape...]
  transfers between devices with their start and end apart: 7 -> 3, of which waited for: 7 -> 3; matrix products, arithmetic and copies ran while one was open for 1% -> 1% of each run, Pallas kernels for 0% -> 0%
where the time goes in v1:
time: 155 us; the launch traced here: 154 us
  blocking collectives  55.7 us (36%)
  waiting for transfers between devices  45.6 us (29%)
  starting transfers between devices  24.1 us (16%)
  Pallas kernels  18.1 us (12%)
  matrix products  4.61 us (3%)
  other arithmetic  3.41 us (2%)
  local copies, waits for them, and re-layouts  2.57 us (2%)
    all_to_all x3, blocking collectives, exchange(): return lax.all_to_all(pieces, axes, split_axis=0, concat_axis=0, tiled=True)  50.5 us
    all_to_all x3, waiting for transfers between devices, exchange(): return lax.all_to_all(pieces, axes, split_axis=0, concat_axis=0, tiled=True)  45.6 us
    all_to_all x3, starting transfers between devices, exchange(): return lax.all_to_all(pieces, axes, split_axis=0, concat_axis=0, tiled=True)  24.1 us
    pallas_call x1, Pallas kernels, spatial(): pl.pallas_call(functools.partial(spatial_kernel, 16), out_shape=jax.Shape...  18.1 us
    all_gather x1, blocking collectives, per_device(): third = lax.all_gather(second, CO, axis=0)  5.23 us
    dot_general x1, matrix products, per_device(): jnp.dot(chosen.astype(BF16), forward, preferred_element_type=F32)  4.15 us
  transfers between devices with their start and end apart: 3, of which 3 were waited for; matrix products, arithmetic and copies ran while one was open for 1% of the time, Pallas kernels for 0%

profile of v1, /device:TPU:1, one launch (start us, length us, event | category | flops | bytes accessed | tf_op | source)
XLA Modules:
  0.0 154.3 jit_solution(2509612531020859232)
XLA Ops:
  0.0 0.0 copy-start
  0.0 0.8 convert_element_type.29
  0.9 0.7 pad_maximum_fusion
  1.6 23.2 %all_to_all.30 = bf16[32,12,128]{2,1,0:T(8,128)(2,1)S(1)} all-to-all(bf16[32,12,128]{2,1,0:T(8,128)(2,1)S(1)} %broadcast_in_dim.32), channel_id=1, replica_groups=mesh['tm_0'=4,'tm_1'=2,'tm_2'=2,'cell_0'=8,'cell_1'=4] {'cell_0','cell_1'}, dimensions={0} | all-to-all | bytes 196608 | tf_op jit(solution)/shard_map/all_to_all | solution.py:124
  24.8 0.7 broadcast_in_dim.33
  25.5 9.8 %all-to-all-start.1 = ((bf16[8,128,128]{2,1,0:T(8,128)(2,1)}), bf16[8,128,128]{2,1,0:T(8,128)(2,1)S(1)}, u32[]{:S(2)}, u32[]{:S(2)}) async-start(bf16[8,128,128]{2,1,0:T(8,128)(2,1)} %broadcast_in_dim.33), calls=%async_computation.1 | async-start | bytes 524288 | tf_op jit(solution)/shard_map/all_to_all | solution.py:124
  35.3 0.7 broadcast_compare_fusion
  36.0 9.4 %all-to-all-done.1 = bf16[8,128,128]{2,1,0:T(8,128)(2,1)S(1)} async-done(((bf16[8,128,128]{2,1,0:T(8,128)(2,1)}), bf16[8,128,128]{2,1,0:T(8,128)(2,1)S(1)}, u32[]{:S(2)}, u32[]{:S(2)}) %all-to-all-start.1) | async-done | bytes 262176 | tf_op jit(solution)/shard_map/all_to_all | solution.py:124
  45.4 5.2 %all-gather = bf16[16,128,128]{2,1,0:T(8,128)(2,1)S(1)} all-gather(bf16[8,128,128]{2,1,0:T(8,128)(2,1)S(1)} %all-to-all-done.1), channel_id=2, replica_groups=mesh['tm_0'=4,'tm_1'=2,'tm_2'=2,'cell_0'=8,'cell_1'=4] {'tm_2'}, dimensions={0}, use_global_device_ids=true | all-gather | bytes 786432 | tf_op jit(solution)/shard_map/all_gather | solution.py:148
  50.6 0.3 broadcast_select_fusion
  51.0 0.0 copy-done
  51.1 0.0 copy-start.1
  51.1 0.0 copy-start.2
  51.1 0.0 copy-start.3
  51.1 0.5 fusion.11
  51.6 0.0 copy-start.4
  51.6 0.9 broadcast_in_dim.36
  52.5 8.6 %all-to-all-start.2 = ((bf16[512,4,128]{2,1,0:T(4,128)(2,1)}), bf16[512,4,128]{2,1,0:T(4,128)(2,1)S(1)}, u32[]{:S(2)}, u32[]{:S(2)}) async-start(bf16[512,4,128]{2,1,0:T(4,128)(2,1)} %bitcast.36), calls=%async_computation.2 | async-start | bytes 1048576 | tf_op jit(solution)/shard_map/all_to_all | solution.py:124
  61.2 0.7 constant_dynamic-slice_fusion.weight_ref
  61.9 22.6 %all-to-all-done.2 = bf16[512,4,128]{2,1,0:T(4,128)(2,1)S(1)} async-done(((bf16[512,4,128]{2,1,0:T(4,128)(2,1)}), bf16[512,4,128]{2,1,0:T(4,128)(2,1)S(1)}, u32[]{:S(2)}, u32[]{:S(2)}) %all-to-all-start.2) | async-done | bytes 524320 | tf_op jit(solution)/shard_map/all_to_all | solution.py:124
  84.5 0.0 copy-done.1
  84.5 0.0 copy-done.2
  84.5 0.0 copy-done.3
  84.5 18.1 %shard_map.91 = bf16[512,128]{1,0:T(8,128)(2,1)} custom-call(f32[4,16]{1,0:T(4,128)S(1)} %constant_dynamic-slice_fusion.weight_ref, bf16[16,128,128]{2,1,0:T(8,128)(2,1)S(1)} %bitcast.35, s32[128,128]{1,0:T(8,128)S(1)} %convert.3.rows_ref, s32[128,128]{1,0:T(8,128)S(1)} %convert.4.cols_ref, f32[256,128]{1,0:T(8,128)S(1)} %copy-done.2, ...), custom_call_target="tpu_custom_call" | custom-call | tf_op jit(solution)/shard_map/pallas_call | solution.py:108
  102.6 5.8 %all-to-all-start.3 = ((bf16[128,4,128]{2,1,0:T(4,128)(2,1)}), bf16[128,4,128]{2,1,0:T(4,128)(2,1)S(1)}, u32[]{:S(2)}, u32[]{:S(2)}) async-start(bf16[128,4,128]{2,1,0:T(4,128)(2,1)} %bitcast.12), calls=%async_computation.3 | async-start | bytes 262144 | tf_op jit(solution)/shard_map/all_to_all | solution.py:124
  108.4 0.0 copy-done.4
  108.4 13.6 %all-to-all-done.3 = bf16[128,4,128]{2,1,0:T(4,128)(2,1)S(1)} async-done(((bf16[128,4,128]{2,1,0:T(4,128)(2,1)}), bf16[128,4,128]{2,1,0:T(4,128)(2,1)S(1)}, u32[]{:S(2)}, u32[]{:S(2)}) %all-to-all-start.3) | async-done | bytes 131104 | tf_op jit(solution)/shard_map/all_to_all | solution.py:124
  122.0 4.1 %fusion.5 = bf16[2048,128]{1,0:T(8,128)(2,1)S(1)} fusion(s32[2048]{0:T(1024)S(1)} %bitcast.46, pred[2048]{0:T(1024)(128)(4,1)S(1)} %broadcast_compare_fusion, bf16[2048,1,512]{2,0,1:T(8,128)(2,1)S(1)} %copy-done, bf16[16,8,4,128]{3,2,1,0:T(4,128)(2,1)S(1)} %bitcast.41), kind=kOutput, calls=%fused_computation.5 | convolution fusion | flops 1351090176 | bytes 2762752 | tf_op jit(solution)/shard_map/dot_general | solution.py:165
  126.2 3.8 %all_to_all.31 = bf16[2,1024,128]{2,1,0:T(8,128)(2,1)S(1)} all-to-all(bf16[2,1024,128]{2,1,0:T(8,128)(2,1)S(1)} %bitcast.40), channel_id=1, replica_groups=mesh['tm_0'=4,'tm_1'=2,'tm_2'=2,'cell_0'=8,'cell_1'=4] {'tm_2'}, dimensions={0} | all-to-all | bytes 1048576 | tf_op jit(solution)/shard_map/all_to_all | solution.py:124
  130.0 0.2 reduce_sum.21
  130.2 23.5 %all_to_all.32 = bf16[256,4,128]{2,1,0:T(4,128)(2,1)S(1)} all-to-all(bf16[256,4,128]{2,1,0:T(4,128)(2,1)S(1)} %bitcast.39), channel_id=1, replica_groups=mesh['tm_0'=4,'tm_1'=2,'tm_2'=2,'cell_0'=8,'cell_1'=4] {'tm_0','tm_1','c..., dimensions={0} | all-to-all | bytes 524288 | tf_op jit(solution)/shard_map/all_to_all | solution.py:124
  153.7 0.6 convert_reduce_fusion
  (10 shorter events, 0.2 us)
Async XLA Ops:
  0.0 51.0 %copy-start = (bf16[2048,1,512]{2,0,1:T(8,128)(2,1)S(1)}, bf16[2048,1,512]{2,0,1:T(8,128)(2,1)}, u32[]{:S(2)}) copy-start(bf16[2048,1,512]{2,0,1:T(8,128)(2,1)} %param.9) | copy-start | bytes 6291460
  25.5 19.9 %all-to-all-start.1 = ((bf16[8,128,128]{2,1,0:T(8,128)(2,1)}), bf16[8,128,128]{2,1,0:T(8,128)(2,1)S(1)}, u32[]{:S(2)}, u32[]{:S(2)}) async-start(bf16[8,128,128]{2,1,0:T(8,128)(2,1)} %broadcast_in_dim.33), calls=%async_computation.1 | async-start | bytes 524288 | tf_op jit(solution)/shard_map/all_to_all | solution.py:124
  51.1 33.4 %copy-start.1 = (f32[256,256]{1,0:T(8,128)S(1)}, f32[256,256]{1,0:T(8,128)}, u32[]{:S(2)}) copy-start(f32[256,256]{1,0:T(8,128)} %constant.37.clone.eigen_ref) | copy-start | bytes 786436
  51.1 33.4 %copy-start.2 = (f32[256,128]{1,0:T(8,128)S(1)}, f32[256,128]{1,0:T(8,128)}, u32[]{:S(2)}) copy-start(f32[256,128]{1,0:T(8,128)} %constant.35.clone.basis_ref) | copy-start | bytes 393220
  51.1 33.4 %copy-start.3 = (f32[128,256]{1,0:T(8,128)S(1)}, f32[128,256]{1,0:T(8,128)}, u32[]{:S(2)}) copy-start(f32[128,256]{1,0:T(8,128)} %constant.36.clone.turned_ref) | copy-start | bytes 393220
  51.6 56.8 %copy-start.4 = (s32[2048]{0:T(1024)S(1)}, s32[2048]{0:T(1024)}, u32[]{:S(2)}) copy-start(s32[2048]{0:T(1024)} %param.14) | copy-start | bytes 24580
  52.5 31.9 %all-to-all-start.2 = ((bf16[512,4,128]{2,1,0:T(4,128)(2,1)}), bf16[512,4,128]{2,1,0:T(4,128)(2,1)S(1)}, u32[]{:S(2)}, u32[]{:S(2)}) async-start(bf16[512,4,128]{2,1,0:T(4,128)(2,1)} %bitcast.36), calls=%async_computation.2 | async-start | bytes 1048576 | tf_op jit(solution)/shard_map/all_to_all | solution.py:124
  102.6 19.4 %all-to-all-start.3 = ((bf16[128,4,128]{2,1,0:T(4,128)(2,1)}), bf16[128,4,128]{2,1,0:T(4,128)(2,1)S(1)}, u32[]{:S(2)}, u32[]{:S(2)}) async-start(bf16[128,4,128]{2,1,0:T(4,128)(2,1)} %bitcast.12), calls=%async_computation.3 | async-start | bytes 262144 | tf_op jit(solution)/shard_map/all_to_all | solution.py:124

commit v2 on v1

v2 whole, which is shorter than its diff:
```python
import functools

import jax
import jax.numpy as jnp
import ml_dtypes
import numpy as np
from jax import lax
from jax.experimental import pallas as pl
from jax.experimental.pallas import tpu as pltpu
from jax.sharding import Mesh
from jax.sharding import PartitionSpec as P

LSCALE = 4
GRID = 128
PARTS = 2
LOW = GRID // PARTS
X, ZH, CO, Y, ZL = "tm_0", "tm_1", "tm_2", "cell_0", "cell_1"
CELL = (Y, ZL)
EVERY = (X, ZH, CO, Y, ZL)
BF16 = jnp.bfloat16
F32 = jnp.float32
VMEM = pl.BlockSpec(memory_space=pltpu.VMEM)
SMEM = pl.BlockSpec(memory_space=pltpu.SMEM)


def halves(array):
    high = array.astype(np.float32).astype(ml_dtypes.bfloat16)
    return high, (array - high.astype(np.float64)).astype(np.float32).astype(ml_dtypes.bfloat16)


def spectrum():
    size = 2 * GRID
    gap = np.arange(GRID, dtype=np.float32)
    distance = np.sqrt(gap[:, None] * gap[:, None] + gap[None, :] * gap[None, :])
    table = (np.exp(-distance / np.float32(LSCALE)) / np.float32(8.0 * LSCALE)).astype(ml_dtypes.bfloat16)
    table = table.astype(np.float64)
    wave = np.concatenate([np.arange(GRID + 1), np.arange(1, GRID)])
    angle = 2.0 * np.pi * wave[:, None] * np.arange(GRID)[None, :] / size
    basis = np.where(np.arange(size)[:, None] <= GRID, np.cos(angle), np.sin(angle))
    edge = (wave == 0) | (wave == GRID)
    basis = basis * np.where(edge, np.sqrt(1.0 / size), np.sqrt(2.0 / size))[:, None]
    fold = np.cos(angle) * np.where(np.arange(GRID) == 0, 1.0, 2.0)[None, :]
    eigen = fold @ table @ fold.T
    return (*halves(basis), *halves(basis.T), eigen.astype(np.float32))


def matmul(a, b):
    return jnp.dot(a, b, preferred_element_type=F32)


def parted(a):
    high = a.astype(BF16)
    return high, (a - high.astype(F32)).astype(BF16)


def matmul_parted(a, b):
    return matmul(a[0], b[0]) + (matmul(a[0], b[1]) + matmul(a[1], b[0]))


def places_kernel(rows_ref, cols_ref, low_ref, wide_ref, turned_ref):
    wide_at = lax.broadcasted_iota(jnp.int32, (PARTS * GRID, GRID), 0)
    low_at = lax.broadcasted_iota(jnp.int32, (LOW, GRID), 0)
    rows = rows_ref[...]
    low = rows % LOW
    wide = (rows // LOW) * GRID + cols_ref[...]
    for g in range(rows.shape[0]):
        span = slice(g * GRID, (g + 1) * GRID)
        low_ref[:, span] = jnp.where(low_at == low[g : g + 1, :], 1.0, 0.0).astype(BF16)
        hit = jnp.where(wide_at == wide[g : g + 1, :], 1.0, 0.0).astype(BF16)
        wide_ref[:, span] = hit
        turned_ref[span, :] = hit.T


def places(rows, cols):
    cells = rows.size
    wide = PARTS * GRID
    lot = 8
    return pl.pallas_call(
        places_kernel,
        grid=(rows.shape[0] // lot,),
        out_shape=[
            jax.ShapeDtypeStruct((LOW, cells), BF16),
            jax.ShapeDtypeStruct((wide, cells), BF16),
            jax.ShapeDtypeStruct((cells, wide), BF16),
        ],
        in_specs=[pl.BlockSpec((lot, GRID), lambda i: (i, 0))] * 2,
        out_specs=[
            pl.BlockSpec((LOW, lot * GRID), lambda i: (0, i)),
            pl.BlockSpec((wide, lot * GRID), lambda i: (0, i)),
            pl.BlockSpec((lot * GRID, wide), lambda i: (i, 0)),
        ],
        compiler_params=pltpu.CompilerParams(vmem_limit_bytes=56 << 20),
        cost_estimate=pl.CostEstimate(flops=10**9, bytes_accessed=18 << 20, transcendentals=0),
    )(rows, cols)


def spatial_kernel(lot, lot_back, kept, which_ref, weight_ref, field_ref, low_hbm, wide_hbm, turned_hbm,
                   basis_h, basis_l, side_h, side_l, eigen_ref, out_ref, mixed, grid,
                   low_ref, wide_ref, turned_ref, low_done, wide_done, turned_done):
    times, chunks, _ = field_ref.shape
    pair = 2
    which = which_ref[0]
    strides = times // kept
    lots = chunks // lot

    def turned_copy(j):
        span = pl.ds(pl.multiple_of(j * lot * GRID, lot * GRID), lot * GRID)
        return pltpu.make_async_copy(turned_hbm.at[span], turned_ref.at[span], turned_done.at[j])

    low_copy = pltpu.make_async_copy(low_hbm, low_ref, low_done)
    wide_copy = pltpu.make_async_copy(wide_hbm, wide_ref, wide_done)
    low_copy.start()
    for j in range(lots):
        turned_copy(j).start()
    wide_copy.start()

    def mix(j, carry):
        rows = pl.ds(pl.multiple_of(j * 16, 16), 16)
        totals = [None] * kept
        for k in range(times):
            t = (k % (times // pair)) * pair + k // (times // pair)
            value = field_ref[k, rows, :].astype(F32)
            for s in range(kept):
                term = weight_ref[s * strides + which, t] * value
                totals[s] = term if k == 0 else totals[s] + term
        for s in range(kept):
            mixed[s, rows, :] = totals[s].astype(BF16).astype(F32)
        return carry

    lax.fori_loop(0, chunks // 16, mix, 0)
    grid[...] = jnp.zeros_like(grid)
    low_copy.wait()

    def put(j, carry):
        turned_copy(j).wait()
        first = pl.multiple_of(j * lot, lot)
        values = [mixed[s, pl.ds(first, lot), :] for s in range(kept)]
        lefts = []
        for g in range(lot):
            hit = low_ref[:, pl.ds(pl.multiple_of((first + g) * GRID, GRID), GRID)]
            lines = [jnp.broadcast_to(v[g : g + 1, :], (16, GRID)).astype(BF16) for v in values]
            lefts.append(
                jnp.concatenate([hit[k : k + 16] * line for line in lines for k in range(0, LOW, 16)], axis=0)
            )
        span = pl.ds(pl.multiple_of(first * GRID, lot * GRID), lot * GRID)
        grid[...] += matmul(jnp.concatenate(lefts, axis=1), turned_ref[span, :])
        return carry

    lax.fori_loop(0, lots, put, 0)
    basis = (basis_h[...], basis_l[...])
    side = (side_h[...], side_l[...])
    whole = jnp.concatenate(
        [
            grid[s * LOW : (s + 1) * LOW, p * GRID : (p + 1) * GRID]
            for s in range(kept)
            for p in range(PARTS)
        ],
        axis=0,
    )
    ahead = matmul_parted(parted(whole), side)
    for s in range(kept):
        waves = matmul_parted(basis, parted(ahead[s * GRID : (s + 1) * GRID])) * eigen_ref[...]
        back = matmul_parted(side, parted(waves))
        smooth = matmul_parted(parted(back), basis)
        for p in range(PARTS):
            grid[s * LOW : (s + 1) * LOW, p * GRID : (p + 1) * GRID] = smooth[p * LOW : (p + 1) * LOW]
    weighted = grid[...].astype(BF16)
    wide_copy.wait()

    def take(j, carry):
        first = pl.multiple_of(j * lot_back, lot_back)
        span = pl.ds(pl.multiple_of(first * GRID, lot_back * GRID), lot_back * GRID)
        picked = matmul(weighted, wide_ref[:, span])
        hit = low_ref[:, span].astype(F32)
        for s in range(kept):
            line = jnp.sum(picked[s * LOW : (s + 1) * LOW] * hit, axis=0, keepdims=True)
            block = jnp.concatenate([line[:, g * GRID : (g + 1) * GRID] for g in range(lot_back)], axis=0)
            out_ref[pl.ds(pl.multiple_of(s * chunks + first, lot_back), lot_back), :] = block.astype(BF16)
        return carry

    lax.fori_loop(0, chunks // lot_back, take, 0)


def spatial(which, weight, field, spots, kept):
    chunks = field.shape[1]
    constants = [jnp.asarray(c) for c in spectrum()]
    lot = 16
    return pl.pallas_call(
        functools.partial(spatial_kernel, lot, 32, kept),
        out_shape=jax.ShapeDtypeStruct((kept * chunks, GRID), BF16),
        in_specs=[SMEM] * 2 + [VMEM] + [pl.BlockSpec(memory_space=pl.ANY)] * len(spots) + [VMEM] * len(constants),
        out_specs=VMEM,
        scratch_shapes=[
            pltpu.VMEM((kept, chunks, GRID), F32),
            pltpu.VMEM((kept * LOW, PARTS * GRID), F32),
            *[pltpu.VMEM(spot.shape, spot.dtype) for spot in spots],
            pltpu.SemaphoreType.DMA,
            pltpu.SemaphoreType.DMA,
            pltpu.SemaphoreType.DMA((chunks // lot,)),
        ],
        compiler_params=pltpu.CompilerParams(vmem_limit_bytes=52 << 20),
        cost_estimate=pl.CostEstimate(flops=10**10, bytes_accessed=18 << 20, transcendentals=0),
    )(which, weight, field, *spots, *constants)


def exchange(pieces, axes):
    return lax.all_to_all(pieces, axes, split_axis=0, concat_axis=0, tiled=True)


def copies(array, axes):
    return exchange(jnp.broadcast_to(array, (lax.axis_size(axes), *array.shape)), axes)


def per_device(sensitivity, duals, time_cov, cell_coords, obs_time, obs_owner):
    obs = sensitivity.shape[0]
    own, reals = duals.shape
    flat = sensitivity.reshape(obs, -1)
    live = lax.axis_index((X, ZH, CO)) <= obs_time
    nx, nh, pair = (lax.axis_size(a) for a in (X, ZH, CO))
    which = lax.axis_index((ZH, CO)).reshape(1)

    line = lax.dynamic_slice_in_dim(cell_coords, lax.axis_index(ZH), 1, 0).astype(BF16).reshape(-1, GRID)
    first = copies(jnp.concatenate([duals, line], axis=0), (ZH, Y, ZL))
    coords = first[:, own:].reshape(nh, -1, GRID).astype(jnp.int32)
    second = copies(first[:, :own].reshape(-1, reals), X)
    third = lax.all_gather(second.reshape(nx * nh, -1, reals), CO, axis=0)
    all_duals = third.transpose(1, 0, 2, 3).reshape(obs, reals)

    seen = jnp.where(live[:, None], all_duals, jnp.zeros((), BF16))
    adjoint = lax.dot_general(seen, flat, (((0,), (0,)), ((), ())), preferred_element_type=F32).astype(BF16)
    pieces = adjoint.reshape(nx, 1, reals // nx, -1, GRID)
    pieces = jnp.broadcast_to(pieces, (nx, nh, *pieces.shape[2:]))
    field = exchange(pieces.reshape(-1, *pieces.shape[3:]), (X, ZH, Y, ZL))
    field = lax.all_gather(field.reshape(nx * nh, -1, GRID), CO, axis=0, tiled=True)

    spots = places(coords[0], coords[1])
    weighted = spatial(which, time_cov, field, spots, nx)
    slots, weighted = lax.optimization_barrier((obs_owner, weighted))
    weighted = exchange(weighted.reshape(reals, -1, GRID), (X, Y, ZL)).reshape(reals, -1)
    slots = slots.reshape(nx * nh, pair, -1).transpose(1, 0, 2).reshape(-1)
    chosen = (slots[:, None] == jnp.arange(obs, dtype=jnp.int32)[None, :]) & live[None, :]
    picked = jnp.dot(chosen.astype(BF16), flat, preferred_element_type=F32).astype(BF16)
    picked, weighted = lax.optimization_barrier((picked, weighted))
    product = lax.dot_general(picked, weighted, (((1,), (1,)), ((), ())), preferred_element_type=F32).astype(BF16)
    product = exchange(product.reshape(pair, -1, reals), CO)
    product = jnp.sum(product.astype(F32), axis=0).astype(BF16)
    product = exchange(product.reshape(-1, own, reals), (X, ZH, Y, ZL))
    return jnp.sum(product.astype(F32), axis=0)


def solution(mesh):
    split = Mesh(mesh.devices.reshape(4, 2, 2, 8, 4), EVERY)
    every = P(EVERY, None)
    return jax.shard_map(
        per_device,
        mesh=split,
        in_specs=(P(None, (X, ZH, CO), CELL), every, P(), P(None, CELL), P(), P()),
        out_specs=every,
        check_vma=False,
    )
```

time: 155 us -> 144 us (0.929)
  waiting for transfers between devices: 45.6 us -> 24.1 us
  blocking collectives: 55.7 us -> 38.9 us
  starting transfers between devices: 24.1 us -> 40 us
  Pallas kernels: 18.1 us -> 25.2 us
  matrix products: 4.61 us -> 8.56 us
    all_to_all x3 -> x4, waiting for transfers between devices: 45.6 us -> 24.1 us  [exchange(): return lax.all_to_all(pieces, axes, split_axis=0, concat_axis=0, tiled=True)]
    all_to_all x3 -> x2, blocking collectives: 50.5 us -> 30.1 us  [exchange(): return lax.all_to_all(pieces, axes, split_axis=0, concat_axis=0, tiled=True)]
    all_to_all x3 -> x4, starting transfers between devices: 24.1 us -> 40 us  [exchange(): return lax.all_to_all(pieces, axes, split_axis=0, concat_axis=0, tiled=True)]
    pallas_call x1 -> x2, Pallas kernels: 18.1 us -> 25.2 us  [the longest x1 13.8 us: spatial(): pl.pallas_call(functools.partial(spatial_kernel, lot, 32, kept), out_shap...]
    dot_general x1 -> x2, matrix products: 4.15 us -> 8.09 us  [the longest x1 5.79 us: per_device(): jnp.dot(chosen.astype(BF16), flat, preferred_element_type=F32).astype(BF16)]
    all_gather x1 -> x2, blocking collectives: 5.23 us -> 8.78 us  [the longest x1 5.3 us: per_device(): third = lax.all_gather(second.reshape(nx * nh, -1, reals), CO, axis=0)]
  transfers between devices with their start and end apart: 3 -> 4, of which waited for: 3 -> 4; matrix products, arithmetic and copies ran while one was open for 1% -> 5% of each run, Pallas kernels for 0% -> 8%
where the time goes in v2:
time: 144 us; the launch traced here: 143 us
  starting transfers between devices  40 us (28%)
  blocking collectives  38.9 us (27%)
  Pallas kernels  25.2 us (18%)
  waiting for transfers between devices  24.1 us (17%)
  matrix products  8.56 us (6%)
  other arithmetic  3.47 us (2%)
  local copies, waits for them, and re-layouts  2.95 us (2%)
    all_to_all x4, starting transfers between devices, exchange(): return lax.all_to_all(pieces, axes, split_axis=0, concat_axis=0, tiled=True)  40 us
    all_to_all x2, blocking collectives, exchange(): return lax.all_to_all(pieces, axes, split_axis=0, concat_axis=0, tiled=True)  30.1 us
    all_to_all x4, waiting for transfers between devices, exchange(): return lax.all_to_all(pieces, axes, split_axis=0, concat_axis=0, tiled=True)  24.1 us
    pallas_call x1, Pallas kernels, spatial(): pl.pallas_call(functools.partial(spatial_kernel, lot, 32, kept), out_shap...  13.8 us
    pallas_call x1, Pallas kernels, places(): pl.pallas_call(places_kernel, grid=(rows.shape[0] // lot,), out_shape=[ja...  11.3 us
    dot_general x1, matrix products, per_device(): jnp.dot(chosen.astype(BF16), flat, preferred_element_type=F32).astype(BF16)  5.79 us
    all_gather x1, blocking collectives, per_device(): third = lax.all_gather(second.reshape(nx * nh, -1, reals), CO, axis=0)  5.3 us
    all_gather x1, blocking collectives, per_device(): lax.all_gather(field.reshape(nx * nh, -1, GRID), CO, axis=0, tiled=True)  3.49 us
  transfers between devices with their start and end apart: 4, of which 4 were waited for; matrix products, arithmetic and copies ran while one was open for 5% of the time, Pallas kernels for 8%

profile of v2, /device:TPU:1, one launch (start us, length us, event | category | flops | bytes accessed | tf_op | source)
XLA Modules:
  0.0 143.3 jit_solution(8193731663659381947)
XLA Ops:
  0.0 0.0 copy-start
  0.0 0.9 convert_reduce_fusion.1
  0.9 0.7 pad_maximum_fusion
  1.5 0.7 broadcast_in_dim.32
  2.2 17.1 %all-to-all-start = ((bf16[64,8,128]{2,1,0:T(8,128)(2,1)}), bf16[64,8,128]{2,1,0:T(8,128)(2,1)S(1)}, u32[]{:S(2)}, u32[]{:S(2)}) async-start(bf16[64,8,128]{2,1,0:T(8,128)(2,1)} %broadcast_in_dim.32), calls=%async_computation | async-start | bytes 262144 | tf_op jit(solution)/shard_map/all_to_all | solution.py:207
  19.4 11.6 %all-to-all-done = bf16[64,8,128]{2,1,0:T(8,128)(2,1)S(1)} async-done(((bf16[64,8,128]{2,1,0:T(8,128)(2,1)}), bf16[64,8,128]{2,1,0:T(8,128)(2,1)S(1)}, u32[]{:S(2)}, u32[]{:S(2)}) %all-to-all-start) | async-done | bytes 131104 | tf_op jit(solution)/shard_map/all_to_all | solution.py:207
  31.0 0.1 slice_convert_fusion
  31.0 0.7 broadcast_in_dim.33
  31.8 4.0 %all-to-all-start.1 = ((bf16[4,256,128]{2,1,0:T(8,128)(2,1)}), bf16[4,256,128]{2,1,0:T(8,128)(2,1)S(1)}, u32[]{:S(2)}, u32[]{:S(2)}) async-start(bf16[4,256,128]{2,1,0:T(8,128)(2,1)} %broadcast_in_dim.33), calls=%async_computation.1 | async-start | bytes 524288 | tf_op jit(solution)/shard_map/all_to_all | solution.py:207
  35.8 0.7 broadcast_compare_fusion
  36.5 4.8 %all-to-all-done.1 = bf16[4,256,128]{2,1,0:T(8,128)(2,1)S(1)} async-done(((bf16[4,256,128]{2,1,0:T(8,128)(2,1)}), bf16[4,256,128]{2,1,0:T(8,128)(2,1)S(1)}, u32[]{:S(2)}, u32[]{:S(2)}) %all-to-all-start.1) | async-done | bytes 262176 | tf_op jit(solution)/shard_map/all_to_all | solution.py:207
  41.3 5.3 %all_gather.6 = bf16[2,8,128,128]{3,2,0,1:T(8,128)(2,1)S(1)} all-gather(bf16[1,8,128,128]{3,2,0,1:T(8,128)(2,1)S(1)} %bitcast.37), channel_id=1, replica_groups=mesh['tm_0'=4,'tm_1'=2,'tm_2'=2,'cell_0'=8,'cell_1'=4] {'tm_2'}, dimensions={0}, use_global_device_ids=true | all-gather | bytes 786432 | tf_op jit(solution)/shard_map/all_gather | solution.py:226
  46.6 0.3 bitcast_select_fusion
  47.0 0.5 fusion.11
  47.5 0.8 broadcast_in_dim.36
  48.3 9.2 %all-to-all-start.2 = ((bf16[256,4,128]{2,1,0:T(4,128)(2,1)}), bf16[256,4,128]{2,1,0:T(4,128)(2,1)S(1)}, u32[]{:S(2)}, u32[]{:S(2)}) async-start(bf16[256,4,128]{2,1,0:T(4,128)(2,1)} %bitcast.6), calls=%async_computation.2 | async-start | bytes 524288 | tf_op jit(solution)/shard_map/all_to_all | solution.py:207
  57.4 0.7 fusion.14
  58.1 0.0 copy-start.5
  58.1 0.0 copy-start.6
  58.1 11.3 %shard_map.109 = (bf16[64,16384]{1,0:T(8,128)(2,1)}, bf16[256,16384]{1,0:T(8,128)(2,1)}, bf16[16384,256]{1,0:T(8,128)(2,1)}) custom-call(s32[128,128]{1,0:T(8,128)} %bitcast.43, s32[128,128]{1,0:T(8,128)} %bitcast.42), custom_call_target="tpu_custom_call" | custom-call | flops 1000000000 | bytes 18874368 | tf_op jit(solution)/shard_map/pallas_call | solution.py:78
  69.5 2.7 %all-to-all-done.2 = bf16[256,4,128]{2,1,0:T(4,128)(2,1)S(1)} async-done(((bf16[256,4,128]{2,1,0:T(4,128)(2,1)}), bf16[256,4,128]{2,1,0:T(4,128)(2,1)S(1)}, u32[]{:S(2)}, u32[]{:S(2)}) %all-to-all-start.2) | async-done | bytes 262176 | tf_op jit(solution)/shard_map/all_to_all | solution.py:207
  72.1 3.5 %all_gather.7.field_ref = bf16[16,128,128]{2,1,0:T(8,128)(2,1)S(1)} all-gather(bf16[8,128,128]{2,1,0:T(8,128)(2,1)S(1)} %bitcast.36), channel_id=1, replica_groups=mesh['tm_0'=4,'tm_1'=2,'tm_2'=2,'cell_0'=8,'cell_1'=4] {'tm_2'}, dimensions={0}, use_global_device_ids=true | all-gather | bytes 786432 | tf_op jit(solution)/shard_map/all_gather | solution.py:234
  75.6 0.0 copy-start.7
  75.7 13.8 %shard_map.110 = bf16[512,128]{1,0:T(8,128)(2,1)} custom-call(s32[1]{0:T(128)} %bitcast.which_ref, f32[16,16]{1,0:T(8,128)S(1)} %copy-done.1, bf16[16,128,128]{2,1,0:T(8,128)(2,1)S(1)} %all_gather.7.field_ref, bf16[64,16384]{1,0:T(8,128)(2,1)} %get-tuple-element.12.low_hbm, bf16[256,16384]{1,0:T(8,128)(2,1)} %get-tuple-element.13.wide_hbm, ...), custom_call_target="tpu_custom_call" | custom-call | flops 10000000000 | bytes 18874368 | tf_op jit(solution)/shard_map/pallas_call | solution.py:188
  89.5 9.7 %all-to-all-start.3 = ((bf16[128,4,128]{2,1,0:T(4,128)(2,1)}), bf16[128,4,128]{2,1,0:T(4,128)(2,1)S(1)}, u32[]{:S(2)}, u32[]{:S(2)}) async-start(bf16[128,4,128]{2,1,0:T(4,128)(2,1)} %bitcast.13), calls=%async_computation.3 | async-start | bytes 262144 | tf_op jit(solution)/shard_map/all_to_all | solution.py:207
  99.3 5.8 %fusion.5 = bf16[2048,512]{1,0:T(8,128)(2,1)} fusion(s32[2048]{0:T(1024)S(1)} %bitcast.45, pred[2048]{0:T(1024)(128)(4,1)S(1)} %broadcast_compare_fusion, bf16[2048,1,512]{2,0,1:T(8,128)(2,1)S(1)} %copy-done), kind=kOutput, calls=%fused_computation.5 | convolution fusion | flops 4304404480 | bytes 4204544 | tf_op jit(solution)/shard_map/dot_general | solution.py:242
  105.0 5.0 %all-to-all-done.3 = bf16[128,4,128]{2,1,0:T(4,128)(2,1)S(1)} async-done(((bf16[128,4,128]{2,1,0:T(4,128)(2,1)}), bf16[128,4,128]{2,1,0:T(4,128)(2,1)S(1)}, u32[]{:S(2)}, u32[]{:S(2)}) %all-to-all-start.3) | async-done | bytes 131104 | tf_op jit(solution)/shard_map/all_to_all | solution.py:207
  110.1 2.3 %convolution_convert_fusion = bf16[2048,128]{1,0:T(8,128)(2,1)S(1)} fusion(bf16[2048,512]{1,0:T(8,128)(2,1)} %fusion.5, bf16[128,512]{1,0:T(8,128)(2,1)S(1)} %bitcast.40), kind=kOutput, calls=%fused_computation.6 | convolution fusion | flops 268697600 | bytes 2752512 | tf_op jit(solution)/shard_map/dot_general | solution.py:244
  112.4 5.8 %all_to_all.30 = bf16[2,1024,128]{2,1,0:T(8,128)(2,1)S(1)} all-to-all(bf16[2,1024,128]{2,1,0:T(8,128)(2,1)S(1)} %bitcast.35), channel_id=1, replica_groups=mesh['tm_0'=4,'tm_1'=2,'tm_2'=2,'cell_0'=8,'cell_1'=4] {'tm_2'}, dimensions={0} | all-to-all | bytes 1048576 | tf_op jit(solution)/shard_map/all_to_all | solution.py:207
  118.1 0.2 reduce_sum.21
  118.3 24.3 %all_to_all.31 = bf16[256,4,128]{2,1,0:T(4,128)(2,1)S(1)} all-to-all(bf16[256,4,128]{2,1,0:T(4,128)(2,1)S(1)} %bitcast.38), channel_id=1, replica_groups=mesh['tm_0'=4,'tm_1'=2,'tm_2'=2,'cell_0'=8,'cell_1'=4] {'tm_0','tm_1','c..., dimensions={0} | all-to-all | bytes 524288 | tf_op jit(solution)/shard_map/all_to_all | solution.py:207
  142.6 0.6 convert_reduce_fusion
  (16 shorter events, 0.1 us)
Async XLA Ops:
  0.0 47.0 %copy-start = (bf16[2048,1,512]{2,0,1:T(8,128)(2,1)S(1)}, bf16[2048,1,512]{2,0,1:T(8,128)(2,1)}, u32[]{:S(2)}) copy-start(bf16[2048,1,512]{2,0,1:T(8,128)(2,1)} %param.11) | copy-start | bytes 6291460
  2.2 28.7 %all-to-all-start = ((bf16[64,8,128]{2,1,0:T(8,128)(2,1)}), bf16[64,8,128]{2,1,0:T(8,128)(2,1)S(1)}, u32[]{:S(2)}, u32[]{:S(2)}) async-start(bf16[64,8,128]{2,1,0:T(8,128)(2,1)} %broadcast_in_dim.32), calls=%async_computation | async-start | bytes 262144 | tf_op jit(solution)/shard_map/all_to_all | solution.py:207
  31.8 9.5 %all-to-all-start.1 = ((bf16[4,256,128]{2,1,0:T(8,128)(2,1)}), bf16[4,256,128]{2,1,0:T(8,128)(2,1)S(1)}, u32[]{:S(2)}, u32[]{:S(2)}) async-start(bf16[4,256,128]{2,1,0:T(8,128)(2,1)} %broadcast_in_dim.33), calls=%async_computation.1 | async-start | bytes 524288 | tf_op jit(solution)/shard_map/all_to_all | solution.py:207
  48.3 23.9 %all-to-all-start.2 = ((bf16[256,4,128]{2,1,0:T(4,128)(2,1)}), bf16[256,4,128]{2,1,0:T(4,128)(2,1)S(1)}, u32[]{:S(2)}, u32[]{:S(2)}) async-start(bf16[256,4,128]{2,1,0:T(4,128)(2,1)} %bitcast.6), calls=%async_computation.2 | async-start | bytes 524288 | tf_op jit(solution)/shard_map/all_to_all | solution.py:207
  58.1 17.5 %copy-start.1 = (f32[16,16]{1,0:T(8,128)S(1)}, f32[16,16]{1,0:T(8,128)}, u32[]{:S(2)}) copy-start(f32[16,16]{1,0:T(8,128)} %weight_ref.1) | copy-start | bytes 3076
  58.1 17.5 %copy-start.2 = (f32[256,256]{1,0:T(8,128)S(1)}, f32[256,256]{1,0:T(8,128)}, u32[]{:S(2)}) copy-start(f32[256,256]{1,0:T(8,128)} %constant.41.clone.eigen_ref) | copy-start | bytes 786436
  58.1 17.5 %copy-start.3 = (bf16[128,256]{1,0:T(8,128)(2,1)S(1)}, bf16[128,256]{1,0:T(8,128)(2,1)}, u32[]{:S(2)}) copy-start(bf16[128,256]{1,0:T(8,128)(2,1)} %constant.40.clone.side_l) | copy-start | bytes 196612
  58.1 17.5 %copy-start.4 = (bf16[128,256]{1,0:T(8,128)(2,1)S(1)}, bf16[128,256]{1,0:T(8,128)(2,1)}, u32[]{:S(2)}) copy-start(bf16[128,256]{1,0:T(8,128)(2,1)} %constant.39.clone.side_h) | copy-start | bytes 196612
  58.1 17.5 %copy-start.5 = (bf16[256,128]{1,0:T(8,128)(2,1)S(1)}, bf16[256,128]{1,0:T(8,128)(2,1)}, u32[]{:S(2)}) copy-start(bf16[256,128]{1,0:T(8,128)(2,1)} %constant.38.clone.basis_l) | copy-start | bytes 196612
  58.1 17.5 %copy-start.6 = (bf16[256,128]{1,0:T(8,128)(2,1)S(1)}, bf16[256,128]{1,0:T(8,128)(2,1)}, u32[]{:S(2)}) copy-start(bf16[256,128]{1,0:T(8,128)(2,1)} %constant.37.clone.basis_h) | copy-start | bytes 196612
  75.6 13.8 %copy-start.7 = (s32[2048]{0:T(1024)S(1)}, s32[2048]{0:T(1024)}, u32[]{:S(2)}) copy-start(s32[2048]{0:T(1024)} %param.16) | copy-start | bytes 24580
  89.5 20.5 %all-to-all-start.3 = ((bf16[128,4,128]{2,1,0:T(4,128)(2,1)}), bf16[128,4,128]{2,1,0:T(4,128)(2,1)S(1)}, u32[]{:S(2)}, u32[]{:S(2)}) async-start(bf16[128,4,128]{2,1,0:T(4,128)(2,1)} %bitcast.13), calls=%async_computation.3 | async-start | bytes 262144 | tf_op jit(solution)/shard_map/all_to_all | solution.py:207

commit v3 on v2

v3 whole, which is shorter than its diff:
```python
import functools

import jax
import jax.numpy as jnp
import ml_dtypes
import numpy as np
from jax import lax
from jax.experimental import pallas as pl
from jax.experimental.pallas import tpu as pltpu
from jax.sharding import Mesh
from jax.sharding import PartitionSpec as P

LSCALE = 4
GRID = 128
PARTS = 2
LOW = GRID // PARTS
X, ZH, CO, Y, ZL = "tm_0", "tm_1", "tm_2", "cell_0", "cell_1"
CELL = (Y, ZL)
EVERY = (X, ZH, CO, Y, ZL)
BF16 = jnp.bfloat16
F32 = jnp.float32
VMEM = pl.BlockSpec(memory_space=pltpu.VMEM)
SMEM = pl.BlockSpec(memory_space=pltpu.SMEM)


def halves(array):
    high = array.astype(np.float32).astype(ml_dtypes.bfloat16)
    return high, (array - high.astype(np.float64)).astype(np.float32).astype(ml_dtypes.bfloat16)


def spectrum():
    size = 2 * GRID
    gap = np.arange(GRID, dtype=np.float32)
    distance = np.sqrt(gap[:, None] * gap[:, None] + gap[None, :] * gap[None, :])
    table = (np.exp(-distance / np.float32(LSCALE)) / np.float32(8.0 * LSCALE)).astype(ml_dtypes.bfloat16)
    table = table.astype(np.float64)
    wave = np.concatenate([np.arange(GRID + 1), np.arange(1, GRID)])
    angle = 2.0 * np.pi * wave[:, None] * np.arange(GRID)[None, :] / size
    basis = np.where(np.arange(size)[:, None] <= GRID, np.cos(angle), np.sin(angle))
    edge = (wave == 0) | (wave == GRID)
    basis = basis * np.where(edge, np.sqrt(1.0 / size), np.sqrt(2.0 / size))[:, None]
    fold = np.cos(angle) * np.where(np.arange(GRID) == 0, 1.0, 2.0)[None, :]
    eigen = fold @ table @ fold.T
    return (*halves(basis), *halves(basis.T), eigen.astype(np.float32))


def matmul(a, b):
    return jnp.dot(a, b, preferred_element_type=F32)


def parted(a):
    high = a.astype(BF16)
    return high, (a - high.astype(F32)).astype(BF16)


def matmul_parted(a, b):
    return matmul(a[0], b[0]) + (matmul(a[0], b[1]) + matmul(a[1], b[0]))


def hits(at, line):
    spread = jnp.broadcast_to(line.astype(F32), (16, line.shape[1])).astype(BF16)
    one = jnp.ones(spread.shape, BF16)
    zero = jnp.zeros(spread.shape, BF16)
    return [jnp.where(rows == spread, one, zero) for rows in at]


def spatial_kernel(lot, kept, which_ref, weight_ref, field_ref, rows_ref, cols_ref,
                   basis_h, basis_l, side_h, side_l, eigen_ref, out_ref, mixed, grid, low_ref, wide_ref):
    times, chunks, _ = field_ref.shape
    pair = 2
    which = which_ref[0]
    strides = times // kept

    def mix(j, carry):
        rows = pl.ds(pl.multiple_of(j * 16, 16), 16)
        totals = [None] * kept
        for k in range(times):
            t = (k % (times // pair)) * pair + k // (times // pair)
            value = field_ref[k, rows, :].astype(F32)
            for s in range(kept):
                term = weight_ref[s * strides + which, t] * value
                totals[s] = term if k == 0 else totals[s] + term
        for s in range(kept):
            mixed[s, rows, :] = totals[s].astype(BF16).astype(F32)
        return carry

    lax.fori_loop(0, chunks // 16, mix, 0)
    grid[...] = jnp.zeros_like(grid)
    first_at = lax.broadcasted_iota(jnp.int32, (16, GRID), 0).astype(F32)
    wide_at = [(first_at + float(k)).astype(BF16) for k in range(0, PARTS * GRID, 16)]
    low_at = wide_at[: LOW // 16]

    def put(j, carry):
        first = pl.multiple_of(j * lot, lot)
        values = [mixed[s, pl.ds(first, lot), :] for s in range(kept)]
        rows = rows_ref[pl.ds(first, lot), :]
        low = rows % LOW
        wide = (rows // LOW) * GRID + cols_ref[pl.ds(first, lot), :]
        lefts = []
        rights = []
        for g in range(lot):
            span = pl.ds(pl.multiple_of((first + g) * GRID, GRID), GRID)
            low_hit = hits(low_at, low[g : g + 1, :])
            wide_hit = jnp.concatenate(hits(wide_at, wide[g : g + 1, :]), axis=0)
            lines = [jnp.broadcast_to(v[g : g + 1, :], (16, GRID)).astype(BF16) for v in values]
            lefts.append(jnp.concatenate([hit * line for line in lines for hit in low_hit], axis=0))
            rights.append(wide_hit)
            low_ref[:, span] = jnp.concatenate(low_hit, axis=0)
            wide_ref[:, span] = wide_hit
        grid[...] += lax.dot_general(
            jnp.concatenate(lefts, axis=1),
            jnp.concatenate(rights, axis=1),
            (((1,), (1,)), ((), ())),
            preferred_element_type=F32,
        )
        return carry

    lax.fori_loop(0, chunks // lot, put, 0)
    basis = (basis_h[...], basis_l[...])
    side = (side_h[...], side_l[...])
    whole = jnp.concatenate(
        [
            grid[s * LOW : (s + 1) * LOW, p * GRID : (p + 1) * GRID]
            for s in range(kept)
            for p in range(PARTS)
        ],
        axis=0,
    )
    ahead = matmul_parted(parted(whole), side)
    for s in range(kept):
        waves = matmul_parted(basis, parted(ahead[s * GRID : (s + 1) * GRID])) * eigen_ref[...]
        back = matmul_parted(side, parted(waves))
        smooth = matmul_parted(parted(back), basis)
        for p in range(PARTS):
            grid[s * LOW : (s + 1) * LOW, p * GRID : (p + 1) * GRID] = smooth[p * LOW : (p + 1) * LOW]
    weighted = grid[...].astype(BF16)

    def take(j, carry):
        first = pl.multiple_of(j * lot, lot)
        span = pl.ds(pl.multiple_of(first * GRID, lot * GRID), lot * GRID)
        picked = matmul(weighted, wide_ref[:, span])
        hit = low_ref[:, span].astype(F32)
        for s in range(kept):
            line = jnp.sum(picked[s * LOW : (s + 1) * LOW] * hit, axis=0, keepdims=True)
            block = jnp.concatenate([line[:, g * GRID : (g + 1) * GRID] for g in range(lot)], axis=0)
            out_ref[pl.ds(pl.multiple_of(s * chunks + first, lot), lot), :] = block.astype(BF16)
        return carry

    lax.fori_loop(0, chunks // lot, take, 0)


def spatial(which, weight, field, rows, cols, kept):
    chunks = field.shape[1]
    constants = [jnp.asarray(c) for c in spectrum()]
    return pl.pallas_call(
        functools.partial(spatial_kernel, 64, kept),
        out_shape=jax.ShapeDtypeStruct((kept * chunks, GRID), BF16),
        in_specs=[SMEM] * 2 + [VMEM] * (3 + len(constants)),
        out_specs=VMEM,
        scratch_shapes=[
            pltpu.VMEM((kept, chunks, GRID), F32),
            pltpu.VMEM((kept * LOW, PARTS * GRID), F32),
            pltpu.VMEM((LOW, chunks * GRID), BF16),
            pltpu.VMEM((PARTS * GRID, chunks * GRID), BF16),
        ],
        compiler_params=pltpu.CompilerParams(vmem_limit_bytes=48 << 20),
        cost_estimate=pl.CostEstimate(flops=10**10, bytes_accessed=18 << 20, transcendentals=0),
    )(which, weight, field, rows, cols, *constants)


def opening_kernel(half_ref, duals_ref, coords_ref, out_ref):
    width = coords_ref.shape[1]
    picked = jnp.where(half_ref[0] == 0, coords_ref[0:1, :], coords_ref[1:2, :]).astype(F32)
    lines = [picked[:, k : k + GRID] for k in range(0, width, GRID)]
    block = jnp.concatenate([duals_ref[...].astype(F32), *lines], axis=0).astype(BF16)
    out_ref[...] = jnp.broadcast_to(block, out_ref.shape)


def opening(half, duals, coords, count):
    rows = duals.shape[0] + coords.shape[1] // GRID
    return pl.pallas_call(
        opening_kernel,
        out_shape=jax.ShapeDtypeStruct((count, rows, GRID), BF16),
        in_specs=[SMEM, VMEM, VMEM],
        out_specs=VMEM,
    )(half, duals, coords)


def exchange(pieces, axes):
    return lax.all_to_all(pieces, axes, split_axis=0, concat_axis=0, tiled=True)


def copies(array, axes):
    return exchange(jnp.broadcast_to(array, (lax.axis_size(axes), *array.shape)), axes)


def per_device(sensitivity, duals, time_cov, cell_coords, obs_time, obs_owner):
    obs = sensitivity.shape[0]
    own, reals = duals.shape
    flat = sensitivity.reshape(obs, -1)
    live = lax.axis_index((X, ZH, CO)) <= obs_time
    nx, nh, pair = (lax.axis_size(a) for a in (X, ZH, CO))
    which = lax.axis_index((ZH, CO)).reshape(1)

    plane = (ZH, Y, ZL)
    first = exchange(opening(lax.axis_index(ZH).reshape(1), duals, cell_coords, lax.axis_size(plane)), plane)
    coords = first[:, own:].reshape(nh, -1, GRID).astype(jnp.int32)
    second = copies(first[:, :own].reshape(-1, reals), X)
    third = lax.all_gather(second.reshape(nx * nh, -1, reals), CO, axis=0)
    all_duals = third.transpose(1, 0, 2, 3).reshape(obs, reals)

    seen = jnp.where(live[:, None], all_duals, jnp.zeros((), BF16))
    adjoint = lax.dot_general(seen, flat, (((0,), (0,)), ((), ())), preferred_element_type=F32).astype(BF16)
    pieces = adjoint.reshape(nx, 1, reals // nx, -1, GRID)
    pieces = jnp.broadcast_to(pieces, (nx, nh, *pieces.shape[2:]))
    pieces, slots = lax.optimization_barrier((pieces, obs_owner))
    field = exchange(pieces.reshape(-1, *pieces.shape[3:]), (X, ZH, Y, ZL))
    slots = slots.reshape(nx * nh, pair, -1).transpose(1, 0, 2).reshape(-1)
    chosen = (slots[:, None] == jnp.arange(obs, dtype=jnp.int32)[None, :]) & live[None, :]
    picked = jnp.dot(chosen.astype(BF16), flat, preferred_element_type=F32).astype(BF16)
    field, picked = lax.optimization_barrier((field, picked))
    field = lax.all_gather(field.reshape(nx * nh, -1, GRID), CO, axis=0, tiled=True)

    weighted = spatial(which, time_cov, field, coords[0], coords[1], nx)
    weighted = exchange(weighted.reshape(reals, -1, GRID), (X, Y, ZL)).reshape(reals, -1)
    product = lax.dot_general(picked, weighted, (((1,), (1,)), ((), ())), preferred_element_type=F32).astype(BF16)
    product = exchange(product.reshape(pair, -1, reals), CO)
    product = jnp.sum(product.astype(F32), axis=0).astype(BF16)
    product = exchange(product.reshape(-1, own, reals), (X, ZH, Y, ZL))
    return jnp.sum(product.astype(F32), axis=0)


def solution(mesh):
    split = Mesh(mesh.devices.reshape(4, 2, 2, 8, 4), EVERY)
    every = P(EVERY, None)
    return jax.shard_map(
        per_device,
        mesh=split,
        in_specs=(P(None, (X, ZH, CO), CELL), every, P(), P(None, CELL), P(), P()),
        out_specs=every,
        check_vma=False,
    )
```

time: 144 us -> 134 us (0.931)
  blocking collectives: 38.9 us -> 55.9 us
  Pallas kernels: 25.2 us -> 11.8 us
  starting transfers between devices: 40 us -> 30.3 us
  matrix products: 8.56 us -> 6.95 us
  other arithmetic: 3.47 us -> 1.93 us
    all_to_all x2 -> x3, blocking collectives: 30.1 us -> 46.9 us  [exchange(): return lax.all_to_all(pieces, axes, split_axis=0, concat_axis=0, tiled=True)]
    pallas_call x2, Pallas kernels: 25.2 us -> 11.8 us  [the longest x1 10.3 us: spatial(): pl.pallas_call(functools.partial(spatial_kernel, 64, kept), out_shape=jax...]
    all_to_all x4 -> x3, starting transfers between devices: 40 us -> 30.3 us  [exchange(): return lax.all_to_all(pieces, axes, split_axis=0, concat_axis=0, tiled=True)]
    dot_general x1, matrix products: 2.3 us -> 0.71 us  [per_device(): lax.dot_general(picked, weighted, (((1,), (1,)), ((), ())), preferred_ele...]
    all_to_all x4 -> x3, waiting for transfers between devices: 24.1 us -> 25.2 us  [exchange(): return lax.all_to_all(pieces, axes, split_axis=0, concat_axis=0, tiled=True)]
  transfers between devices with their start and end apart: 4 -> 3, of which waited for: 4 -> 3; matrix products, arithmetic and copies ran while one was open for 5% -> 5% of each run, Pallas kernels for 8% -> 0%
where the time goes in v3:
time: 134 us
  blocking collectives  55.9 us (42%)
  starting transfers between devices  30.3 us (23%)
  waiting for transfers between devices  25.2 us (19%)
  Pallas kernels  11.8 us (9%)
  matrix products  6.95 us (5%)
  other arithmetic  1.93 us (1%)
  local copies, waits for them, and re-layouts  1.62 us (1%)
    all_to_all x3, blocking collectives, exchange(): return lax.all_to_all(pieces, axes, split_axis=0, concat_axis=0, tiled=True)  46.9 us
    all_to_all x3, starting transfers between devices, exchange(): return lax.all_to_all(pieces, axes, split_axis=0, concat_axis=0, tiled=True)  30.3 us
    all_to_all x3, waiting for transfers between devices, exchange(): return lax.all_to_all(pieces, axes, split_axis=0, concat_axis=0, tiled=True)  25.2 us
    pallas_call x1, Pallas kernels, spatial(): pl.pallas_call(functools.partial(spatial_kernel, 64, kept), out_shape=jax...  10.3 us
    dot_general x1, matrix products, per_device(): jnp.dot(chosen.astype(BF16), flat, preferred_element_type=F32).astype(BF16)  5.77 us
    all_gather x1, blocking collectives, per_device(): third = lax.all_gather(second.reshape(nx * nh, -1, reals), CO, axis=0)  5.3 us
    all_gather x1, blocking collectives, per_device(): lax.all_gather(field.reshape(nx * nh, -1, GRID), CO, axis=0, tiled=True)  3.68 us
  transfers between devices with their start and end apart: 3, of which 3 were waited for; matrix products, arithmetic and copies ran while one was open for 5% of the time, Pallas kernels for 0%

profile of v3, /device:TPU:1, one launch (start us, length us, event | category | flops | bytes accessed | tf_op | source)
XLA Modules:
  0.0 133.9 jit_solution(494998943865922554)
XLA Ops:
  0.0 0.0 copy-start
  0.0 1.5 %shard_map.109 = bf16[64,8,128]{2,1,0:T(8,128)(2,1)} custom-call(s32[1]{0:T(128)} %bitcast.half_ref, bf16[4,128]{1,0:T(4,128)(2,1)} %duals_ref.1, s32[2,512]{1,0:T(2,128)} %coords_ref.1), custom_call_target="tpu_custom_call" | custom-call | tf_op jit(solution)/shard_map/pallas_call | solution.py:181
  1.5 17.1 %all-to-all-start = ((bf16[64,8,128]{2,1,0:T(8,128)(2,1)}), bf16[64,8,128]{2,1,0:T(8,128)(2,1)S(1)}, u32[]{:S(2)}, u32[]{:S(2)}) async-start(bf16[64,8,128]{2,1,0:T(8,128)(2,1)} %shard_map.109), calls=%async_computation | async-start | bytes 262144 | tf_op jit(solution)/shard_map/all_to_all | solution.py:190
  18.7 0.7 broadcast_compare_fusion
  19.4 10.9 %all-to-all-done = bf16[64,8,128]{2,1,0:T(8,128)(2,1)S(1)} async-done(((bf16[64,8,128]{2,1,0:T(8,128)(2,1)}), bf16[64,8,128]{2,1,0:T(8,128)(2,1)S(1)}, u32[]{:S(2)}, u32[]{:S(2)}) %all-to-all-start) | async-done | bytes 131104 | tf_op jit(solution)/shard_map/all_to_all | solution.py:190
  30.3 0.1 slice_convert_fusion
  30.3 0.7 broadcast_in_dim.29
  31.1 4.0 %all-to-all-start.1 = ((bf16[4,256,128]{2,1,0:T(8,128)(2,1)}), bf16[4,256,128]{2,1,0:T(8,128)(2,1)S(1)}, u32[]{:S(2)}, u32[]{:S(2)}) async-start(bf16[4,256,128]{2,1,0:T(8,128)(2,1)} %broadcast_in_dim.29), calls=%async_computation.1 | async-start | bytes 524288 | tf_op jit(solution)/shard_map/all_to_all | solution.py:190
  35.1 5.5 %all-to-all-done.1 = bf16[4,256,128]{2,1,0:T(8,128)(2,1)S(1)} async-done(((bf16[4,256,128]{2,1,0:T(8,128)(2,1)}), bf16[4,256,128]{2,1,0:T(8,128)(2,1)S(1)}, u32[]{:S(2)}, u32[]{:S(2)}) %all-to-all-start.1) | async-done | bytes 262176 | tf_op jit(solution)/shard_map/all_to_all | solution.py:190
  40.6 5.3 %all_gather.6 = bf16[2,8,128,128]{3,2,0,1:T(8,128)(2,1)S(1)} all-gather(bf16[1,8,128,128]{3,2,0,1:T(8,128)(2,1)S(1)} %bitcast.38), channel_id=1, replica_groups=mesh['tm_0'=4,'tm_1'=2,'tm_2'=2,'cell_0'=8,'cell_1'=4] {'tm_2'}, dimensions={0}, use_global_device_ids=true | all-gather | bytes 786432 | tf_op jit(solution)/shard_map/all_gather | solution.py:209
  45.9 0.3 bitcast_select_fusion
  46.3 0.5 fusion.11
  46.8 0.8 broadcast_in_dim.32
  47.6 9.2 %all-to-all-start.2 = ((bf16[256,4,128]{2,1,0:T(4,128)(2,1)}), bf16[256,4,128]{2,1,0:T(4,128)(2,1)S(1)}, u32[]{:S(2)}, u32[]{:S(2)}) async-start(bf16[256,4,128]{2,1,0:T(4,128)(2,1)} %bitcast.6), calls=%async_computation.2 | async-start | bytes 524288 | tf_op jit(solution)/shard_map/all_to_all | solution.py:190
  56.7 0.0 copy-start.1
  56.7 0.0 copy-start.2
  56.7 0.0 copy-start.3
  56.8 0.0 copy-start.4
  56.8 0.0 copy-start.5
  56.8 0.0 copy-start.6
  56.8 5.8 %fusion.5 = bf16[2048,512]{1,0:T(8,128)(2,1)} fusion(s32[2048]{0:T(1024)S(1)} %bitcast.44, pred[2048]{0:T(1024)(128)(4,1)S(1)} %broadcast_compare_fusion, bf16[2048,1,512]{2,0,1:T(8,128)(2,1)S(1)} %copy-done), kind=kOutput, calls=%fused_computation.5 | convolution fusion | flops 4304404480 | bytes 4204544 | tf_op jit(solution)/shard_map/dot_general | solution.py:220
  62.6 8.8 %all-to-all-done.2 = bf16[256,4,128]{2,1,0:T(4,128)(2,1)S(1)} async-done(((bf16[256,4,128]{2,1,0:T(4,128)(2,1)}), bf16[256,4,128]{2,1,0:T(4,128)(2,1)S(1)}, u32[]{:S(2)}, u32[]{:S(2)}) %all-to-all-start.2) | async-done | bytes 262176 | tf_op jit(solution)/shard_map/all_to_all | solution.py:190
  71.4 3.7 %all_gather.7.field_ref = bf16[16,128,128]{2,1,0:T(8,128)(2,1)S(1)} all-gather(bf16[8,128,128]{2,1,0:T(8,128)(2,1)S(1)} %bitcast.39), channel_id=1, replica_groups=mesh['tm_0'=4,'tm_1'=2,'tm_2'=2,'cell_0'=8,'cell_1'=4] {'tm_2'}, dimensions={0}, use_global_device_ids=true | all-gather | bytes 786432 | tf_op jit(solution)/shard_map/all_gather | solution.py:222
  75.1 0.0 copy-done.1
  75.1 0.0 copy-done.3
  75.1 10.3 %shard_map.110 = bf16[512,128]{1,0:T(8,128)(2,1)S(1)} custom-call(s32[1]{0:T(128)} %bitcast.10.which_ref, f32[16,16]{1,0:T(8,128)S(1)} %copy-done.1, bf16[16,128,128]{2,1,0:T(8,128)(2,1)S(1)} %all_gather.7.field_ref, s32[128,128]{1,0:T(8,128)S(1)} %bitcast.35, s32[128,128]{1,0:T(8,128)S(1)} %bitcast.34, bf16[256,128]{1,0:T(8,128)(2,1)S(1)} %copy-done.6, ...), custom_call_target="tpu_custom_call" | custom-call | flops 10000000000 | bytes 18874368 | tf_op jit(solution)/shard_map/pallas_call | solution.py:155
  85.4 17.1 %all_to_all.30 = bf16[128,4,128]{2,1,0:T(4,128)(2,1)S(1)} all-to-all(bf16[128,4,128]{2,1,0:T(4,128)(2,1)S(1)} %bitcast.33), channel_id=1, replica_groups=mesh['tm_0'=4,'tm_1'=2,'tm_2'=2,'cell_0'=8,'cell_1'=4] {'tm_0','cell_0',..., dimensions={0} | all-to-all | bytes 262144 | tf_op jit(solution)/shard_map/all_to_all | solution.py:190
  102.5 0.7 convolution_convert_fusion
  103.2 5.4 %all_to_all.31 = bf16[2,1024,128]{2,1,0:T(8,128)(2,1)S(1)} all-to-all(bf16[2,1024,128]{2,1,0:T(8,128)(2,1)S(1)} %bitcast.37), channel_id=1, replica_groups=mesh['tm_0'=4,'tm_1'=2,'tm_2'=2,'cell_0'=8,'cell_1'=4] {'tm_2'}, dimensions={0} | all-to-all | bytes 1048576 | tf_op jit(solution)/shard_map/all_to_all | solution.py:190
  108.6 0.2 reduce_sum.21
  108.8 24.4 %all_to_all.32 = bf16[256,4,128]{2,1,0:T(4,128)(2,1)S(1)} all-to-all(bf16[256,4,128]{2,1,0:T(4,128)(2,1)S(1)} %bitcast.40), channel_id=1, replica_groups=mesh['tm_0'=4,'tm_1'=2,'tm_2'=2,'cell_0'=8,'cell_1'=4] {'tm_0','tm_1','c..., dimensions={0} | all-to-all | bytes 524288 | tf_op jit(solution)/shard_map/all_to_all | solution.py:190
  133.2 0.6 convert_reduce_fusion
  (13 shorter events, 0.1 us)
Async XLA Ops:
  0.0 46.3 %copy-start = (bf16[2048,1,512]{2,0,1:T(8,128)(2,1)S(1)}, bf16[2048,1,512]{2,0,1:T(8,128)(2,1)}, u32[]{:S(2)}) copy-start(bf16[2048,1,512]{2,0,1:T(8,128)(2,1)} %param.11) | copy-start | bytes 6291460
  1.5 28.7 %all-to-all-start = ((bf16[64,8,128]{2,1,0:T(8,128)(2,1)}), bf16[64,8,128]{2,1,0:T(8,128)(2,1)S(1)}, u32[]{:S(2)}, u32[]{:S(2)}) async-start(bf16[64,8,128]{2,1,0:T(8,128)(2,1)} %shard_map.109), calls=%async_computation | async-start | bytes 262144 | tf_op jit(solution)/shard_map/all_to_all | solution.py:190
  31.1 9.5 %all-to-all-start.1 = ((bf16[4,256,128]{2,1,0:T(8,128)(2,1)}), bf16[4,256,128]{2,1,0:T(8,128)(2,1)S(1)}, u32[]{:S(2)}, u32[]{:S(2)}) async-start(bf16[4,256,128]{2,1,0:T(8,128)(2,1)} %broadcast_in_dim.29), calls=%async_computation.1 | async-start | bytes 524288 | tf_op jit(solution)/shard_map/all_to_all | solution.py:190
  45.9 1.6 %copy-start.8 = (s32[2048]{0:T(1024)S(1)}, s32[2048]{0:T(1024)}, u32[]{:S(2)}) copy-start(s32[2048]{0:T(1024)} %param.16) | copy-start | bytes 24580
  47.6 23.9 %all-to-all-start.2 = ((bf16[256,4,128]{2,1,0:T(4,128)(2,1)}), bf16[256,4,128]{2,1,0:T(4,128)(2,1)S(1)}, u32[]{:S(2)}, u32[]{:S(2)}) async-start(bf16[256,4,128]{2,1,0:T(4,128)(2,1)} %bitcast.6), calls=%async_computation.2 | async-start | bytes 524288 | tf_op jit(solution)/shard_map/all_to_all | solution.py:190
  56.7 18.4 %copy-start.1 = (f32[16,16]{1,0:T(8,128)S(1)}, f32[16,16]{1,0:T(8,128)}, u32[]{:S(2)}) copy-start(f32[16,16]{1,0:T(8,128)} %weight_ref.1) | copy-start | bytes 3076
  56.7 18.4 %copy-start.2 = (f32[256,256]{1,0:T(8,128)S(1)}, f32[256,256]{1,0:T(8,128)}, u32[]{:S(2)}) copy-start(f32[256,256]{1,0:T(8,128)} %constant.39.clone.eigen_ref) | copy-start | bytes 786436
  56.7 18.4 %copy-start.3 = (bf16[128,256]{1,0:T(8,128)(2,1)S(1)}, bf16[128,256]{1,0:T(8,128)(2,1)}, u32[]{:S(2)}) copy-start(bf16[128,256]{1,0:T(8,128)(2,1)} %constant.38.clone.side_l) | copy-start | bytes 196612
  56.8 18.4 %copy-start.4 = (bf16[128,256]{1,0:T(8,128)(2,1)S(1)}, bf16[128,256]{1,0:T(8,128)(2,1)}, u32[]{:S(2)}) copy-start(bf16[128,256]{1,0:T(8,128)(2,1)} %constant.37.clone.side_h) | copy-start | bytes 196612
  56.8 18.3 %copy-start.5 = (bf16[256,128]{1,0:T(8,128)(2,1)S(1)}, bf16[256,128]{1,0:T(8,128)(2,1)}, u32[]{:S(2)}) copy-start(bf16[256,128]{1,0:T(8,128)(2,1)} %constant.36.clone.basis_l) | copy-start | bytes 196612
  56.8 18.3 %copy-start.6 = (bf16[256,128]{1,0:T(8,128)(2,1)S(1)}, bf16[256,128]{1,0:T(8,128)(2,1)}, u32[]{:S(2)}) copy-start(bf16[256,128]{1,0:T(8,128)(2,1)} %constant.35.clone.basis_h) | copy-start | bytes 196612
  75.1 27.4 %copy-start.7 = (bf16[2048,512]{1,0:T(8,128)(2,1)S(1)}, bf16[2048,512]{1,0:T(8,128)(2,1)}, u32[]{:S(2)}) copy-start(bf16[2048,512]{1,0:T(8,128)(2,1)} %fusion.5) | copy-start | bytes 6291460

commit v4 on v3

--- a/solution.py
+++ b/solution.py
@@ -64,27 +64,41 @@
     return [jnp.where(rows == spread, one, zero) for rows in at]
 
 
-def spatial_kernel(lot, kept, which_ref, weight_ref, field_ref, rows_ref, cols_ref,
+def spatial_kernel(lot, kept, folds, which_ref, cov_ref, field_ref, rows_ref, cols_ref,
                    basis_h, basis_l, side_h, side_l, eigen_ref, out_ref, mixed, grid, low_ref, wide_ref):
-    times, chunks, _ = field_ref.shape
+    chunks = rows_ref.shape[0]
+    sets = field_ref.shape[0]
+    height = kept * folds
+    blocks = chunks // folds
+    times = cov_ref.shape[1]
     pair = 2
+    high = sets // pair
     which = which_ref[0]
-    strides = times // kept
-
-    def mix(j, carry):
-        rows = pl.ds(pl.multiple_of(j * 16, 16), 16)
-        totals = [None] * kept
-        for k in range(times):
-            t = (k % (times // pair)) * pair + k // (times // pair)
-            value = field_ref[k, rows, :].astype(F32)
-            for s in range(kept):
-                term = weight_ref[s * strides + which, t] * value
-                totals[s] = term if k == 0 else totals[s] + term
+    line = lax.broadcasted_iota(jnp.int32, (height, times * folds), 0)
+    column = lax.broadcasted_iota(jnp.int32, (height, times * folds), 1)
+    weight = jnp.zeros(line.shape, F32)
+    for k in range(times):
+        core, rest = divmod(k, times // pair)
+        half, place = divmod(rest, times // sets)
+        t = (place * high + half) * pair + core
         for s in range(kept):
-            mixed[s, rows, :] = totals[s].astype(BF16).astype(F32)
-        return carry
-
-    lax.fori_loop(0, chunks // 16, mix, 0)
+            here = (line // folds == s) & (column // folds == k)
+            weight = jnp.where(here, cov_ref[s * sets + which, t], weight)
+    weight = jnp.where(line % folds == column % folds, weight, 0.0)
+    first_part = weight.astype(BF16)
+    rest = weight - first_part.astype(F32)
+    second_part = rest.astype(BF16)
+    third_part = (rest - second_part.astype(F32)).astype(BF16)
+    parts = jnp.concatenate([first_part, second_part, third_part], axis=0)
+    tall = field_ref.shape[1] // blocks
+    for c in range(0, blocks, 8):
+        columns = [
+            jnp.concatenate([field_ref[k, (c + i) * tall : (c + i + 1) * tall, :] for k in range(sets)], axis=0)
+            for i in range(8)
+        ]
+        got = matmul(parts, jnp.concatenate(columns, axis=1))
+        total = got[2 * height :] + got[height : 2 * height] + got[:height]
+        mixed[:, c * GRID : (c + 8) * GRID] = total.astype(BF16).astype(F32)
     grid[...] = jnp.zeros_like(grid)
     first_at = lax.broadcasted_iota(jnp.int32, (16, GRID), 0).astype(F32)
     wide_at = [(first_at + float(k)).astype(BF16) for k in range(0, PARTS * GRID, 16)]
@@ -92,7 +106,8 @@
 
     def put(j, carry):
         first = pl.multiple_of(j * lot, lot)
-        values = [mixed[s, pl.ds(first, lot), :] for s in range(kept)]
+        length = lot // folds * GRID
+        values = mixed[:, pl.ds(pl.multiple_of(j * length, length), length)]
         rows = rows_ref[pl.ds(first, lot), :]
         low = rows % LOW
         wide = (rows // LOW) * GRID + cols_ref[pl.ds(first, lot), :]
@@ -102,7 +117,9 @@
             span = pl.ds(pl.multiple_of((first + g) * GRID, GRID), GRID)
             low_hit = hits(low_at, low[g : g + 1, :])
             wide_hit = jnp.concatenate(hits(wide_at, wide[g : g + 1, :]), axis=0)
-            lines = [jnp.broadcast_to(v[g : g + 1, :], (16, GRID)).astype(BF16) for v in values]
+            column = slice(g // folds * GRID, (g // folds + 1) * GRID)
+            tops = [s * folds + g % folds for s in range(kept)]
+            lines = [jnp.broadcast_to(values[k : k + 1, column], (16, GRID)).astype(BF16) for k in tops]
             lefts.append(jnp.concatenate([hit * line for line in lines for hit in low_hit], axis=0))
             rights.append(wide_hit)
             low_ref[:, span] = jnp.concatenate(low_hit, axis=0)
@@ -126,7 +143,8 @@
         ],
         axis=0,
     )
-    ahead = matmul_parted(parted(whole), side)
+    exact = whole.astype(BF16)
+    ahead = matmul(exact, side[0]) + matmul(exact, side[1])
     for s in range(kept):
         waves = matmul_parted(basis, parted(ahead[s * GRID : (s + 1) * GRID])) * eigen_ref[...]
         back = matmul_parted(side, parted(waves))
@@ -149,23 +167,23 @@
     lax.fori_loop(0, chunks // lot, take, 0)
 
 
-def spatial(which, weight, field, rows, cols, kept):
-    chunks = field.shape[1]
+def spatial(which, time_cov, field, rows, cols, kept, folds):
+    chunks = rows.shape[0]
     constants = [jnp.asarray(c) for c in spectrum()]
     return pl.pallas_call(
-        functools.partial(spatial_kernel, 64, kept),
+        functools.partial(spatial_kernel, 64, kept, folds),
         out_shape=jax.ShapeDtypeStruct((kept * chunks, GRID), BF16),
         in_specs=[SMEM] * 2 + [VMEM] * (3 + len(constants)),
         out_specs=VMEM,
         scratch_shapes=[
-            pltpu.VMEM((kept, chunks, GRID), F32),
+            pltpu.VMEM((kept * folds, chunks // folds * GRID), F32),
             pltpu.VMEM((kept * LOW, PARTS * GRID), F32),
             pltpu.VMEM((LOW, chunks * GRID), BF16),
             pltpu.VMEM((PARTS * GRID, chunks * GRID), BF16),
         ],
         compiler_params=pltpu.CompilerParams(vmem_limit_bytes=48 << 20),
         cost_estimate=pl.CostEstimate(flops=10**10, bytes_accessed=18 << 20, transcendentals=0),
-    )(which, weight, field, rows, cols, *constants)
+    )(which, time_cov, field, rows, cols, *constants)
 
 
 def opening_kernel(half_ref, duals_ref, coords_ref, out_ref):
@@ -211,22 +229,27 @@
 
     seen = jnp.where(live[:, None], all_duals, jnp.zeros((), BF16))
     adjoint = lax.dot_general(seen, flat, (((0,), (0,)), ((), ())), preferred_element_type=F32).astype(BF16)
-    pieces = adjoint.reshape(nx, 1, reals // nx, -1, GRID)
-    pieces = jnp.broadcast_to(pieces, (nx, nh, *pieces.shape[2:]))
-    pieces, slots = lax.optimization_barrier((pieces, obs_owner))
-    field = exchange(pieces.reshape(-1, *pieces.shape[3:]), (X, ZH, Y, ZL))
-    slots = slots.reshape(nx * nh, pair, -1).transpose(1, 0, 2).reshape(-1)
+    folds = flat.shape[1] // GRID
+    part = reals // nx
+    pieces = exchange(adjoint.reshape(nx, part, folds, GRID), X)
+    slots = obs_owner.reshape(nx * nh, pair, -1).transpose(1, 0, 2).reshape(-1)
+    pieces, slots = lax.optimization_barrier((pieces, slots))
+    pieces = jnp.broadcast_to(pieces.transpose(1, 0, 2, 3)[None], (nh, part, nx, folds, GRID))
+    field = exchange(pieces.reshape(-1, nx * folds, GRID), plane)
+
     chosen = (slots[:, None] == jnp.arange(obs, dtype=jnp.int32)[None, :]) & live[None, :]
     picked = jnp.dot(chosen.astype(BF16), flat, preferred_element_type=F32).astype(BF16)
     field, picked = lax.optimization_barrier((field, picked))
-    field = lax.all_gather(field.reshape(nx * nh, -1, GRID), CO, axis=0, tiled=True)
-
-    weighted = spatial(which, time_cov, field, coords[0], coords[1], nx)
+    field = lax.all_gather(field.reshape(nh, -1, GRID), CO, axis=0, tiled=True)
+
+    weighted = spatial(which, time_cov, field, coords[0], coords[1], nx, folds)
     weighted = exchange(weighted.reshape(reals, -1, GRID), (X, Y, ZL)).reshape(reals, -1)
     product = lax.dot_general(picked, weighted, (((1,), (1,)), ((), ())), preferred_element_type=F32).astype(BF16)
     product = exchange(product.reshape(pair, -1, reals), CO)
     product = jnp.sum(product.astype(F32), axis=0).astype(BF16)
-    product = exchange(product.reshape(-1, own, reals), (X, ZH, Y, ZL))
+    product = exchange(product.reshape(nx, -1, reals), X)
+    product = jnp.sum(product.astype(F32), axis=0).astype(BF16)
+    product = exchange(product.reshape(-1, own, reals), plane)
     return jnp.sum(product.astype(F32), axis=0)
 
 

time: 134 us -> 139 us (1.037)
  blocking collectives: 55.9 us -> 58.2 us
  waiting for transfers between devices: 25.2 us -> 27.2 us
    all_to_all x3 -> x4, waiting for transfers between devices: 25.2 us -> 27.2 us  [exchange(): return lax.all_to_all(pieces, axes, split_axis=0, concat_axis=0, tiled=True)]
    all_gather x1, blocking collectives: 3.68 us -> 5.28 us  [per_device(): field = lax.all_gather(field.reshape(nh, -1, GRID), CO, axis=0, tiled=True)]
    all_to_all x3 -> x4, starting transfers between devices: 30.3 us -> 29.1 us  [exchange(): return lax.all_to_all(pieces, axes, split_axis=0, concat_axis=0, tiled=True)]
    all_to_all x3 -> x4, blocking collectives: 46.9 us -> 47.6 us  [exchange(): return lax.all_to_all(pieces, axes, split_axis=0, concat_axis=0, tiled=True)]
  transfers between devices with their start and end apart: 3 -> 4, of which waited for: 3 -> 4; matrix products, arithmetic and copies ran while one was open for 5% -> 5% of each run, Pallas kernels for 0% -> 0%
where the time goes in v4:
time: 139 us; the launch traced here: 138 us
  blocking collectives  58.2 us (42%)
  starting transfers between devices  29.1 us (21%)
  waiting for transfers between devices  27.2 us (20%)
  Pallas kernels  11.8 us (8%)
  matrix products  6.97 us (5%)
  local copies, waits for them, and re-layouts  3 us (2%)
  other arithmetic  1.94 us (1%)
    all_to_all x4, blocking collectives, exchange(): return lax.all_to_all(pieces, axes, split_axis=0, concat_axis=0, tiled=True)  47.6 us
    all_to_all x4, starting transfers between devices, exchange(): return lax.all_to_all(pieces, axes, split_axis=0, concat_axis=0, tiled=True)  29.1 us
    all_to_all x4, waiting for transfers between devices, exchange(): return lax.all_to_all(pieces, axes, split_axis=0, concat_axis=0, tiled=True)  27.2 us
    pallas_call x1, Pallas kernels, spatial(): pl.pallas_call(functools.partial(spatial_kernel, 64, kept, folds), out_sh...  10.3 us
    dot_general x1, matrix products, per_device(): jnp.dot(chosen.astype(BF16), flat, preferred_element_type=F32).astype(BF16)  5.8 us
    all_gather x1, blocking collectives, per_device(): third = lax.all_gather(second.reshape(nx * nh, -1, reals), CO, axis=0)  5.3 us
    all_gather x1, blocking collectives, per_device(): field = lax.all_gather(field.reshape(nh, -1, GRID), CO, axis=0, tiled=True)  5.28 us
  transfers between devices with their start and end apart: 4, of which 4 were waited for; matrix products, arithmetic and copies ran while one was open for 5% of the time, Pallas kernels for 0%

profile of v4, /device:TPU:1, one launch (start us, length us, event | category | flops | bytes accessed | tf_op | source)
XLA Modules:
  0.0 138.4 jit_solution(13276701954186570046)
XLA Ops:
  0.0 1.5 %shard_map.109 = bf16[64,8,128]{2,1,0:T(8,128)(2,1)} custom-call(s32[1]{0:T(128)} %bitcast.half_ref, bf16[4,128]{1,0:T(4,128)(2,1)} %duals_ref.1, s32[2,512]{1,0:T(2,128)} %coords_ref.1), custom_call_target="tpu_custom_call" | custom-call | tf_op jit(solution)/shard_map/pallas_call | solution.py:199
  1.5 17.1 %all-to-all-start = ((bf16[64,8,128]{2,1,0:T(8,128)(2,1)}), bf16[64,8,128]{2,1,0:T(8,128)(2,1)S(1)}, u32[]{:S(2)}, u32[]{:S(2)}) async-start(bf16[64,8,128]{2,1,0:T(8,128)(2,1)} %shard_map.109), calls=%async_computation | async-start | bytes 262144 | tf_op jit(solution)/shard_map/all_to_all | solution.py:208
  18.7 11.6 %all-to-all-done = bf16[64,8,128]{2,1,0:T(8,128)(2,1)S(1)} async-done(((bf16[64,8,128]{2,1,0:T(8,128)(2,1)}), bf16[64,8,128]{2,1,0:T(8,128)(2,1)S(1)}, u32[]{:S(2)}, u32[]{:S(2)}) %all-to-all-start) | async-done | bytes 131104 | tf_op jit(solution)/shard_map/all_to_all | solution.py:208
  30.3 0.1 slice_convert_fusion
  30.3 0.7 broadcast_in_dim.29
  31.1 4.0 %all-to-all-start.1 = ((bf16[4,256,128]{2,1,0:T(8,128)(2,1)}), bf16[4,256,128]{2,1,0:T(8,128)(2,1)S(1)}, u32[]{:S(2)}, u32[]{:S(2)}) async-start(bf16[4,256,128]{2,1,0:T(8,128)(2,1)} %broadcast_in_dim.29), calls=%async_computation.1 | async-start | bytes 524288 | tf_op jit(solution)/shard_map/all_to_all | solution.py:208
  35.1 0.7 broadcast_compare_fusion
  35.8 0.7 copy.34
  36.5 4.1 %all-to-all-done.1 = bf16[4,256,128]{2,1,0:T(8,128)(2,1)S(1)} async-done(((bf16[4,256,128]{2,1,0:T(8,128)(2,1)}), bf16[4,256,128]{2,1,0:T(8,128)(2,1)S(1)}, u32[]{:S(2)}, u32[]{:S(2)}) %all-to-all-start.1) | async-done | bytes 262176 | tf_op jit(solution)/shard_map/all_to_all | solution.py:208
  40.6 5.3 %all_gather.6 = bf16[2,8,128,128]{3,2,0,1:T(8,128)(2,1)S(1)} all-gather(bf16[1,8,128,128]{3,2,0,1:T(8,128)(2,1)S(1)} %bitcast.40), channel_id=1, replica_groups=mesh['tm_0'=4,'tm_1'=2,'tm_2'=2,'cell_0'=8,'cell_1'=4] {'tm_2'}, dimensions={0}, use_global_device_ids=true | all-gather | bytes 786432 | tf_op jit(solution)/shard_map/all_gather | solution.py:227
  45.9 0.3 bitcast_select_fusion
  46.3 0.5 fusion.11
  46.7 0.7 reshape.62
  47.4 3.3 %all-to-all-start.2 = ((bf16[4,32,4,128]{3,2,1,0:T(4,128)(2,1)}), bf16[4,32,4,128]{3,2,1,0:T(4,128)(2,1)S(1)}, u32[]{:S(2)}, u32[]{:S(2)}) async-start(bf16[4,32,4,128]{3,2,1,0:T(4,128)(2,1)} %reshape.62), calls=%async_computation.2 | async-start | bytes 262144 | tf_op jit(solution)/shard_map/all_to_all | solution.py:208
  50.8 4.8 %all-to-all-done.2 = bf16[4,32,4,128]{3,2,1,0:T(4,128)(2,1)S(1)} async-done(((bf16[4,32,4,128]{3,2,1,0:T(4,128)(2,1)}), bf16[4,32,4,128]{3,2,1,0:T(4,128)(2,1)S(1)}, u32[]{:S(2)}, u32[]{:S(2)}) %all-to-all-start.2) | async-done | bytes 131104 | tf_op jit(solution)/shard_map/all_to_all | solution.py:208
  55.6 0.8 broadcast_in_dim.31
  56.4 4.6 %all-to-all-start.3 = ((bf16[64,16,128]{2,1,0:T(8,128)(2,1)}), bf16[64,16,128]{2,1,0:T(8,128)(2,1)S(1)}, u32[]{:S(2)}, u32[]{:S(2)}) async-start(bf16[64,16,128]{2,1,0:T(8,128)(2,1)} %bitcast.10), calls=%async_computation.3 | async-start | bytes 524288 | tf_op jit(solution)/shard_map/all_to_all | solution.py:208
  61.0 0.0 copy-start.3
  61.0 0.0 copy-start.4
  61.1 0.0 copy-start.5
  61.1 0.0 copy-start.6
  61.1 5.8 %fusion.5 = bf16[2048,512]{1,0:T(8,128)(2,1)} fusion(s32[2048]{0:T(1024)S(1)} %bitcast.48, pred[2048]{0:T(1024)(128)(4,1)S(1)} %broadcast_compare_fusion, bf16[2048,1,512]{2,0,1:T(8,128)(2,1)S(1)} %copy-done), kind=kOutput, calls=%fused_computation.5 | convolution fusion | flops 4304404480 | bytes 4204544 | tf_op jit(solution)/shard_map/dot_general | solution.py:241
  66.9 6.7 %all-to-all-done.3 = bf16[64,16,128]{2,1,0:T(8,128)(2,1)S(1)} async-done(((bf16[64,16,128]{2,1,0:T(8,128)(2,1)}), bf16[64,16,128]{2,1,0:T(8,128)(2,1)S(1)}, u32[]{:S(2)}, u32[]{:S(2)}) %all-to-all-start.3) | async-done | bytes 262176 | tf_op jit(solution)/shard_map/all_to_all | solution.py:208
  73.6 5.3 %all_gather.7.field_ref = bf16[4,512,128]{2,1,0:T(8,128)(2,1)S(1)} all-gather(bf16[2,512,128]{2,1,0:T(8,128)(2,1)S(1)} %bitcast.41), channel_id=1, replica_groups=mesh['tm_0'=4,'tm_1'=2,'tm_2'=2,'cell_0'=8,'cell_1'=4] {'tm_2'}, dimensions={0}, use_global_device_ids=true | all-gather | bytes 786432 | tf_op jit(solution)/shard_map/all_gather | solution.py:243
  78.9 10.3 %shard_map.110 = bf16[512,128]{1,0:T(8,128)(2,1)S(1)} custom-call(s32[1]{0:T(128)} %bitcast.11.which_ref, f32[16,16]{1,0:T(8,128)S(1)} %copy-done.1, bf16[4,512,128]{2,1,0:T(8,128)(2,1)S(1)} %all_gather.7.field_ref, s32[128,128]{1,0:T(8,128)S(1)} %bitcast.37, s32[128,128]{1,0:T(8,128)S(1)} %bitcast.36, bf16[256,128]{1,0:T(8,128)(2,1)S(1)} %copy-done.6, ...), custom_call_target="tpu_custom_call" | custom-call | flops 10000000000 | bytes 18874368 | tf_op jit(solution)/shard_map/pallas_call | solution.py:173
  89.2 17.0 %all_to_all.40 = bf16[128,4,128]{2,1,0:T(4,128)(2,1)S(1)} all-to-all(bf16[128,4,128]{2,1,0:T(4,128)(2,1)S(1)} %bitcast.35), channel_id=1, replica_groups=mesh['tm_0'=4,'tm_1'=2,'tm_2'=2,'cell_0'=8,'cell_1'=4] {'tm_0','cell_0',..., dimensions={0} | all-to-all | bytes 262144 | tf_op jit(solution)/shard_map/all_to_all | solution.py:208
  106.2 0.7 convolution_convert_fusion
  106.9 5.5 %all_to_all.41 = bf16[2,1024,128]{2,1,0:T(8,128)(2,1)S(1)} all-to-all(bf16[2,1024,128]{2,1,0:T(8,128)(2,1)S(1)} %bitcast.39), channel_id=1, replica_groups=mesh['tm_0'=4,'tm_1'=2,'tm_2'=2,'cell_0'=8,'cell_1'=4] {'tm_2'}, dimensions={0} | all-to-all | bytes 1048576 | tf_op jit(solution)/shard_map/all_to_all | solution.py:208
  112.3 0.2 reduce_sum.33
  112.5 8.6 %all_to_all.42 = bf16[4,256,128]{2,1,0:T(8,128)(2,1)S(1)} all-to-all(bf16[4,256,128]{2,1,0:T(8,128)(2,1)S(1)} %bitcast.42), channel_id=1, replica_groups=mesh['tm_0'=4,'tm_1'=2,'tm_2'=2,'cell_0'=8,'cell_1'=4] {'tm_0'}, dimensions={0} | all-to-all | bytes 524288 | tf_op jit(solution)/shard_map/all_to_all | solution.py:208
  121.2 16.6 %all_to_all.43 = bf16[64,4,128]{2,1,0:T(4,128)(2,1)S(1)} all-to-all(bf16[64,4,128]{2,1,0:T(4,128)(2,1)S(1)} %bitcast.46), channel_id=1, replica_groups=mesh['tm_0'=4,'tm_1'=2,'tm_2'=2,'cell_0'=8,'cell_1'=4] {'tm_1','cell_0',..., dimensions={0} | all-to-all | bytes 131072 | tf_op jit(solution)/shard_map/all_to_all | solution.py:208
  137.8 0.6 convert_reduce_fusion
  (16 shorter events, 0.1 us)
Async XLA Ops:
  0.0 46.3 %copy-start = (bf16[2048,1,512]{2,0,1:T(8,128)(2,1)S(1)}, bf16[2048,1,512]{2,0,1:T(8,128)(2,1)}, u32[]{:S(2)}) copy-start(bf16[2048,1,512]{2,0,1:T(8,128)(2,1)} %param.11) | copy-start | bytes 6291460
  1.5 28.7 %all-to-all-start = ((bf16[64,8,128]{2,1,0:T(8,128)(2,1)}), bf16[64,8,128]{2,1,0:T(8,128)(2,1)S(1)}, u32[]{:S(2)}, u32[]{:S(2)}) async-start(bf16[64,8,128]{2,1,0:T(8,128)(2,1)} %shard_map.109), calls=%async_computation | async-start | bytes 262144 | tf_op jit(solution)/shard_map/all_to_all | solution.py:208
  31.1 9.5 %all-to-all-start.1 = ((bf16[4,256,128]{2,1,0:T(8,128)(2,1)}), bf16[4,256,128]{2,1,0:T(8,128)(2,1)S(1)}, u32[]{:S(2)}, u32[]{:S(2)}) async-start(bf16[4,256,128]{2,1,0:T(8,128)(2,1)} %broadcast_in_dim.29), calls=%async_computation.1 | async-start | bytes 524288 | tf_op jit(solution)/shard_map/all_to_all | solution.py:208
  47.4 8.1 %all-to-all-start.2 = ((bf16[4,32,4,128]{3,2,1,0:T(4,128)(2,1)}), bf16[4,32,4,128]{3,2,1,0:T(4,128)(2,1)S(1)}, u32[]{:S(2)}, u32[]{:S(2)}) async-start(bf16[4,32,4,128]{3,2,1,0:T(4,128)(2,1)} %reshape.62), calls=%async_computation.2 | async-start | bytes 262144 | tf_op jit(solution)/shard_map/all_to_all | solution.py:208
  56.4 17.2 %all-to-all-start.3 = ((bf16[64,16,128]{2,1,0:T(8,128)(2,1)}), bf16[64,16,128]{2,1,0:T(8,128)(2,1)S(1)}, u32[]{:S(2)}, u32[]{:S(2)}) async-start(bf16[64,16,128]{2,1,0:T(8,128)(2,1)} %bitcast.10), calls=%async_computation.3 | async-start | bytes 524288 | tf_op jit(solution)/shard_map/all_to_all | solution.py:208
  61.0 17.8 %copy-start.1 = (f32[16,16]{1,0:T(8,128)S(1)}, f32[16,16]{1,0:T(8,128)}, u32[]{:S(2)}) copy-start(f32[16,16]{1,0:T(8,128)} %cov_ref.1) | copy-start | bytes 3076
  61.0 17.8 %copy-start.2 = (f32[256,256]{1,0:T(8,128)S(1)}, f32[256,256]{1,0:T(8,128)}, u32[]{:S(2)}) copy-start(f32[256,256]{1,0:T(8,128)} %constant.40.clone.eigen_ref) | copy-start | bytes 786436
  61.0 17.8 %copy-start.3 = (bf16[128,256]{1,0:T(8,128)(2,1)S(1)}, bf16[128,256]{1,0:T(8,128)(2,1)}, u32[]{:S(2)}) copy-start(bf16[128,256]{1,0:T(8,128)(2,1)} %constant.39.clone.side_l) | copy-start | bytes 196612
  61.0 17.8 %copy-start.4 = (bf16[128,256]{1,0:T(8,128)(2,1)S(1)}, bf16[128,256]{1,0:T(8,128)(2,1)}, u32[]{:S(2)}) copy-start(bf16[128,256]{1,0:T(8,128)(2,1)} %constant.38.clone.side_h) | copy-start | bytes 196612
  61.1 17.8 %copy-start.5 = (bf16[256,128]{1,0:T(8,128)(2,1)S(1)}, bf16[256,128]{1,0:T(8,128)(2,1)}, u32[]{:S(2)}) copy-start(bf16[256,128]{1,0:T(8,128)(2,1)} %constant.37.clone.basis_l) | copy-start | bytes 196612
  61.1 17.8 %copy-start.6 = (bf16[256,128]{1,0:T(8,128)(2,1)S(1)}, bf16[256,128]{1,0:T(8,128)(2,1)}, u32[]{:S(2)}) copy-start(bf16[256,128]{1,0:T(8,128)(2,1)} %constant.36.clone.basis_h) | copy-start | bytes 196612
  78.9 27.3 %copy-start.7 = (bf16[2048,512]{1,0:T(8,128)(2,1)S(1)}, bf16[2048,512]{1,0:T(8,128)(2,1)}, u32[]{:S(2)}) copy-start(bf16[2048,512]{1,0:T(8,128)(2,1)} %fusion.5) | copy-start | bytes 6291460

commit v5 on v3

--- a/solution.py
+++ b/solution.py
@@ -65,7 +65,7 @@
 
 
 def spatial_kernel(lot, kept, which_ref, weight_ref, field_ref, rows_ref, cols_ref,
-                   basis_h, basis_l, side_h, side_l, eigen_ref, out_ref, mixed, grid, low_ref, wide_ref):
+                   basis_h, basis_l, side_h, side_l, eigen_ref, out_ref, mixed, grid):
     times, chunks, _ = field_ref.shape
     pair = 2
     which = which_ref[0]
@@ -99,14 +99,10 @@
         lefts = []
         rights = []
         for g in range(lot):
-            span = pl.ds(pl.multiple_of((first + g) * GRID, GRID), GRID)
             low_hit = hits(low_at, low[g : g + 1, :])
-            wide_hit = jnp.concatenate(hits(wide_at, wide[g : g + 1, :]), axis=0)
             lines = [jnp.broadcast_to(v[g : g + 1, :], (16, GRID)).astype(BF16) for v in values]
             lefts.append(jnp.concatenate([hit * line for line in lines for hit in low_hit], axis=0))
-            rights.append(wide_hit)
-            low_ref[:, span] = jnp.concatenate(low_hit, axis=0)
-            wide_ref[:, span] = wide_hit
+            rights.append(jnp.concatenate(hits(wide_at, wide[g : g + 1, :]), axis=0))
         grid[...] += lax.dot_general(
             jnp.concatenate(lefts, axis=1),
             jnp.concatenate(rights, axis=1),
@@ -126,7 +122,8 @@
         ],
         axis=0,
     )
-    ahead = matmul_parted(parted(whole), side)
+    exact = whole.astype(BF16)
+    ahead = matmul(exact, side[0]) + matmul(exact, side[1])
     for s in range(kept):
         waves = matmul_parted(basis, parted(ahead[s * GRID : (s + 1) * GRID])) * eigen_ref[...]
         back = matmul_parted(side, parted(waves))
@@ -135,15 +132,23 @@
             grid[s * LOW : (s + 1) * LOW, p * GRID : (p + 1) * GRID] = smooth[p * LOW : (p + 1) * LOW]
     weighted = grid[...].astype(BF16)
 
+    line_at = lax.broadcasted_iota(jnp.int32, (LOW, GRID), 0)
+
     def take(j, carry):
         first = pl.multiple_of(j * lot, lot)
-        span = pl.ds(pl.multiple_of(first * GRID, lot * GRID), lot * GRID)
-        picked = matmul(weighted, wide_ref[:, span])
-        hit = low_ref[:, span].astype(F32)
+        rows = rows_ref[pl.ds(first, lot), :]
+        low = rows % LOW
+        wide = (rows // LOW) * GRID + cols_ref[pl.ds(first, lot), :]
+        rights = [jnp.concatenate(hits(wide_at, wide[g : g + 1, :]), axis=0) for g in range(lot)]
+        picked = matmul(weighted, jnp.concatenate(rights, axis=1))
+        hit = [line_at == low[g : g + 1, :] for g in range(lot)]
         for s in range(kept):
-            line = jnp.sum(picked[s * LOW : (s + 1) * LOW] * hit, axis=0, keepdims=True)
-            block = jnp.concatenate([line[:, g * GRID : (g + 1) * GRID] for g in range(lot)], axis=0)
-            out_ref[pl.ds(pl.multiple_of(s * chunks + first, lot), lot), :] = block.astype(BF16)
+            lines = []
+            for g in range(lot):
+                block = picked[s * LOW : (s + 1) * LOW, g * GRID : (g + 1) * GRID]
+                lines.append(jnp.sum(jnp.where(hit[g], block, 0.0), axis=0, keepdims=True))
+            span = pl.ds(pl.multiple_of(s * chunks + first, lot), lot)
+            out_ref[span, :] = jnp.concatenate(lines, axis=0).astype(BF16)
         return carry
 
     lax.fori_loop(0, chunks // lot, take, 0)
@@ -160,8 +165,6 @@
         scratch_shapes=[
             pltpu.VMEM((kept, chunks, GRID), F32),
             pltpu.VMEM((kept * LOW, PARTS * GRID), F32),
-            pltpu.VMEM((LOW, chunks * GRID), BF16),
-            pltpu.VMEM((PARTS * GRID, chunks * GRID), BF16),
         ],
         compiler_params=pltpu.CompilerParams(vmem_limit_bytes=48 << 20),
         cost_estimate=pl.CostEstimate(flops=10**10, bytes_accessed=18 << 20, transcendentals=0),
@@ -186,6 +189,35 @@
     )(half, duals, coords)
 
 
+def adjoint_kernel(here_ref, time_ref, duals_ref, flat_ref, out_ref):
+    pair, groups, rows, reals = duals_ref.shape
+    outer, again, part, folds, _ = out_ref.shape
+    times = time_ref[...].astype(F32).T
+    here = here_ref[0].astype(F32)
+    seen = []
+    for k in range(pair * groups):
+        block = duals_ref[k % pair, k // pair].astype(F32)
+        seen.append(jnp.where(times[:, k : k + 1] >= here, block, 0.0).astype(BF16))
+    total = lax.dot_general(
+        jnp.concatenate(seen, axis=0), flat_ref[...], (((0,), (0,)), ((), ())), preferred_element_type=F32
+    )
+    pieces = jnp.stack([total[:, k * GRID : (k + 1) * GRID] for k in range(folds)], axis=1).astype(BF16)
+    for i in range(outer):
+        for j in range(again):
+            out_ref[i, j] = pieces[i * part : (i + 1) * part]
+
+
+def adjoint(here, obs_time, duals, flat, outer, again):
+    rows, reals = duals.shape[2:]
+    return pl.pallas_call(
+        adjoint_kernel,
+        out_shape=jax.ShapeDtypeStruct((outer, again, reals // outer, flat.shape[1] // GRID, GRID), BF16),
+        in_specs=[SMEM] + [VMEM] * 3,
+        out_specs=VMEM,
+        compiler_params=pltpu.CompilerParams(vmem_limit_bytes=24 << 20),
+    )(here, obs_time.reshape(-1, rows), duals, flat)
+
+
 def exchange(pieces, axes):
     return lax.all_to_all(pieces, axes, split_axis=0, concat_axis=0, tiled=True)
 
@@ -198,7 +230,7 @@
     obs = sensitivity.shape[0]
     own, reals = duals.shape
     flat = sensitivity.reshape(obs, -1)
-    live = lax.axis_index((X, ZH, CO)) <= obs_time
+    here = lax.axis_index((X, ZH, CO))
     nx, nh, pair = (lax.axis_size(a) for a in (X, ZH, CO))
     which = lax.axis_index((ZH, CO)).reshape(1)
 
@@ -207,25 +239,27 @@
     coords = first[:, own:].reshape(nh, -1, GRID).astype(jnp.int32)
     second = copies(first[:, :own].reshape(-1, reals), X)
     third = lax.all_gather(second.reshape(nx * nh, -1, reals), CO, axis=0)
-    all_duals = third.transpose(1, 0, 2, 3).reshape(obs, reals)
-
-    seen = jnp.where(live[:, None], all_duals, jnp.zeros((), BF16))
-    adjoint = lax.dot_general(seen, flat, (((0,), (0,)), ((), ())), preferred_element_type=F32).astype(BF16)
-    pieces = adjoint.reshape(nx, 1, reals // nx, -1, GRID)
-    pieces = jnp.broadcast_to(pieces, (nx, nh, *pieces.shape[2:]))
-    pieces, slots = lax.optimization_barrier((pieces, obs_owner))
+    pieces = adjoint(here.reshape(1), obs_time, third, flat, nx, nh)
+    core = lax.axis_index(CO)
+    slots = obs_owner.reshape(nx * nh, pair, -1)
+    slots = jnp.concatenate([lax.dynamic_index_in_dim(slots, i, 1, keepdims=False) for i in (1 - core, core)])
+    live = here <= obs_time
+    pieces, slots, live = lax.optimization_barrier((pieces, slots, live))
     field = exchange(pieces.reshape(-1, *pieces.shape[3:]), (X, ZH, Y, ZL))
-    slots = slots.reshape(nx * nh, pair, -1).transpose(1, 0, 2).reshape(-1)
-    chosen = (slots[:, None] == jnp.arange(obs, dtype=jnp.int32)[None, :]) & live[None, :]
+    chosen = (slots.reshape(-1)[:, None] == jnp.arange(obs, dtype=jnp.int32)[None, :]) & live[None, :]
     picked = jnp.dot(chosen.astype(BF16), flat, preferred_element_type=F32).astype(BF16)
     field, picked = lax.optimization_barrier((field, picked))
     field = lax.all_gather(field.reshape(nx * nh, -1, GRID), CO, axis=0, tiled=True)
 
     weighted = spatial(which, time_cov, field, coords[0], coords[1], nx)
     weighted = exchange(weighted.reshape(reals, -1, GRID), (X, Y, ZL)).reshape(reals, -1)
-    product = lax.dot_general(picked, weighted, (((1,), (1,)), ((), ())), preferred_element_type=F32).astype(BF16)
-    product = exchange(product.reshape(pair, -1, reals), CO)
-    product = jnp.sum(product.astype(F32), axis=0).astype(BF16)
+    theirs, ours = (
+        lax.dot_general(rows, weighted, (((1,), (1,)), ((), ())), preferred_element_type=F32)
+        for rows in jnp.split(picked, pair)
+    )
+    swapped = lax.all_gather(theirs.astype(BF16), CO, axis=0)
+    got = lax.dynamic_index_in_dim(swapped, 1 - core, 0, keepdims=False)
+    product = (ours + got.astype(F32)).astype(BF16)
     product = exchange(product.reshape(-1, own, reals), (X, ZH, Y, ZL))
     return jnp.sum(product.astype(F32), axis=0)
 

time: 134 us -> 132 us (0.985)
  blocking collectives: 55.9 us -> 53.9 us
    all_to_all x3 -> x2, blocking collectives: 46.9 us -> 41.4 us  [exchange(): return lax.all_to_all(pieces, axes, split_axis=0, concat_axis=0, tiled=True)]
    all_gather x0 -> x1, blocking collectives: none -> 3.41 us  [per_device(): swapped = lax.all_gather(theirs.astype(BF16), CO, axis=0)]
    pallas_call x0 -> x1, Pallas kernels: none -> 1.93 us  [adjoint(): pl.pallas_call(adjoint_kernel, out_shape=jax.ShapeDtypeStruct((outer, aga...]
  transfers between devices with their start and end apart: 3 -> 3, of which waited for: 3 -> 3; matrix products, arithmetic and copies ran while one was open for 5% -> 6% of each run, Pallas kernels for 0% -> 0%
where the time goes in v5:
time: 132 us; the launch traced here: 131 us
  blocking collectives  53.9 us (41%)
  starting transfers between devices  30.2 us (23%)
  waiting for transfers between devices  24.4 us (18%)
  Pallas kernels  12.7 us (10%)
  matrix products  6.63 us (5%)
  other arithmetic  1.63 us (1%)
  local copies, waits for them, and re-layouts  1.58 us (1%)
    all_to_all x2, blocking collectives, exchange(): return lax.all_to_all(pieces, axes, split_axis=0, concat_axis=0, tiled=True)  41.4 us
    all_to_all x3, starting transfers between devices, exchange(): return lax.all_to_all(pieces, axes, split_axis=0, concat_axis=0, tiled=True)  30.2 us
    all_to_all x3, waiting for transfers between devices, exchange(): return lax.all_to_all(pieces, axes, split_axis=0, concat_axis=0, tiled=True)  24.4 us
    pallas_call x1, Pallas kernels, spatial(): pl.pallas_call(functools.partial(spatial_kernel, 64, kept), out_shape=jax...  9.28 us
    dot_general x1, matrix products, per_device(): jnp.dot(chosen.astype(BF16), flat, preferred_element_type=F32).astype(BF16)  5.77 us
    all_gather x1, blocking collectives, per_device(): third = lax.all_gather(second.reshape(nx * nh, -1, reals), CO, axis=0)  5.3 us
    all_gather x1, blocking collectives, per_device(): lax.all_gather(field.reshape(nx * nh, -1, GRID), CO, axis=0, tiled=True)  3.77 us
    all_gather x1, blocking collectives, per_device(): swapped = lax.all_gather(theirs.astype(BF16), CO, axis=0)  3.41 us
  transfers between devices with their start and end apart: 3, of which 3 were waited for; matrix products, arithmetic and copies ran while one was open for 6% of the time, Pallas kernels for 0%

profile of v5, /device:TPU:1, one launch (start us, length us, event | category | flops | bytes accessed | tf_op | source)
XLA Modules:
  0.0 131.3 jit_solution(9098013268046420654)
XLA Ops:
  0.0 1.5 %shard_map.109 = bf16[64,8,128]{2,1,0:T(8,128)(2,1)} custom-call(s32[1]{0:T(128)} %bitcast.2.half_ref, bf16[4,128]{1,0:T(4,128)(2,1)} %duals_ref.1, s32[2,512]{1,0:T(2,128)} %coords_ref.1), custom_call_target="tpu_custom_call" | custom-call | tf_op jit(solution)/shard_map/pallas_call | solution.py:184
  1.5 17.1 %all-to-all-start = ((bf16[64,8,128]{2,1,0:T(8,128)(2,1)}), bf16[64,8,128]{2,1,0:T(8,128)(2,1)S(1)}, u32[]{:S(2)}, u32[]{:S(2)}) async-start(bf16[64,8,128]{2,1,0:T(8,128)(2,1)} %shard_map.109), calls=%async_computation | async-start | bytes 262144 | tf_op jit(solution)/shard_map/all_to_all | solution.py:222
  18.7 0.8 constant_dynamic-slice_fusion.1
  19.5 0.7 broadcast_compare_fusion
  20.2 10.1 %all-to-all-done = bf16[64,8,128]{2,1,0:T(8,128)(2,1)S(1)} async-done(((bf16[64,8,128]{2,1,0:T(8,128)(2,1)}), bf16[64,8,128]{2,1,0:T(8,128)(2,1)S(1)}, u32[]{:S(2)}, u32[]{:S(2)}) %all-to-all-start) | async-done | bytes 131104 | tf_op jit(solution)/shard_map/all_to_all | solution.py:222
  30.3 0.1 slice_convert_fusion
  30.4 0.7 broadcast_in_dim.2
  31.1 4.0 %all-to-all-start.1 = ((bf16[4,256,128]{2,1,0:T(8,128)(2,1)}), bf16[4,256,128]{2,1,0:T(8,128)(2,1)S(1)}, u32[]{:S(2)}, u32[]{:S(2)}) async-start(bf16[4,256,128]{2,1,0:T(8,128)(2,1)} %broadcast_in_dim.2), calls=%async_computation.1 | async-start | bytes 524288 | tf_op jit(solution)/shard_map/all_to_all | solution.py:222
  35.1 5.5 %all-to-all-done.1 = bf16[4,256,128]{2,1,0:T(8,128)(2,1)S(1)} async-done(((bf16[4,256,128]{2,1,0:T(8,128)(2,1)}), bf16[4,256,128]{2,1,0:T(8,128)(2,1)S(1)}, u32[]{:S(2)}, u32[]{:S(2)}) %all-to-all-start.1) | async-done | bytes 262176 | tf_op jit(solution)/shard_map/all_to_all | solution.py:222
  40.6 5.3 %all_gather.12.duals_ref = bf16[2,8,128,128]{3,2,1,0:T(8,128)(2,1)S(1)} all-gather(bf16[1,8,128,128]{3,2,1,0:T(8,128)(2,1)S(1)} %bitcast.34), channel_id=1, replica_groups=mesh['tm_0'=4,'tm_1'=2,'tm_2'=2,'cell_0'=8,'cell_1'=4] {'tm_2'}, dimensions={0}, use_global_device_ids=true | all-gather | bytes 786432 | tf_op jit(solution)/shard_map/all_gather | solution.py:241
  45.9 0.0 copy-done.1
  45.9 0.0 copy-done
  45.9 1.9 %shard_map.110 = bf16[4,2,32,4,128]{4,3,2,1,0:T(4,128)(2,1)} custom-call(s32[1]{0:T(128)} %bitcast.here_ref, s32[16,128]{1,0:T(8,128)S(1)} %bitcast.33, bf16[2,8,128,128]{3,2,1,0:T(8,128)(2,1)S(1)} %all_gather.12.duals_ref, bf16[2048,512]{1,0:T(8,128)(2,1)S(1)} %bitcast.29), custom_call_target="tpu_custom_call" | custom-call | tf_op jit(solution)/shard_map/pallas_call | solution.py:212
  47.9 9.1 %all-to-all-start.2 = ((bf16[256,4,128]{2,1,0:T(4,128)(2,1)}), bf16[256,4,128]{2,1,0:T(4,128)(2,1)S(1)}, u32[]{:S(2)}, u32[]{:S(2)}) async-start(bf16[256,4,128]{2,1,0:T(4,128)(2,1)} %bitcast.9), calls=%async_computation.2 | async-start | bytes 524288 | tf_op jit(solution)/shard_map/all_to_all | solution.py:222
  57.0 0.0 copy-start.2
  57.0 0.0 copy-start.3
  57.0 0.0 copy-start.4
  57.0 0.0 copy-start.5
  57.0 0.0 copy-start.6
  57.0 0.0 copy-start.7
  57.0 5.8 %fusion.5 = bf16[2048,512]{1,0:T(8,128)(2,1)} fusion(s32[2048]{0:T(1024)S(1)} %bitcast.44, pred[2048]{0:T(1024)(128)(4,1)S(1)} %broadcast_compare_fusion, bf16[2048,1,512]{2,0,1:T(8,128)(2,1)S(1)} %copy-done), kind=kOutput, calls=%fused_computation.5 | convolution fusion | flops 4304404480 | bytes 4204544 | tf_op jit(solution)/shard_map/dot_general | solution.py:250
  62.8 8.8 %all-to-all-done.2 = bf16[256,4,128]{2,1,0:T(4,128)(2,1)S(1)} async-done(((bf16[256,4,128]{2,1,0:T(4,128)(2,1)}), bf16[256,4,128]{2,1,0:T(4,128)(2,1)S(1)}, u32[]{:S(2)}, u32[]{:S(2)}) %all-to-all-start.2) | async-done | bytes 262176 | tf_op jit(solution)/shard_map/all_to_all | solution.py:222
  71.7 3.8 %all_gather.13.field_ref = bf16[16,128,128]{2,1,0:T(8,128)(2,1)S(1)} all-gather(bf16[8,128,128]{2,1,0:T(8,128)(2,1)S(1)} %bitcast.35), channel_id=1, replica_groups=mesh['tm_0'=4,'tm_1'=2,'tm_2'=2,'cell_0'=8,'cell_1'=4] {'tm_2'}, dimensions={0}, use_global_device_ids=true | all-gather | bytes 786432 | tf_op jit(solution)/shard_map/all_gather | solution.py:252
  75.4 0.0 copy-done.3
  75.4 0.0 copy-done.5
  75.5 9.3 %shard_map.111 = bf16[512,128]{1,0:T(8,128)(2,1)S(1)} custom-call(s32[1]{0:T(128)} %bitcast.11.which_ref, f32[16,16]{1,0:T(8,128)S(1)} %copy-done.2, bf16[16,128,128]{2,1,0:T(8,128)(2,1)S(1)} %all_gather.13.field_ref, s32[128,128]{1,0:T(8,128)S(1)} %bitcast.32, s32[128,128]{1,0:T(8,128)S(1)} %bitcast.31, bf16[256,128]{1,0:T(8,128)(2,1)S(1)} %copy-done.7, ...), custom_call_target="tpu_custom_call" | custom-call | flops 10000000000 | bytes 18874368 | tf_op jit(solution)/shard_map/pallas_call | solution.py:160
  84.8 17.0 %all_to_all.25 = bf16[128,4,128]{2,1,0:T(4,128)(2,1)S(1)} all-to-all(bf16[128,4,128]{2,1,0:T(4,128)(2,1)S(1)} %bitcast.30), channel_id=1, replica_groups=mesh['tm_0'=4,'tm_1'=2,'tm_2'=2,'cell_0'=8,'cell_1'=4] {'tm_0','cell_0',..., dimensions={0} | all-to-all | bytes 262144 | tf_op jit(solution)/shard_map/all_to_all | solution.py:222
  101.8 0.4 convolution_convert_fusion
  102.2 3.4 %all-gather = bf16[2048,128]{1,0:T(8,128)(2,1)S(1)} all-gather(bf16[1024,128]{1,0:T(8,128)(2,1)S(1)} %convolution_convert_fusion), channel_id=2, replica_groups=mesh['tm_0'=4,'tm_1'=2,'tm_2'=2,'cell_0'=8,'cell_1'=4] {'tm_2'}, dimensions={0}, use_global_device_ids=true | all-gather | bytes 786432 | tf_op jit(solution)/shard_map/all_gather | solution.py:260
  105.7 0.4 fusion.8
  106.1 24.4 %all_to_all.26 = bf16[256,4,128]{2,1,0:T(4,128)(2,1)S(1)} all-to-all(bf16[256,4,128]{2,1,0:T(4,128)(2,1)S(1)} %bitcast.38), channel_id=1, replica_groups=mesh['tm_0'=4,'tm_1'=2,'tm_2'=2,'cell_0'=8,'cell_1'=4] {'tm_0','tm_1','c..., dimensions={0} | all-to-all | bytes 524288 | tf_op jit(solution)/shard_map/all_to_all | solution.py:222
  130.5 0.9 convert_reduce_fusion
  (10 shorter events, 0.0 us)
Async XLA Ops:
  0.0 45.9 %copy-start.1 = (s32[2048]{0:T(1024)S(1)}, s32[2048]{0:T(1024)}, u32[]{:S(2)}) copy-start(s32[2048]{0:T(1024)} %param.15) | copy-start | bytes 24580
  0.0 45.9 %copy-start = (bf16[2048,1,512]{2,0,1:T(8,128)(2,1)S(1)}, bf16[2048,1,512]{2,0,1:T(8,128)(2,1)}, u32[]{:S(2)}) copy-start(bf16[2048,1,512]{2,0,1:T(8,128)(2,1)} %param.11) | copy-start | bytes 6291460
  1.5 28.7 %all-to-all-start = ((bf16[64,8,128]{2,1,0:T(8,128)(2,1)}), bf16[64,8,128]{2,1,0:T(8,128)(2,1)S(1)}, u32[]{:S(2)}, u32[]{:S(2)}) async-start(bf16[64,8,128]{2,1,0:T(8,128)(2,1)} %shard_map.109), calls=%async_computation | async-start | bytes 262144 | tf_op jit(solution)/shard_map/all_to_all | solution.py:222
  31.1 9.5 %all-to-all-start.1 = ((bf16[4,256,128]{2,1,0:T(8,128)(2,1)}), bf16[4,256,128]{2,1,0:T(8,128)(2,1)S(1)}, u32[]{:S(2)}, u32[]{:S(2)}) async-start(bf16[4,256,128]{2,1,0:T(8,128)(2,1)} %broadcast_in_dim.2), calls=%async_computation.1 | async-start | bytes 524288 | tf_op jit(solution)/shard_map/all_to_all | solution.py:222
  47.9 23.8 %all-to-all-start.2 = ((bf16[256,4,128]{2,1,0:T(4,128)(2,1)}), bf16[256,4,128]{2,1,0:T(4,128)(2,1)S(1)}, u32[]{:S(2)}, u32[]{:S(2)}) async-start(bf16[256,4,128]{2,1,0:T(4,128)(2,1)} %bitcast.9), calls=%async_computation.2 | async-start | bytes 524288 | tf_op jit(solution)/shard_map/all_to_all | solution.py:222
  57.0 18.5 %copy-start.2 = (f32[16,16]{1,0:T(8,128)S(1)}, f32[16,16]{1,0:T(8,128)}, u32[]{:S(2)}) copy-start(f32[16,16]{1,0:T(8,128)} %weight_ref.1) | copy-start | bytes 3076
  57.0 18.4 %copy-start.3 = (f32[256,256]{1,0:T(8,128)S(1)}, f32[256,256]{1,0:T(8,128)}, u32[]{:S(2)}) copy-start(f32[256,256]{1,0:T(8,128)} %constant.51.clone.eigen_ref) | copy-start | bytes 786436
  57.0 18.4 %copy-start.4 = (bf16[128,256]{1,0:T(8,128)(2,1)S(1)}, bf16[128,256]{1,0:T(8,128)(2,1)}, u32[]{:S(2)}) copy-start(bf16[128,256]{1,0:T(8,128)(2,1)} %constant.50.clone.side_l) | copy-start | bytes 196612
  57.0 18.4 %copy-start.5 = (bf16[128,256]{1,0:T(8,128)(2,1)S(1)}, bf16[128,256]{1,0:T(8,128)(2,1)}, u32[]{:S(2)}) copy-start(bf16[128,256]{1,0:T(8,128)(2,1)} %constant.49.clone.side_h) | copy-start | bytes 196612
  57.0 18.4 %copy-start.6 = (bf16[256,128]{1,0:T(8,128)(2,1)S(1)}, bf16[256,128]{1,0:T(8,128)(2,1)}, u32[]{:S(2)}) copy-start(bf16[256,128]{1,0:T(8,128)(2,1)} %constant.48.clone.basis_l) | copy-start | bytes 196612
  57.0 18.4 %copy-start.7 = (bf16[256,128]{1,0:T(8,128)(2,1)S(1)}, bf16[256,128]{1,0:T(8,128)(2,1)}, u32[]{:S(2)}) copy-start(bf16[256,128]{1,0:T(8,128)(2,1)} %constant.47.clone.basis_h) | copy-start | bytes 196612
  75.5 26.3 %copy-start.8 = (bf16[2048,512]{1,0:T(8,128)(2,1)S(1)}, bf16[2048,512]{1,0:T(8,128)(2,1)}, u32[]{:S(2)}) copy-start(bf16[2048,512]{1,0:T(8,128)(2,1)} %fusion.5) | copy-start | bytes 6291460

commit v6 on v5

--- a/solution.py
+++ b/solution.py
@@ -41,7 +41,15 @@
     basis = basis * np.where(edge, np.sqrt(1.0 / size), np.sqrt(2.0 / size))[:, None]
     fold = np.cos(angle) * np.where(np.arange(GRID) == 0, 1.0, 2.0)[None, :]
     eigen = fold @ table @ fold.T
-    return (*halves(basis), *halves(basis.T), eigen.astype(np.float32))
+    high, low = halves(basis)
+    return (
+        np.concatenate([high.T, low.T], axis=0),
+        np.concatenate([high, high], axis=1),
+        low,
+        np.concatenate([high.T, low.T], axis=0),
+        np.concatenate([high, low], axis=1),
+        eigen.astype(np.float32),
+    )
 
 
 def matmul(a, b):
@@ -51,10 +59,6 @@
 def parted(a):
     high = a.astype(BF16)
     return high, (a - high.astype(F32)).astype(BF16)
-
-
-def matmul_parted(a, b):
-    return matmul(a[0], b[0]) + (matmul(a[0], b[1]) + matmul(a[1], b[0]))
 
 
 def hits(at, line):
@@ -65,7 +69,7 @@
 
 
 def spatial_kernel(lot, kept, which_ref, weight_ref, field_ref, rows_ref, cols_ref,
-                   basis_h, basis_l, side_h, side_l, eigen_ref, out_ref, mixed, grid):
+                   side_tall, basis_twice, basis_low, side_both, basis_wide, eigen_ref, out_ref, mixed, grid):
     times, chunks, _ = field_ref.shape
     pair = 2
     which = which_ref[0]
@@ -112,8 +116,6 @@
         return carry
 
     lax.fori_loop(0, chunks // lot, put, 0)
-    basis = (basis_h[...], basis_l[...])
-    side = (side_h[...], side_l[...])
     whole = jnp.concatenate(
         [
             grid[s * LOW : (s + 1) * LOW, p * GRID : (p + 1) * GRID]
@@ -121,15 +123,22 @@
             for p in range(PARTS)
         ],
         axis=0,
-    )
-    exact = whole.astype(BF16)
-    ahead = matmul(exact, side[0]) + matmul(exact, side[1])
+    ).astype(BF16)
+    ahead = matmul(jnp.concatenate([whole, whole], axis=1), side_tall[...])
+    backs = []
     for s in range(kept):
-        waves = matmul_parted(basis, parted(ahead[s * GRID : (s + 1) * GRID])) * eigen_ref[...]
-        back = matmul_parted(side, parted(waves))
-        smooth = matmul_parted(parted(back), basis)
+        high, rest = parted(ahead[s * GRID : (s + 1) * GRID])
+        waves = matmul(basis_twice[...], jnp.concatenate([high, rest], axis=0)) + matmul(basis_low[...], high)
+        high, rest = parted(waves * eigen_ref[...])
+        both = matmul(side_both[...], high)
+        backs.append(both[:GRID] + (both[GRID:] + matmul(side_both[:GRID, :], rest)))
+    high, rest = parted(jnp.concatenate(backs, axis=0))
+    both = matmul(high, basis_wide[...])
+    smooth = both[:, :GRID] + (both[:, GRID:] + matmul(rest, basis_wide[:, :GRID]))
+    for s in range(kept):
         for p in range(PARTS):
-            grid[s * LOW : (s + 1) * LOW, p * GRID : (p + 1) * GRID] = smooth[p * LOW : (p + 1) * LOW]
+            top = s * GRID + p * LOW
+            grid[s * LOW : (s + 1) * LOW, p * GRID : (p + 1) * GRID] = smooth[top : top + LOW]
     weighted = grid[...].astype(BF16)
 
     line_at = lax.broadcasted_iota(jnp.int32, (LOW, GRID), 0)
@@ -189,6 +198,37 @@
     )(half, duals, coords)
 
 
+def picking_kernel(here_ref, core_ref, owner_ref, time_ref, flat_ref, out_ref):
+    count = owner_ref.shape[0]
+    pair = 2
+    lane = lax.broadcasted_iota(jnp.int32, (1, GRID), 1)
+    ids = [jnp.where(time_ref[k : k + 1, :] >= here_ref[0], lane + k * GRID, -1) for k in range(count)]
+    ids = jnp.concatenate(ids, axis=1).astype(F32)
+    owners = owner_ref[...].astype(F32)
+    first = core_ref[0] == 0
+    order = []
+    for side in range(pair):
+        for k in range(0, count, pair):
+            other, same = owners[k + 1 - side : k + 2 - side], owners[k + side : k + side + 1]
+            order.append(jnp.where(first, other, same))
+    slots = jnp.concatenate(order, axis=0).T
+    flat = flat_ref[...]
+    for k in range(count):
+        chosen = jnp.where(slots[:, k : k + 1] == ids, 1.0, 0.0).astype(BF16)
+        out_ref[k * GRID : (k + 1) * GRID, :] = matmul(chosen, flat).astype(BF16)
+
+
+def picking(here, core, obs_owner, obs_time, flat):
+    return pl.pallas_call(
+        picking_kernel,
+        out_shape=jax.ShapeDtypeStruct(flat.shape, BF16),
+        in_specs=[SMEM] * 2 + [VMEM] * 3,
+        out_specs=VMEM,
+        compiler_params=pltpu.CompilerParams(vmem_limit_bytes=24 << 20),
+        cost_estimate=pl.CostEstimate(flops=2 * flat.size * flat.shape[0], bytes_accessed=4 * flat.size, transcendentals=0),
+    )(here, core, obs_owner.reshape(-1, GRID), obs_time.reshape(-1, GRID), flat)
+
+
 def adjoint_kernel(here_ref, time_ref, duals_ref, flat_ref, out_ref):
     pair, groups, rows, reals = duals_ref.shape
     outer, again, part, folds, _ = out_ref.shape
@@ -230,24 +270,23 @@
     obs = sensitivity.shape[0]
     own, reals = duals.shape
     flat = sensitivity.reshape(obs, -1)
-    here = lax.axis_index((X, ZH, CO))
+    here = lax.axis_index((X, ZH, CO)).reshape(1)
+    core = lax.axis_index(CO).reshape(1)
     nx, nh, pair = (lax.axis_size(a) for a in (X, ZH, CO))
     which = lax.axis_index((ZH, CO)).reshape(1)
 
     plane = (ZH, Y, ZL)
-    first = exchange(opening(lax.axis_index(ZH).reshape(1), duals, cell_coords, lax.axis_size(plane)), plane)
+    first = opening(lax.axis_index(ZH).reshape(1), duals, cell_coords, lax.axis_size(plane))
+    even = core[0] == 0
+    first, here, core, which, even = lax.optimization_barrier((first, here, core, which, even))
+    first = exchange(first, plane)
     coords = first[:, own:].reshape(nh, -1, GRID).astype(jnp.int32)
     second = copies(first[:, :own].reshape(-1, reals), X)
     third = lax.all_gather(second.reshape(nx * nh, -1, reals), CO, axis=0)
-    pieces = adjoint(here.reshape(1), obs_time, third, flat, nx, nh)
-    core = lax.axis_index(CO)
-    slots = obs_owner.reshape(nx * nh, pair, -1)
-    slots = jnp.concatenate([lax.dynamic_index_in_dim(slots, i, 1, keepdims=False) for i in (1 - core, core)])
-    live = here <= obs_time
-    pieces, slots, live = lax.optimization_barrier((pieces, slots, live))
+    pieces = adjoint(here, obs_time, third, flat, nx, nh)
+    pieces, owner = lax.optimization_barrier((pieces, obs_owner))
     field = exchange(pieces.reshape(-1, *pieces.shape[3:]), (X, ZH, Y, ZL))
-    chosen = (slots.reshape(-1)[:, None] == jnp.arange(obs, dtype=jnp.int32)[None, :]) & live[None, :]
-    picked = jnp.dot(chosen.astype(BF16), flat, preferred_element_type=F32).astype(BF16)
+    picked = picking(here, core, owner, obs_time, flat)
     field, picked = lax.optimization_barrier((field, picked))
     field = lax.all_gather(field.reshape(nx * nh, -1, GRID), CO, axis=0, tiled=True)
 
@@ -258,7 +297,7 @@
         for rows in jnp.split(picked, pair)
     )
     swapped = lax.all_gather(theirs.astype(BF16), CO, axis=0)
-    got = lax.dynamic_index_in_dim(swapped, 1 - core, 0, keepdims=False)
+    got = jnp.where(even, swapped[1], swapped[0])
     product = (ours + got.astype(F32)).astype(BF16)
     product = exchange(product.reshape(-1, own, reals), (X, ZH, Y, ZL))
     return jnp.sum(product.astype(F32), axis=0)

time: 132 us -> 130 us (0.985)
  blocking collectives: 53.9 us -> 92.1 us
  starting transfers between devices: 30.2 us -> 9.17 us
  waiting for transfers between devices: 24.4 us -> 8.61 us
  matrix products: 6.63 us -> 0.89 us
  Pallas kernels: 12.7 us -> 16.3 us
    all_to_all x2 -> x4, blocking collectives: 41.4 us -> 79.6 us  [exchange(): return lax.all_to_all(pieces, axes, split_axis=0, concat_axis=0, tiled=True)]
    all_to_all x3 -> x1, starting transfers between devices: 30.2 us -> 9.17 us  [exchange(): return lax.all_to_all(pieces, axes, split_axis=0, concat_axis=0, tiled=True)]
    all_to_all x3 -> x1, waiting for transfers between devices: 24.4 us -> 8.61 us  [exchange(): return lax.all_to_all(pieces, axes, split_axis=0, concat_axis=0, tiled=True)]
    dot_general x1 -> x0, matrix products: 5.77 us -> none  [per_device(): jnp.dot(chosen.astype(BF16), flat, preferred_element_type=F32).astype(BF16)]
    pallas_call x0 -> x1, Pallas kernels: none -> 4.64 us  [picking(): pl.pallas_call(picking_kernel, out_shape=jax.ShapeDtypeStruct(flat.shape,...]
    unnamed x18 -> x22, local copies, waits for them, and re-layouts: 0.05 us -> 1.38 us
  transfers between devices with their start and end apart: 3 -> 1, of which waited for: 3 -> 1; matrix products, arithmetic and copies ran while one was open for 6% -> 0% of each run, Pallas kernels for 0% -> 4%
where the time goes in v6:
time: 130 us
  blocking collectives  92.1 us (71%)
  Pallas kernels  16.3 us (13%)
  starting transfers between devices  9.17 us (7%)
  waiting for transfers between devices  8.61 us (7%)
  local copies, waits for them, and re-layouts  1.43 us (1%)
    all_to_all x4, blocking collectives, exchange(): return lax.all_to_all(pieces, axes, split_axis=0, concat_axis=0, tiled=True)  79.6 us
    all_to_all x1, starting transfers between devices, exchange(): return lax.all_to_all(pieces, axes, split_axis=0, concat_axis=0, tiled=True)  9.17 us
    all_to_all x1, waiting for transfers between devices, exchange(): return lax.all_to_all(pieces, axes, split_axis=0, concat_axis=0, tiled=True)  8.61 us
    pallas_call x1, Pallas kernels, spatial(): pl.pallas_call(functools.partial(spatial_kernel, 64, kept), out_shape=jax...  8.18 us
    all_gather x1, blocking collectives, per_device(): third = lax.all_gather(second.reshape(nx * nh, -1, reals), CO, axis=0)  5.43 us
    pallas_call x1, Pallas kernels, picking(): pl.pallas_call(picking_kernel, out_shape=jax.ShapeDtypeStruct(flat.shape,...  4.64 us
    all_gather x1, blocking collectives, per_device(): lax.all_gather(field.reshape(nx * nh, -1, GRID), CO, axis=0, tiled=True)  3.68 us
    all_gather x1, blocking collectives, per_device(): swapped = lax.all_gather(theirs.astype(BF16), CO, axis=0)  3.44 us
  transfers between devices with their start and end apart: 1, of which 1 were waited for; matrix products, arithmetic and copies ran while one was open for 0% of the time, Pallas kernels for 4%

profile of v6, /device:TPU:1, one launch (start us, length us, event | category | flops | bytes accessed | tf_op | source)
XLA Modules:
  0.0 129.5 jit_solution(9167102289412618921)
XLA Ops:
  0.0 1.5 %shard_map.118 = bf16[64,8,128]{2,1,0:T(8,128)(2,1)} custom-call(s32[1]{0:T(128)} %bitcast.half_ref, bf16[4,128]{1,0:T(4,128)(2,1)} %duals_ref.1, s32[2,512]{1,0:T(2,128)} %coords_ref.1), custom_call_target="tpu_custom_call" | custom-call | tf_op jit(solution)/shard_map/pallas_call | solution.py:193
  1.5 28.7 %all_to_all.25 = bf16[64,8,128]{2,1,0:T(8,128)(2,1)S(1)} all-to-all(bf16[64,8,128]{2,1,0:T(8,128)(2,1)} %shard_map.118), channel_id=1, replica_groups=mesh['tm_0'=4,'tm_1'=2,'tm_2'=2,'cell_0'=8,'cell_1'=4] {'tm_1','cell_0',..., dimensions={0} | all-to-all | bytes 262144 | tf_op jit(solution)/shard_map/all_to_all | solution.py:262
  30.3 0.1 slice_convert_fusion
  30.4 9.3 %all_to_all.26 = bf16[4,256,128]{2,1,0:T(8,128)(2,1)S(1)} all-to-all(bf16[4,256,128]{2,1,0:T(8,128)(2,1)S(1)} %broadcast_in_dim.3), channel_id=1, replica_groups=mesh['tm_0'=4,'tm_1'=2,'tm_2'=2,'cell_0'=8,'cell_1'=4] {'tm_0'}, dimensions={0} | all-to-all | bytes 524288 | tf_op jit(solution)/shard_map/all_to_all | solution.py:262
  39.7 5.4 %all_gather.12.duals_ref = bf16[2,8,128,128]{3,2,1,0:T(8,128)(2,1)S(1)} all-gather(bf16[1,8,128,128]{3,2,1,0:T(8,128)(2,1)S(1)} %bitcast.30), channel_id=1, replica_groups=mesh['tm_0'=4,'tm_1'=2,'tm_2'=2,'cell_0'=8,'cell_1'=4] {'tm_2'}, dimensions={0}, use_global_device_ids=true | all-gather | bytes 786432 | tf_op jit(solution)/shard_map/all_gather | solution.py:285
  45.2 0.0 copy-done.1
  45.2 0.0 copy-done
  45.2 1.9 %shard_map.119 = bf16[4,2,32,4,128]{4,3,2,1,0:T(4,128)(2,1)} custom-call(s32[1]{0:T(128)} %bitcast.1.here_ref, s32[16,128]{1,0:T(8,128)S(1)} %bitcast.26, bf16[2,8,128,128]{3,2,1,0:T(8,128)(2,1)S(1)} %all_gather.12.duals_ref, bf16[2048,512]{1,0:T(8,128)(2,1)S(1)} %bitcast.21), custom_call_target="tpu_custom_call" | custom-call | tf_op jit(solution)/shard_map/pallas_call | solution.py:252
  47.1 9.2 %all-to-all-start.2 = ((bf16[256,4,128]{2,1,0:T(4,128)(2,1)}), bf16[256,4,128]{2,1,0:T(4,128)(2,1)S(1)}, u32[]{:S(2)}, u32[]{:S(2)}) async-start(bf16[256,4,128]{2,1,0:T(4,128)(2,1)} %bitcast.8), calls=%async_computation.2 | async-start | bytes 524288 | tf_op jit(solution)/shard_map/all_to_all | solution.py:262
  56.3 0.0 copy-start.3
  56.3 0.0 copy-start.4
  56.3 0.0 copy-start.5
  56.3 0.0 copy-start.6
  56.3 0.0 copy-start.7
  56.4 0.0 copy-start.8
  56.4 4.6 %shard_map.120 = bf16[2048,512]{1,0:T(8,128)(2,1)S(1)} custom-call(s32[1]{0:T(128)} %bitcast.1.here_ref, s32[1]{0:T(128)} %bitcast.2.core_ref, s32[16,128]{1,0:T(8,128)S(1)} %bitcast.28, s32[16,128]{1,0:T(8,128)S(1)} %bitcast.27, bf16[2048,512]{1,0:T(8,128)(2,1)S(1)} %bitcast.22), custom_call_target="tpu_custom_call" | custom-call | flops 4294967296 | bytes 4194304 | tf_op jit(solution)/shard_map/pallas_call | solution.py:222
  61.0 0.0 copy-start.9
  61.0 1.3 %copy-done.9 = bf16[2048,512]{1,0:T(8,128)(2,1)} copy-done((bf16[2048,512]{1,0:T(8,128)(2,1)}, bf16[2048,512]{1,0:T(8,128)(2,1)S(1)}, u32[]{:S(2)}) %copy-start.9) | copy-done | bytes 2097176
  62.3 8.6 %all-to-all-done.2 = bf16[256,4,128]{2,1,0:T(4,128)(2,1)S(1)} async-done(((bf16[256,4,128]{2,1,0:T(4,128)(2,1)}), bf16[256,4,128]{2,1,0:T(4,128)(2,1)S(1)}, u32[]{:S(2)}, u32[]{:S(2)}) %all-to-all-start.2) | async-done | bytes 262176 | tf_op jit(solution)/shard_map/all_to_all | solution.py:262
  71.0 3.7 %all_gather.13.field_ref = bf16[16,128,128]{2,1,0:T(8,128)(2,1)S(1)} all-gather(bf16[8,128,128]{2,1,0:T(8,128)(2,1)S(1)} %bitcast.29), channel_id=1, replica_groups=mesh['tm_0'=4,'tm_1'=2,'tm_2'=2,'cell_0'=8,'cell_1'=4] {'tm_2'}, dimensions={0}, use_global_device_ids=true | all-gather | bytes 786432 | tf_op jit(solution)/shard_map/all_gather | solution.py:291
  74.6 0.0 copy-done.6
  74.6 0.0 copy-done.7
  74.7 0.0 copy-done.8
  74.7 0.0 copy-start.10
  74.7 8.2 %shard_map.121 = bf16[512,128]{1,0:T(8,128)(2,1)S(1)} custom-call(s32[1]{0:T(128)} %bitcast.3.which_ref, f32[16,16]{1,0:T(8,128)S(1)} %copy-done.3, bf16[16,128,128]{2,1,0:T(8,128)(2,1)S(1)} %all_gather.13.field_ref, s32[128,128]{1,0:T(8,128)S(1)} %bitcast.25, s32[128,128]{1,0:T(8,128)S(1)} %bitcast.24, bf16[256,256]{1,0:T(8,128)(2,1)S(1)} %copy-done.7, ...), custom_call_target="tpu_custom_call" | custom-call | flops 10000000000 | bytes 18874368 | tf_op jit(solution)/shard_map/pallas_call | solution.py:169
  82.9 17.1 %all_to_all.27 = bf16[128,4,128]{2,1,0:T(4,128)(2,1)S(1)} all-to-all(bf16[128,4,128]{2,1,0:T(4,128)(2,1)S(1)} %bitcast.23), channel_id=1, replica_groups=mesh['tm_0'=4,'tm_1'=2,'tm_2'=2,'cell_0'=8,'cell_1'=4] {'tm_0','cell_0',..., dimensions={0} | all-to-all | bytes 262144 | tf_op jit(solution)/shard_map/all_to_all | solution.py:262
  100.0 0.0 copy-done.10
  100.0 0.4 convolution_convert_fusion
  100.4 3.4 %all-gather = bf16[2048,128]{1,0:T(8,128)(2,1)S(1)} all-gather(bf16[1024,128]{1,0:T(8,128)(2,1)S(1)} %convolution_convert_fusion), channel_id=2, replica_groups=mesh['tm_0'=4,'tm_1'=2,'tm_2'=2,'cell_0'=8,'cell_1'=4] {'tm_2'}, dimensions={0}, use_global_device_ids=true | all-gather | bytes 786432 | tf_op jit(solution)/shard_map/all_gather | solution.py:299
  103.9 0.5 fusion
  104.3 24.4 %all_to_all.28 = bf16[256,4,128]{2,1,0:T(4,128)(2,1)S(1)} all-to-all(bf16[256,4,128]{2,1,0:T(4,128)(2,1)S(1)} %bitcast.32), channel_id=1, replica_groups=mesh['tm_0'=4,'tm_1'=2,'tm_2'=2,'cell_0'=8,'cell_1'=4] {'tm_0','tm_1','c..., dimensions={0} | all-to-all | bytes 524288 | tf_op jit(solution)/shard_map/all_to_all | solution.py:262
  128.7 0.9 convert_reduce_fusion
  (9 shorter events, 0.1 us)
Async XLA Ops:
  0.0 45.2 %copy-start.1 = (s32[2048]{0:T(1024)S(1)}, s32[2048]{0:T(1024)}, u32[]{:S(2)}) copy-start(s32[2048]{0:T(1024)} %param.16) | copy-start | bytes 24580
  0.0 45.2 %copy-start = (bf16[2048,1,512]{2,0,1:T(8,128)(2,1)S(1)}, bf16[2048,1,512]{2,0,1:T(8,128)(2,1)}, u32[]{:S(2)}) copy-start(bf16[2048,1,512]{2,0,1:T(8,128)(2,1)} %param.12) | copy-start | bytes 6291460
  39.7 16.6 %copy-start.2 = (s32[2048]{0:T(1024)S(1)}, s32[2048]{0:T(1024)}, u32[]{:S(2)}) copy-start(s32[2048]{0:T(1024)} %param.17) | copy-start | bytes 24580
  47.1 23.9 %all-to-all-start.2 = ((bf16[256,4,128]{2,1,0:T(4,128)(2,1)}), bf16[256,4,128]{2,1,0:T(4,128)(2,1)S(1)}, u32[]{:S(2)}, u32[]{:S(2)}) async-start(bf16[256,4,128]{2,1,0:T(4,128)(2,1)} %bitcast.8), calls=%async_computation.2 | async-start | bytes 524288 | tf_op jit(solution)/shard_map/all_to_all | solution.py:262
  56.3 18.3 %copy-start.3 = (f32[16,16]{1,0:T(8,128)S(1)}, f32[16,16]{1,0:T(8,128)}, u32[]{:S(2)}) copy-start(f32[16,16]{1,0:T(8,128)} %weight_ref.1) | copy-start | bytes 3076
  56.3 18.3 %copy-start.4 = (f32[256,256]{1,0:T(8,128)S(1)}, f32[256,256]{1,0:T(8,128)}, u32[]{:S(2)}) copy-start(f32[256,256]{1,0:T(8,128)} %constant.38.clone.eigen_ref) | copy-start | bytes 786436
  56.3 18.3 %copy-start.5 = (bf16[256,256]{1,0:T(8,128)(2,1)S(1)}, bf16[256,256]{1,0:T(8,128)(2,1)}, u32[]{:S(2)}) copy-start(bf16[256,256]{1,0:T(8,128)(2,1)} %constant.37.clone.basis_wide) | copy-start | bytes 393220
  56.3 18.3 %copy-start.6 = (bf16[256,256]{1,0:T(8,128)(2,1)S(1)}, bf16[256,256]{1,0:T(8,128)(2,1)}, u32[]{:S(2)}) copy-start(bf16[256,256]{1,0:T(8,128)(2,1)} %constant.35.clone.basis_twice) | copy-start | bytes 393220
  56.3 18.3 %copy-start.7 = (bf16[256,256]{1,0:T(8,128)(2,1)S(1)}, bf16[256,256]{1,0:T(8,128)(2,1)}, u32[]{:S(2)}) copy-start(bf16[256,256]{1,0:T(8,128)(2,1)} %constant.34.clone.side_tall.side_both) | copy-start | bytes 393220
  56.4 18.3 %copy-start.8 = (bf16[256,128]{1,0:T(8,128)(2,1)S(1)}, bf16[256,128]{1,0:T(8,128)(2,1)}, u32[]{:S(2)}) copy-start(bf16[256,128]{1,0:T(8,128)(2,1)} %constant.36.clone.basis_low) | copy-start | bytes 196612
  61.0 1.3 %copy-start.9 = (bf16[2048,512]{1,0:T(8,128)(2,1)}, bf16[2048,512]{1,0:T(8,128)(2,1)S(1)}, u32[]{:S(2)}) copy-start(bf16[2048,512]{1,0:T(8,128)(2,1)S(1)} %shard_map.120) | copy-start | bytes 6291460
  74.7 25.3 %copy-start.10 = (bf16[2048,512]{1,0:T(8,128)(2,1)S(1)}, bf16[2048,512]{1,0:T(8,128)(2,1)}, u32[]{:S(2)}) copy-start(bf16[2048,512]{1,0:T(8,128)(2,1)} %copy-done.9) | copy-start | bytes 6291460

commit v7 on v6

--- a/solution.py
+++ b/solution.py
@@ -76,7 +76,7 @@
     strides = times // kept
 
     def mix(j, carry):
-        rows = pl.ds(pl.multiple_of(j * 16, 16), 16)
+        rows = pl.ds(pl.multiple_of(j * 32, 32), 32)
         totals = [None] * kept
         for k in range(times):
             t = (k % (times // pair)) * pair + k // (times // pair)
@@ -88,7 +88,7 @@
             mixed[s, rows, :] = totals[s].astype(BF16).astype(F32)
         return carry
 
-    lax.fori_loop(0, chunks // 16, mix, 0)
+    lax.fori_loop(0, chunks // 32, mix, 0)
     grid[...] = jnp.zeros_like(grid)
     first_at = lax.broadcasted_iota(jnp.int32, (16, GRID), 0).astype(F32)
     wide_at = [(first_at + float(k)).astype(BF16) for k in range(0, PARTS * GRID, 16)]
@@ -232,16 +232,15 @@
 def adjoint_kernel(here_ref, time_ref, duals_ref, flat_ref, out_ref):
     pair, groups, rows, reals = duals_ref.shape
     outer, again, part, folds, _ = out_ref.shape
-    times = time_ref[...].astype(F32).T
-    here = here_ref[0].astype(F32)
+    keep = jnp.where(time_ref[...] >= here_ref[0], 1.0, 0.0).T
     seen = []
     for k in range(pair * groups):
-        block = duals_ref[k % pair, k // pair].astype(F32)
-        seen.append(jnp.where(times[:, k : k + 1] >= here, block, 0.0).astype(BF16))
+        column = jnp.broadcast_to(keep[:, k : k + 1], (rows, reals)).astype(BF16)
+        seen.append(duals_ref[k % pair, k // pair] * column)
     total = lax.dot_general(
         jnp.concatenate(seen, axis=0), flat_ref[...], (((0,), (0,)), ((), ())), preferred_element_type=F32
     )
-    pieces = jnp.stack([total[:, k * GRID : (k + 1) * GRID] for k in range(folds)], axis=1).astype(BF16)
+    pieces = total.reshape(reals, folds, GRID).astype(BF16)
     for i in range(outer):
         for j in range(again):
             out_ref[i, j] = pieces[i * part : (i + 1) * part]

time: 130 us -> 130 us (level)
  no operation moved by 1% of the time
where the time goes in v7:
time: 130 us; the launch traced here: 129 us
  blocking collectives  92.1 us (71%)
  Pallas kernels  15.9 us (12%)
  starting transfers between devices  9.17 us (7%)
  waiting for transfers between devices  8.6 us (7%)
  local copies, waits for them, and re-layouts  1.43 us (1%)
    all_to_all x4, blocking collectives, exchange(): return lax.all_to_all(pieces, axes, split_axis=0, concat_axis=0, tiled=True)  79.6 us
    all_to_all x1, starting transfers between devices, exchange(): return lax.all_to_all(pieces, axes, split_axis=0, concat_axis=0, tiled=True)  9.17 us
    all_to_all x1, waiting for transfers between devices, exchange(): return lax.all_to_all(pieces, axes, split_axis=0, concat_axis=0, tiled=True)  8.6 us
    pallas_call x1, Pallas kernels, spatial(): pl.pallas_call(functools.partial(spatial_kernel, 64, kept), out_shape=jax...  8.11 us
    all_gather x1, blocking collectives, per_device(): third = lax.all_gather(second.reshape(nx * nh, -1, reals), CO, axis=0)  5.43 us
    pallas_call x1, Pallas kernels, picking(): pl.pallas_call(picking_kernel, out_shape=jax.ShapeDtypeStruct(flat.shape,...  4.65 us
    all_gather x1, blocking collectives, per_device(): lax.all_gather(field.reshape(nx * nh, -1, GRID), CO, axis=0, tiled=True)  3.68 us
    all_gather x1, blocking collectives, per_device(): swapped = lax.all_gather(theirs.astype(BF16), CO, axis=0)  3.42 us
  transfers between devices with their start and end apart: 1, of which 1 were waited for; matrix products, arithmetic and copies ran while one was open for 0% of the time, Pallas kernels for 4%

profile of v7, /device:TPU:1, one launch (start us, length us, event | category | flops | bytes accessed | tf_op | source)
XLA Modules:
  0.0 129.1 jit_solution(471608587475452318)
XLA Ops:
  0.0 1.5 %shard_map.118 = bf16[64,8,128]{2,1,0:T(8,128)(2,1)} custom-call(s32[1]{0:T(128)} %bitcast.half_ref, bf16[4,128]{1,0:T(4,128)(2,1)} %duals_ref.1, s32[2,512]{1,0:T(2,128)} %coords_ref.1), custom_call_target="tpu_custom_call" | custom-call | tf_op jit(solution)/shard_map/pallas_call | solution.py:193
  1.5 28.7 %all_to_all.25 = bf16[64,8,128]{2,1,0:T(8,128)(2,1)S(1)} all-to-all(bf16[64,8,128]{2,1,0:T(8,128)(2,1)} %shard_map.118), channel_id=1, replica_groups=mesh['tm_0'=4,'tm_1'=2,'tm_2'=2,'cell_0'=8,'cell_1'=4] {'tm_1','cell_0',..., dimensions={0} | all-to-all | bytes 262144 | tf_op jit(solution)/shard_map/all_to_all | solution.py:261
  30.3 0.1 slice_convert_fusion
  30.4 9.3 %all_to_all.26 = bf16[4,256,128]{2,1,0:T(8,128)(2,1)S(1)} all-to-all(bf16[4,256,128]{2,1,0:T(8,128)(2,1)S(1)} %broadcast_in_dim.3), channel_id=1, replica_groups=mesh['tm_0'=4,'tm_1'=2,'tm_2'=2,'cell_0'=8,'cell_1'=4] {'tm_0'}, dimensions={0} | all-to-all | bytes 524288 | tf_op jit(solution)/shard_map/all_to_all | solution.py:261
  39.7 5.4 %all_gather.12.duals_ref = bf16[2,8,128,128]{3,2,1,0:T(8,128)(2,1)S(1)} all-gather(bf16[1,8,128,128]{3,2,1,0:T(8,128)(2,1)S(1)} %bitcast.30), channel_id=1, replica_groups=mesh['tm_0'=4,'tm_1'=2,'tm_2'=2,'cell_0'=8,'cell_1'=4] {'tm_2'}, dimensions={0}, use_global_device_ids=true | all-gather | bytes 786432 | tf_op jit(solution)/shard_map/all_gather | solution.py:284
  45.2 0.0 copy-done.1
  45.2 0.0 copy-done
  45.2 1.6 %shard_map.119 = bf16[4,2,32,4,128]{4,3,2,1,0:T(4,128)(2,1)} custom-call(s32[1]{0:T(128)} %bitcast.1.here_ref, s32[16,128]{1,0:T(8,128)S(1)} %bitcast.26, bf16[2,8,128,128]{3,2,1,0:T(8,128)(2,1)S(1)} %all_gather.12.duals_ref, bf16[2048,512]{1,0:T(8,128)(2,1)S(1)} %bitcast.21), custom_call_target="tpu_custom_call" | custom-call | tf_op jit(solution)/shard_map/pallas_call | solution.py:251
  46.8 9.2 %all-to-all-start.2 = ((bf16[256,4,128]{2,1,0:T(4,128)(2,1)}), bf16[256,4,128]{2,1,0:T(4,128)(2,1)S(1)}, u32[]{:S(2)}, u32[]{:S(2)}) async-start(bf16[256,4,128]{2,1,0:T(4,128)(2,1)} %bitcast.8), calls=%async_computation.2 | async-start | bytes 524288 | tf_op jit(solution)/shard_map/all_to_all | solution.py:261
  55.9 0.0 copy-done.2
  56.0 0.0 copy-start.3
  56.0 0.0 copy-start.4
  56.0 0.0 copy-start.5
  56.0 0.0 copy-start.6
  56.0 0.0 copy-start.7
  56.0 0.0 copy-start.8
  56.0 4.6 %shard_map.120 = bf16[2048,512]{1,0:T(8,128)(2,1)S(1)} custom-call(s32[1]{0:T(128)} %bitcast.1.here_ref, s32[1]{0:T(128)} %bitcast.2.core_ref, s32[16,128]{1,0:T(8,128)S(1)} %bitcast.28, s32[16,128]{1,0:T(8,128)S(1)} %bitcast.27, bf16[2048,512]{1,0:T(8,128)(2,1)S(1)} %bitcast.22), custom_call_target="tpu_custom_call" | custom-call | flops 4294967296 | bytes 4194304 | tf_op jit(solution)/shard_map/pallas_call | solution.py:222
  60.7 0.0 copy-start.9
  60.7 1.3 %copy-done.9 = bf16[2048,512]{1,0:T(8,128)(2,1)} copy-done((bf16[2048,512]{1,0:T(8,128)(2,1)}, bf16[2048,512]{1,0:T(8,128)(2,1)S(1)}, u32[]{:S(2)}) %copy-start.9) | copy-done | bytes 2097176
  62.0 8.6 %all-to-all-done.2 = bf16[256,4,128]{2,1,0:T(4,128)(2,1)S(1)} async-done(((bf16[256,4,128]{2,1,0:T(4,128)(2,1)}), bf16[256,4,128]{2,1,0:T(4,128)(2,1)S(1)}, u32[]{:S(2)}, u32[]{:S(2)}) %all-to-all-start.2) | async-done | bytes 262176 | tf_op jit(solution)/shard_map/all_to_all | solution.py:261
  70.6 3.7 %all_gather.13.field_ref = bf16[16,128,128]{2,1,0:T(8,128)(2,1)S(1)} all-gather(bf16[8,128,128]{2,1,0:T(8,128)(2,1)S(1)} %bitcast.29), channel_id=1, replica_groups=mesh['tm_0'=4,'tm_1'=2,'tm_2'=2,'cell_0'=8,'cell_1'=4] {'tm_2'}, dimensions={0}, use_global_device_ids=true | all-gather | bytes 786432 | tf_op jit(solution)/shard_map/all_gather | solution.py:290
  74.3 0.0 copy-done.3
  74.3 0.0 copy-done.4
  74.3 0.0 copy-done.5
  74.3 8.1 %shard_map.121 = bf16[512,128]{1,0:T(8,128)(2,1)S(1)} custom-call(s32[1]{0:T(128)} %bitcast.3.which_ref, f32[16,16]{1,0:T(8,128)S(1)} %copy-done.3, bf16[16,128,128]{2,1,0:T(8,128)(2,1)S(1)} %all_gather.13.field_ref, s32[128,128]{1,0:T(8,128)S(1)} %bitcast.25, s32[128,128]{1,0:T(8,128)S(1)} %bitcast.24, bf16[256,256]{1,0:T(8,128)(2,1)S(1)} %copy-done.7, ...), custom_call_target="tpu_custom_call" | custom-call | flops 10000000000 | bytes 18874368 | tf_op jit(solution)/shard_map/pallas_call | solution.py:169
  82.5 17.1 %all_to_all.27 = bf16[128,4,128]{2,1,0:T(4,128)(2,1)S(1)} all-to-all(bf16[128,4,128]{2,1,0:T(4,128)(2,1)S(1)} %bitcast.23), channel_id=1, replica_groups=mesh['tm_0'=4,'tm_1'=2,'tm_2'=2,'cell_0'=8,'cell_1'=4] {'tm_0','cell_0',..., dimensions={0} | all-to-all | bytes 262144 | tf_op jit(solution)/shard_map/all_to_all | solution.py:261
  99.6 0.0 copy-done.10
  99.6 0.4 convolution_convert_fusion
  100.0 3.4 %all-gather = bf16[2048,128]{1,0:T(8,128)(2,1)S(1)} all-gather(bf16[1024,128]{1,0:T(8,128)(2,1)S(1)} %convolution_convert_fusion), channel_id=2, replica_groups=mesh['tm_0'=4,'tm_1'=2,'tm_2'=2,'cell_0'=8,'cell_1'=4] {'tm_2'}, dimensions={0}, use_global_device_ids=true | all-gather | bytes 786432 | tf_op jit(solution)/shard_map/all_gather | solution.py:298
  103.5 0.5 fusion
  103.9 24.4 %all_to_all.28 = bf16[256,4,128]{2,1,0:T(4,128)(2,1)S(1)} all-to-all(bf16[256,4,128]{2,1,0:T(4,128)(2,1)S(1)} %bitcast.32), channel_id=1, replica_groups=mesh['tm_0'=4,'tm_1'=2,'tm_2'=2,'cell_0'=8,'cell_1'=4] {'tm_0','tm_1','c..., dimensions={0} | all-to-all | bytes 524288 | tf_op jit(solution)/shard_map/all_to_all | solution.py:261
  128.3 0.9 convert_reduce_fusion
  (9 shorter events, 0.1 us)
Async XLA Ops:
  0.0 45.2 %copy-start.1 = (s32[2048]{0:T(1024)S(1)}, s32[2048]{0:T(1024)}, u32[]{:S(2)}) copy-start(s32[2048]{0:T(1024)} %param.16) | copy-start | bytes 24580
  0.0 45.2 %copy-start = (bf16[2048,1,512]{2,0,1:T(8,128)(2,1)S(1)}, bf16[2048,1,512]{2,0,1:T(8,128)(2,1)}, u32[]{:S(2)}) copy-start(bf16[2048,1,512]{2,0,1:T(8,128)(2,1)} %param.12) | copy-start | bytes 6291460
  39.7 16.2 %copy-start.2 = (s32[2048]{0:T(1024)S(1)}, s32[2048]{0:T(1024)}, u32[]{:S(2)}) copy-start(s32[2048]{0:T(1024)} %param.17) | copy-start | bytes 24580
  46.8 23.9 %all-to-all-start.2 = ((bf16[256,4,128]{2,1,0:T(4,128)(2,1)}), bf16[256,4,128]{2,1,0:T(4,128)(2,1)S(1)}, u32[]{:S(2)}, u32[]{:S(2)}) async-start(bf16[256,4,128]{2,1,0:T(4,128)(2,1)} %bitcast.8), calls=%async_computation.2 | async-start | bytes 524288 | tf_op jit(solution)/shard_map/all_to_all | solution.py:261
  56.0 18.3 %copy-start.3 = (f32[16,16]{1,0:T(8,128)S(1)}, f32[16,16]{1,0:T(8,128)}, u32[]{:S(2)}) copy-start(f32[16,16]{1,0:T(8,128)} %weight_ref.1) | copy-start | bytes 3076
  56.0 18.3 %copy-start.4 = (f32[256,256]{1,0:T(8,128)S(1)}, f32[256,256]{1,0:T(8,128)}, u32[]{:S(2)}) copy-start(f32[256,256]{1,0:T(8,128)} %constant.38.clone.eigen_ref) | copy-start | bytes 786436
  56.0 18.3 %copy-start.5 = (bf16[256,256]{1,0:T(8,128)(2,1)S(1)}, bf16[256,256]{1,0:T(8,128)(2,1)}, u32[]{:S(2)}) copy-start(bf16[256,256]{1,0:T(8,128)(2,1)} %constant.37.clone.basis_wide) | copy-start | bytes 393220
  56.0 18.3 %copy-start.6 = (bf16[256,256]{1,0:T(8,128)(2,1)S(1)}, bf16[256,256]{1,0:T(8,128)(2,1)}, u32[]{:S(2)}) copy-start(bf16[256,256]{1,0:T(8,128)(2,1)} %constant.35.clone.basis_twice) | copy-start | bytes 393220
  56.0 18.3 %copy-start.7 = (bf16[256,256]{1,0:T(8,128)(2,1)S(1)}, bf16[256,256]{1,0:T(8,128)(2,1)}, u32[]{:S(2)}) copy-start(bf16[256,256]{1,0:T(8,128)(2,1)} %constant.34.clone.side_tall.side_both) | copy-start | bytes 393220
  56.0 18.3 %copy-start.8 = (bf16[256,128]{1,0:T(8,128)(2,1)S(1)}, bf16[256,128]{1,0:T(8,128)(2,1)}, u32[]{:S(2)}) copy-start(bf16[256,128]{1,0:T(8,128)(2,1)} %constant.36.clone.basis_low) | copy-start | bytes 196612
  60.7 1.3 %copy-start.9 = (bf16[2048,512]{1,0:T(8,128)(2,1)}, bf16[2048,512]{1,0:T(8,128)(2,1)S(1)}, u32[]{:S(2)}) copy-start(bf16[2048,512]{1,0:T(8,128)(2,1)S(1)} %shard_map.120) | copy-start | bytes 6291460
  74.3 25.3 %copy-start.10 = (bf16[2048,512]{1,0:T(8,128)(2,1)S(1)}, bf16[2048,512]{1,0:T(8,128)(2,1)}, u32[]{:S(2)}) copy-start(bf16[2048,512]{1,0:T(8,128)(2,1)} %copy-done.9) | copy-start | bytes 6291460

commit v8 on v7

--- a/solution.py
+++ b/solution.py
@@ -75,6 +75,8 @@
     which = which_ref[0]
     strides = times // kept
 
+    picked = [weight_ref[pl.ds(s * strides + which, 1), :] for s in range(kept)]
+
     def mix(j, carry):
         rows = pl.ds(pl.multiple_of(j * 32, 32), 32)
         totals = [None] * kept
@@ -82,7 +84,7 @@
             t = (k % (times // pair)) * pair + k // (times // pair)
             value = field_ref[k, rows, :].astype(F32)
             for s in range(kept):
-                term = weight_ref[s * strides + which, t] * value
+                term = jnp.broadcast_to(picked[s][:, t : t + 1], value.shape) * value
                 totals[s] = term if k == 0 else totals[s] + term
         for s in range(kept):
             mixed[s, rows, :] = totals[s].astype(BF16).astype(F32)
@@ -169,7 +171,7 @@
     return pl.pallas_call(
         functools.partial(spatial_kernel, 64, kept),
         out_shape=jax.ShapeDtypeStruct((kept * chunks, GRID), BF16),
-        in_specs=[SMEM] * 2 + [VMEM] * (3 + len(constants)),
+        in_specs=[SMEM] + [VMEM] * (4 + len(constants)),
         out_specs=VMEM,
         scratch_shapes=[
             pltpu.VMEM((kept, chunks, GRID), F32),
@@ -195,6 +197,7 @@
         out_shape=jax.ShapeDtypeStruct((count, rows, GRID), BF16),
         in_specs=[SMEM, VMEM, VMEM],
         out_specs=VMEM,
+        compiler_params=pltpu.CompilerParams(vmem_limit_bytes=2 << 20),
     )(half, duals, coords)
 
 

time: 130 us -> 129 us (level)
  Pallas kernels: 15.9 us -> 14.1 us
  local copies, waits for them, and re-layouts: 1.43 us -> 2.95 us
    unnamed x22 -> x26, local copies, waits for them, and re-layouts: 1.38 us -> 2.9 us
    pallas_call x1, Pallas kernels: 1.52 us -> 0.02 us  [opening(): pl.pallas_call(opening_kernel, out_shape=jax.ShapeDtypeStruct((count, row...]
where the time goes in v8:
time: 129 us
  blocking collectives  91.9 us (71%)
  Pallas kernels  14.1 us (11%)
  starting transfers between devices  9.12 us (7%)
  waiting for transfers between devices  8.6 us (7%)
  local copies, waits for them, and re-layouts  2.95 us (2%)
    all_to_all x4, blocking collectives, exchange(): return lax.all_to_all(pieces, axes, split_axis=0, concat_axis=0, tiled=True)  79.4 us
    all_to_all x1, starting transfers between devices, exchange(): return lax.all_to_all(pieces, axes, split_axis=0, concat_axis=0, tiled=True)  9.12 us
    all_to_all x1, waiting for transfers between devices, exchange(): return lax.all_to_all(pieces, axes, split_axis=0, concat_axis=0, tiled=True)  8.6 us
    pallas_call x1, Pallas kernels, spatial(): pl.pallas_call(functools.partial(spatial_kernel, 64, kept), out_shape=jax...  7.85 us
    all_gather x1, blocking collectives, per_device(): third = lax.all_gather(second.reshape(nx * nh, -1, reals), CO, axis=0)  5.43 us
    pallas_call x1, Pallas kernels, picking(): pl.pallas_call(picking_kernel, out_shape=jax.ShapeDtypeStruct(flat.shape,...  4.64 us
    all_gather x1, blocking collectives, per_device(): lax.all_gather(field.reshape(nx * nh, -1, GRID), CO, axis=0, tiled=True)  3.68 us
    all_gather x1, blocking collectives, per_device(): swapped = lax.all_gather(theirs.astype(BF16), CO, axis=0)  3.41 us
  transfers between devices with their start and end apart: 1, of which 1 were waited for; matrix products, arithmetic and copies ran while one was open for 0% of the time, Pallas kernels for 4%

profile of v8, /device:TPU:1, one launch (start us, length us, event | category | flops | bytes accessed | tf_op | source)
XLA Modules:
  0.0 128.7 jit_solution(2897585472683361777)
XLA Ops:
  0.0 0.8 copy-done.2
  0.8 0.7 copy-done.3
  1.5 28.5 %all_to_all.25 = bf16[64,8,128]{2,1,0:T(8,128)(2,1)S(1)} all-to-all(bf16[64,8,128]{2,1,0:T(8,128)(2,1)S(1)} %shard_map.118), channel_id=1, replica_groups=mesh['tm_0'=4,'tm_1'=2,'tm_2'=2,'cell_0'=8,'cell_1'=4] {'tm_1','cell_0',..., dimensions={0} | all-to-all | bytes 262144 | tf_op jit(solution)/shard_map/all_to_all | solution.py:264
  30.1 0.1 slice_convert_fusion
  30.2 9.3 %all_to_all.26 = bf16[4,256,128]{2,1,0:T(8,128)(2,1)S(1)} all-to-all(bf16[4,256,128]{2,1,0:T(8,128)(2,1)S(1)} %broadcast_in_dim.3), channel_id=1, replica_groups=mesh['tm_0'=4,'tm_1'=2,'tm_2'=2,'cell_0'=8,'cell_1'=4] {'tm_0'}, dimensions={0} | all-to-all | bytes 524288 | tf_op jit(solution)/shard_map/all_to_all | solution.py:264
  39.5 5.4 %all_gather.12.duals_ref = bf16[2,8,128,128]{3,2,1,0:T(8,128)(2,1)S(1)} all-gather(bf16[1,8,128,128]{3,2,1,0:T(8,128)(2,1)S(1)} %bitcast.30), channel_id=1, replica_groups=mesh['tm_0'=4,'tm_1'=2,'tm_2'=2,'cell_0'=8,'cell_1'=4] {'tm_2'}, dimensions={0}, use_global_device_ids=true | all-gather | bytes 786432 | tf_op jit(solution)/shard_map/all_gather | solution.py:287
  45.0 0.0 copy-done.1
  45.0 0.0 copy-done
  45.0 1.6 %shard_map.119 = bf16[4,2,32,4,128]{4,3,2,1,0:T(4,128)(2,1)} custom-call(s32[1]{0:T(128)} %bitcast.1.here_ref, s32[16,128]{1,0:T(8,128)S(1)} %bitcast.26, bf16[2,8,128,128]{3,2,1,0:T(8,128)(2,1)S(1)} %all_gather.12.duals_ref, bf16[2048,512]{1,0:T(8,128)(2,1)S(1)} %bitcast.21), custom_call_target="tpu_custom_call" | custom-call | tf_op jit(solution)/shard_map/pallas_call | solution.py:254
  46.6 9.1 %all-to-all-start.2 = ((bf16[256,4,128]{2,1,0:T(4,128)(2,1)}), bf16[256,4,128]{2,1,0:T(4,128)(2,1)S(1)}, u32[]{:S(2)}, u32[]{:S(2)}) async-start(bf16[256,4,128]{2,1,0:T(4,128)(2,1)} %bitcast.8), calls=%async_computation.2 | async-start | bytes 524288 | tf_op jit(solution)/shard_map/all_to_all | solution.py:264
  55.7 0.0 copy-done.4
  55.8 0.0 copy-start.5
  55.8 0.0 copy-start.6
  55.8 0.0 copy-start.7
  55.8 0.0 copy-start.8
  55.8 0.0 copy-start.9
  55.8 0.0 copy-start.10
  55.8 4.6 %shard_map.120 = bf16[2048,512]{1,0:T(8,128)(2,1)S(1)} custom-call(s32[1]{0:T(128)} %bitcast.1.here_ref, s32[1]{0:T(128)} %bitcast.2.core_ref, s32[16,128]{1,0:T(8,128)S(1)} %bitcast.28, s32[16,128]{1,0:T(8,128)S(1)} %bitcast.27, bf16[2048,512]{1,0:T(8,128)(2,1)S(1)} %bitcast.22), custom_call_target="tpu_custom_call" | custom-call | flops 4294967296 | bytes 4194304 | tf_op jit(solution)/shard_map/pallas_call | solution.py:225
  60.5 1.3 %copy-done.11 = bf16[2048,512]{1,0:T(8,128)(2,1)} copy-done((bf16[2048,512]{1,0:T(8,128)(2,1)}, bf16[2048,512]{1,0:T(8,128)(2,1)S(1)}, u32[]{:S(2)}) %copy-start.11) | copy-done | bytes 2097176
  61.8 8.6 %all-to-all-done.2 = bf16[256,4,128]{2,1,0:T(4,128)(2,1)S(1)} async-done(((bf16[256,4,128]{2,1,0:T(4,128)(2,1)}), bf16[256,4,128]{2,1,0:T(4,128)(2,1)S(1)}, u32[]{:S(2)}, u32[]{:S(2)}) %all-to-all-start.2) | async-done | bytes 262176 | tf_op jit(solution)/shard_map/all_to_all | solution.py:264
  70.4 3.7 %all_gather.13.field_ref = bf16[16,128,128]{2,1,0:T(8,128)(2,1)S(1)} all-gather(bf16[8,128,128]{2,1,0:T(8,128)(2,1)S(1)} %bitcast.29), channel_id=1, replica_groups=mesh['tm_0'=4,'tm_1'=2,'tm_2'=2,'cell_0'=8,'cell_1'=4] {'tm_2'}, dimensions={0}, use_global_device_ids=true | all-gather | bytes 786432 | tf_op jit(solution)/shard_map/all_gather | solution.py:293
  74.1 0.0 copy-done.8
  74.1 0.0 copy-done.9
  74.1 0.0 copy-done.10
  74.1 0.0 copy-start.12
  74.1 7.8 %shard_map.121 = bf16[512,128]{1,0:T(8,128)(2,1)S(1)} custom-call(s32[1]{0:T(128)} %bitcast.3.which_ref, f32[16,16]{1,0:T(8,128)S(1)} %copy-done.5, bf16[16,128,128]{2,1,0:T(8,128)(2,1)S(1)} %all_gather.13.field_ref, s32[128,128]{1,0:T(8,128)S(1)} %bitcast.25, s32[128,128]{1,0:T(8,128)S(1)} %bitcast.24, bf16[256,256]{1,0:T(8,128)(2,1)S(1)} %copy-done.9, ...), custom_call_target="tpu_custom_call" | custom-call | flops 10000000000 | bytes 18874368 | tf_op jit(solution)/shard_map/pallas_call | solution.py:171
  82.0 17.2 %all_to_all.27 = bf16[128,4,128]{2,1,0:T(4,128)(2,1)S(1)} all-to-all(bf16[128,4,128]{2,1,0:T(4,128)(2,1)S(1)} %bitcast.23), channel_id=1, replica_groups=mesh['tm_0'=4,'tm_1'=2,'tm_2'=2,'cell_0'=8,'cell_1'=4] {'tm_0','cell_0',..., dimensions={0} | all-to-all | bytes 262144 | tf_op jit(solution)/shard_map/all_to_all | solution.py:264
  99.2 0.4 convolution_convert_fusion
  99.6 3.4 %all-gather = bf16[2048,128]{1,0:T(8,128)(2,1)S(1)} all-gather(bf16[1024,128]{1,0:T(8,128)(2,1)S(1)} %convolution_convert_fusion), channel_id=2, replica_groups=mesh['tm_0'=4,'tm_1'=2,'tm_2'=2,'cell_0'=8,'cell_1'=4] {'tm_2'}, dimensions={0}, use_global_device_ids=true | all-gather | bytes 786432 | tf_op jit(solution)/shard_map/all_gather | solution.py:301
  103.0 0.5 fusion
  103.5 24.4 %all_to_all.28 = bf16[256,4,128]{2,1,0:T(4,128)(2,1)S(1)} all-to-all(bf16[256,4,128]{2,1,0:T(4,128)(2,1)S(1)} %bitcast.32), channel_id=1, replica_groups=mesh['tm_0'=4,'tm_1'=2,'tm_2'=2,'cell_0'=8,'cell_1'=4] {'tm_0','tm_1','c..., dimensions={0} | all-to-all | bytes 524288 | tf_op jit(solution)/shard_map/all_to_all | solution.py:264
  127.8 0.9 convert_reduce_fusion
  (13 shorter events, 0.1 us)
Async XLA Ops:
  0.0 45.0 %copy-start.1 = (s32[2048]{0:T(1024)S(1)}, s32[2048]{0:T(1024)}, u32[]{:S(2)}) copy-start(s32[2048]{0:T(1024)} %param.16) | copy-start | bytes 24580
  0.0 45.0 %copy-start = (bf16[2048,1,512]{2,0,1:T(8,128)(2,1)S(1)}, bf16[2048,1,512]{2,0,1:T(8,128)(2,1)}, u32[]{:S(2)}) copy-start(bf16[2048,1,512]{2,0,1:T(8,128)(2,1)} %param.12) | copy-start | bytes 6291460
  0.0 0.8 copy-start.2
  0.8 0.7 copy-start.3
  39.5 16.2 %copy-start.4 = (s32[2048]{0:T(1024)S(1)}, s32[2048]{0:T(1024)}, u32[]{:S(2)}) copy-start(s32[2048]{0:T(1024)} %param.17) | copy-start | bytes 24580
  46.6 23.8 %all-to-all-start.2 = ((bf16[256,4,128]{2,1,0:T(4,128)(2,1)}), bf16[256,4,128]{2,1,0:T(4,128)(2,1)S(1)}, u32[]{:S(2)}, u32[]{:S(2)}) async-start(bf16[256,4,128]{2,1,0:T(4,128)(2,1)} %bitcast.8), calls=%async_computation.2 | async-start | bytes 524288 | tf_op jit(solution)/shard_map/all_to_all | solution.py:264
  55.8 18.3 %copy-start.5 = (f32[16,16]{1,0:T(8,128)S(1)}, f32[16,16]{1,0:T(8,128)}, u32[]{:S(2)}) copy-start(f32[16,16]{1,0:T(8,128)} %weight_ref.1) | copy-start | bytes 3076
  55.8 18.3 %copy-start.6 = (f32[256,256]{1,0:T(8,128)S(1)}, f32[256,256]{1,0:T(8,128)}, u32[]{:S(2)}) copy-start(f32[256,256]{1,0:T(8,128)} %constant.38.clone.eigen_ref) | copy-start | bytes 786436
  55.8 18.3 %copy-start.7 = (bf16[256,256]{1,0:T(8,128)(2,1)S(1)}, bf16[256,256]{1,0:T(8,128)(2,1)}, u32[]{:S(2)}) copy-start(bf16[256,256]{1,0:T(8,128)(2,1)} %constant.37.clone.basis_wide) | copy-start | bytes 393220
  55.8 18.3 %copy-start.8 = (bf16[256,256]{1,0:T(8,128)(2,1)S(1)}, bf16[256,256]{1,0:T(8,128)(2,1)}, u32[]{:S(2)}) copy-start(bf16[256,256]{1,0:T(8,128)(2,1)} %constant.35.clone.basis_twice) | copy-start | bytes 393220
  55.8 18.3 %copy-start.9 = (bf16[256,256]{1,0:T(8,128)(2,1)S(1)}, bf16[256,256]{1,0:T(8,128)(2,1)}, u32[]{:S(2)}) copy-start(bf16[256,256]{1,0:T(8,128)(2,1)} %constant.34.clone.side_tall.side_both) | copy-start | bytes 393220
  55.8 18.3 %copy-start.10 = (bf16[256,128]{1,0:T(8,128)(2,1)S(1)}, bf16[256,128]{1,0:T(8,128)(2,1)}, u32[]{:S(2)}) copy-start(bf16[256,128]{1,0:T(8,128)(2,1)} %constant.36.clone.basis_low) | copy-start | bytes 196612
  60.5 1.3 %copy-start.11 = (bf16[2048,512]{1,0:T(8,128)(2,1)}, bf16[2048,512]{1,0:T(8,128)(2,1)S(1)}, u32[]{:S(2)}) copy-start(bf16[2048,512]{1,0:T(8,128)(2,1)S(1)} %shard_map.120) | copy-start | bytes 6291460
  74.1 25.0 %copy-start.12 = (bf16[2048,512]{1,0:T(8,128)(2,1)S(1)}, bf16[2048,512]{1,0:T(8,128)(2,1)}, u32[]{:S(2)}) copy-start(bf16[2048,512]{1,0:T(8,128)(2,1)} %copy-done.11) | copy-start | bytes 6291460

commit v9 on v8

--- a/solution.py
+++ b/solution.py
@@ -232,7 +232,7 @@
     )(here, core, obs_owner.reshape(-1, GRID), obs_time.reshape(-1, GRID), flat)
 
 
-def adjoint_kernel(here_ref, time_ref, duals_ref, flat_ref, out_ref):
+def adjoint_kernel(here_ref, time_ref, duals_ref, flat_ref, out_ref, held, sent):
     pair, groups, rows, reals = duals_ref.shape
     outer, again, part, folds, _ = out_ref.shape
     keep = jnp.where(time_ref[...] >= here_ref[0], 1.0, 0.0).T
@@ -243,10 +243,14 @@
     total = lax.dot_general(
         jnp.concatenate(seen, axis=0), flat_ref[...], (((0,), (0,)), ((), ())), preferred_element_type=F32
     )
-    pieces = total.reshape(reals, folds, GRID).astype(BF16)
+    copies_out = []
     for i in range(outer):
+        held[i] = total[i * part : (i + 1) * part].reshape(part, folds, GRID).astype(BF16)
         for j in range(again):
-            out_ref[i, j] = pieces[i * part : (i + 1) * part]
+            copies_out.append(pltpu.make_async_copy(held.at[i], out_ref.at[i, j], sent.at[i, j]))
+            copies_out[-1].start()
+    for copy in copies_out:
+        copy.wait()
 
 
 def adjoint(here, obs_time, duals, flat, outer, again):
@@ -255,7 +259,11 @@
         adjoint_kernel,
         out_shape=jax.ShapeDtypeStruct((outer, again, reals // outer, flat.shape[1] // GRID, GRID), BF16),
         in_specs=[SMEM] + [VMEM] * 3,
-        out_specs=VMEM,
+        out_specs=pl.BlockSpec(memory_space=pl.ANY),
+        scratch_shapes=[
+            pltpu.VMEM((outer, reals // outer, flat.shape[1] // GRID, GRID), BF16),
+            pltpu.SemaphoreType.DMA((outer, again)),
+        ],
         compiler_params=pltpu.CompilerParams(vmem_limit_bytes=24 << 20),
     )(here, obs_time.reshape(-1, rows), duals, flat)
 

time: 129 us -> 129 us (level)
  no operation moved by 1% of the time
where the time goes in v9:
time: 129 us
  blocking collectives  91.9 us (71%)
  Pallas kernels  14.2 us (11%)
  starting transfers between devices  9.13 us (7%)
  waiting for transfers between devices  8.6 us (7%)
  local copies, waits for them, and re-layouts  2.95 us (2%)
    all_to_all x4, blocking collectives, exchange(): return lax.all_to_all(pieces, axes, split_axis=0, concat_axis=0, tiled=True)  79.4 us
    all_to_all x1, starting transfers between devices, exchange(): return lax.all_to_all(pieces, axes, split_axis=0, concat_axis=0, tiled=True)  9.13 us
    all_to_all x1, waiting for transfers between devices, exchange(): return lax.all_to_all(pieces, axes, split_axis=0, concat_axis=0, tiled=True)  8.6 us
    pallas_call x1, Pallas kernels, spatial(): pl.pallas_call(functools.partial(spatial_kernel, 64, kept), out_shape=jax...  7.86 us
    all_gather x1, blocking collectives, per_device(): third = lax.all_gather(second.reshape(nx * nh, -1, reals), CO, axis=0)  5.43 us
    pallas_call x1, Pallas kernels, picking(): pl.pallas_call(picking_kernel, out_shape=jax.ShapeDtypeStruct(flat.shape,...  4.64 us
    all_gather x1, blocking collectives, per_device(): lax.all_gather(field.reshape(nx * nh, -1, GRID), CO, axis=0, tiled=True)  3.68 us
    all_gather x1, blocking collectives, per_device(): swapped = lax.all_gather(theirs.astype(BF16), CO, axis=0)  3.42 us
  transfers between devices with their start and end apart: 1, of which 1 were waited for; matrix products, arithmetic and copies ran while one was open for 0% of the time, Pallas kernels for 4%

profile of v9, /device:TPU:1, one launch (start us, length us, event | category | flops | bytes accessed | tf_op | source)
XLA Modules:
  0.0 128.7 jit_solution(5569059366120330303)
XLA Ops:
  0.0 0.8 copy-done.2
  0.8 0.7 copy-done.3
  1.5 28.5 %all_to_all.25 = bf16[64,8,128]{2,1,0:T(8,128)(2,1)S(1)} all-to-all(bf16[64,8,128]{2,1,0:T(8,128)(2,1)S(1)} %shard_map.118), channel_id=1, replica_groups=mesh['tm_0'=4,'tm_1'=2,'tm_2'=2,'cell_0'=8,'cell_1'=4] {'tm_1','cell_0',..., dimensions={0} | all-to-all | bytes 262144 | tf_op jit(solution)/shard_map/all_to_all | solution.py:272
  30.1 0.1 slice_convert_fusion
  30.2 9.3 %all_to_all.26 = bf16[4,256,128]{2,1,0:T(8,128)(2,1)S(1)} all-to-all(bf16[4,256,128]{2,1,0:T(8,128)(2,1)S(1)} %broadcast_in_dim.3), channel_id=1, replica_groups=mesh['tm_0'=4,'tm_1'=2,'tm_2'=2,'cell_0'=8,'cell_1'=4] {'tm_0'}, dimensions={0} | all-to-all | bytes 524288 | tf_op jit(solution)/shard_map/all_to_all | solution.py:272
  39.5 5.4 %all_gather.12.duals_ref = bf16[2,8,128,128]{3,2,1,0:T(8,128)(2,1)S(1)} all-gather(bf16[1,8,128,128]{3,2,1,0:T(8,128)(2,1)S(1)} %bitcast.30), channel_id=1, replica_groups=mesh['tm_0'=4,'tm_1'=2,'tm_2'=2,'cell_0'=8,'cell_1'=4] {'tm_2'}, dimensions={0}, use_global_device_ids=true | all-gather | bytes 786432 | tf_op jit(solution)/shard_map/all_gather | solution.py:295
  45.0 0.0 copy-done.1
  45.0 0.0 copy-done
  45.0 1.6 %shard_map.119 = bf16[4,2,32,4,128]{4,3,2,1,0:T(4,128)(2,1)} custom-call(s32[1]{0:T(128)} %bitcast.1.here_ref, s32[16,128]{1,0:T(8,128)S(1)} %bitcast.26, bf16[2,8,128,128]{3,2,1,0:T(8,128)(2,1)S(1)} %all_gather.12.duals_ref, bf16[2048,512]{1,0:T(8,128)(2,1)S(1)} %bitcast.21), custom_call_target="tpu_custom_call" | custom-call | tf_op jit(solution)/shard_map/pallas_call | solution.py:258
  46.6 9.1 %all-to-all-start.2 = ((bf16[256,4,128]{2,1,0:T(4,128)(2,1)}), bf16[256,4,128]{2,1,0:T(4,128)(2,1)S(1)}, u32[]{:S(2)}, u32[]{:S(2)}) async-start(bf16[256,4,128]{2,1,0:T(4,128)(2,1)} %bitcast.8), calls=%async_computation.2 | async-start | bytes 524288 | tf_op jit(solution)/shard_map/all_to_all | solution.py:272
  55.8 0.0 copy-done.4
  55.8 0.0 copy-start.5
  55.8 0.0 copy-start.6
  55.8 0.0 copy-start.7
  55.8 0.0 copy-start.8
  55.8 0.0 copy-start.9
  55.8 0.0 copy-start.10
  55.9 4.6 %shard_map.120 = bf16[2048,512]{1,0:T(8,128)(2,1)S(1)} custom-call(s32[1]{0:T(128)} %bitcast.1.here_ref, s32[1]{0:T(128)} %bitcast.2.core_ref, s32[16,128]{1,0:T(8,128)S(1)} %bitcast.28, s32[16,128]{1,0:T(8,128)S(1)} %bitcast.27, bf16[2048,512]{1,0:T(8,128)(2,1)S(1)} %bitcast.22), custom_call_target="tpu_custom_call" | custom-call | flops 4294967296 | bytes 4194304 | tf_op jit(solution)/shard_map/pallas_call | solution.py:225
  60.5 0.0 copy-start.11
  60.5 1.3 %copy-done.11 = bf16[2048,512]{1,0:T(8,128)(2,1)} copy-done((bf16[2048,512]{1,0:T(8,128)(2,1)}, bf16[2048,512]{1,0:T(8,128)(2,1)S(1)}, u32[]{:S(2)}) %copy-start.11) | copy-done | bytes 2097176
  61.9 8.6 %all-to-all-done.2 = bf16[256,4,128]{2,1,0:T(4,128)(2,1)S(1)} async-done(((bf16[256,4,128]{2,1,0:T(4,128)(2,1)}), bf16[256,4,128]{2,1,0:T(4,128)(2,1)S(1)}, u32[]{:S(2)}, u32[]{:S(2)}) %all-to-all-start.2) | async-done | bytes 262176 | tf_op jit(solution)/shard_map/all_to_all | solution.py:272
  70.4 3.7 %all_gather.13.field_ref = bf16[16,128,128]{2,1,0:T(8,128)(2,1)S(1)} all-gather(bf16[8,128,128]{2,1,0:T(8,128)(2,1)S(1)} %bitcast.29), channel_id=1, replica_groups=mesh['tm_0'=4,'tm_1'=2,'tm_2'=2,'cell_0'=8,'cell_1'=4] {'tm_2'}, dimensions={0}, use_global_device_ids=true | all-gather | bytes 786432 | tf_op jit(solution)/shard_map/all_gather | solution.py:301
  74.1 0.0 copy-done.5
  74.1 0.0 copy-done.6
  74.1 0.0 copy-done.7
  74.2 7.9 %shard_map.121 = bf16[512,128]{1,0:T(8,128)(2,1)S(1)} custom-call(s32[1]{0:T(128)} %bitcast.3.which_ref, f32[16,16]{1,0:T(8,128)S(1)} %copy-done.5, bf16[16,128,128]{2,1,0:T(8,128)(2,1)S(1)} %all_gather.13.field_ref, s32[128,128]{1,0:T(8,128)S(1)} %bitcast.25, s32[128,128]{1,0:T(8,128)S(1)} %bitcast.24, bf16[256,256]{1,0:T(8,128)(2,1)S(1)} %copy-done.9, ...), custom_call_target="tpu_custom_call" | custom-call | flops 10000000000 | bytes 18874368 | tf_op jit(solution)/shard_map/pallas_call | solution.py:171
  82.0 17.1 %all_to_all.27 = bf16[128,4,128]{2,1,0:T(4,128)(2,1)S(1)} all-to-all(bf16[128,4,128]{2,1,0:T(4,128)(2,1)S(1)} %bitcast.23), channel_id=1, replica_groups=mesh['tm_0'=4,'tm_1'=2,'tm_2'=2,'cell_0'=8,'cell_1'=4] {'tm_0','cell_0',..., dimensions={0} | all-to-all | bytes 262144 | tf_op jit(solution)/shard_map/all_to_all | solution.py:272
  99.2 0.4 convolution_convert_fusion
  99.6 3.4 %all-gather = bf16[2048,128]{1,0:T(8,128)(2,1)S(1)} all-gather(bf16[1024,128]{1,0:T(8,128)(2,1)S(1)} %convolution_convert_fusion), channel_id=2, replica_groups=mesh['tm_0'=4,'tm_1'=2,'tm_2'=2,'cell_0'=8,'cell_1'=4] {'tm_2'}, dimensions={0}, use_global_device_ids=true | all-gather | bytes 786432 | tf_op jit(solution)/shard_map/all_gather | solution.py:309
  103.0 0.5 fusion
  103.5 24.4 %all_to_all.28 = bf16[256,4,128]{2,1,0:T(4,128)(2,1)S(1)} all-to-all(bf16[256,4,128]{2,1,0:T(4,128)(2,1)S(1)} %bitcast.32), channel_id=1, replica_groups=mesh['tm_0'=4,'tm_1'=2,'tm_2'=2,'cell_0'=8,'cell_1'=4] {'tm_0','tm_1','c..., dimensions={0} | all-to-all | bytes 524288 | tf_op jit(solution)/shard_map/all_to_all | solution.py:272
  127.9 0.9 convert_reduce_fusion
  (13 shorter events, 0.1 us)
Async XLA Ops:
  0.0 45.0 %copy-start.1 = (s32[2048]{0:T(1024)S(1)}, s32[2048]{0:T(1024)}, u32[]{:S(2)}) copy-start(s32[2048]{0:T(1024)} %param.16) | copy-start | bytes 24580
  0.0 45.0 %copy-start = (bf16[2048,1,512]{2,0,1:T(8,128)(2,1)S(1)}, bf16[2048,1,512]{2,0,1:T(8,128)(2,1)}, u32[]{:S(2)}) copy-start(bf16[2048,1,512]{2,0,1:T(8,128)(2,1)} %param.12) | copy-start | bytes 6291460
  0.0 0.8 copy-start.2
  0.8 0.7 copy-start.3
  39.5 16.2 %copy-start.4 = (s32[2048]{0:T(1024)S(1)}, s32[2048]{0:T(1024)}, u32[]{:S(2)}) copy-start(s32[2048]{0:T(1024)} %param.17) | copy-start | bytes 24580
  46.6 23.8 %all-to-all-start.2 = ((bf16[256,4,128]{2,1,0:T(4,128)(2,1)}), bf16[256,4,128]{2,1,0:T(4,128)(2,1)S(1)}, u32[]{:S(2)}, u32[]{:S(2)}) async-start(bf16[256,4,128]{2,1,0:T(4,128)(2,1)} %bitcast.8), calls=%async_computation.2 | async-start | bytes 524288 | tf_op jit(solution)/shard_map/all_to_all | solution.py:272
  55.8 18.3 %copy-start.5 = (f32[16,16]{1,0:T(8,128)S(1)}, f32[16,16]{1,0:T(8,128)}, u32[]{:S(2)}) copy-start(f32[16,16]{1,0:T(8,128)} %weight_ref.1) | copy-start | bytes 3076
  55.8 18.3 %copy-start.6 = (f32[256,256]{1,0:T(8,128)S(1)}, f32[256,256]{1,0:T(8,128)}, u32[]{:S(2)}) copy-start(f32[256,256]{1,0:T(8,128)} %constant.38.clone.eigen_ref) | copy-start | bytes 786436
  55.8 18.3 %copy-start.7 = (bf16[256,256]{1,0:T(8,128)(2,1)S(1)}, bf16[256,256]{1,0:T(8,128)(2,1)}, u32[]{:S(2)}) copy-start(bf16[256,256]{1,0:T(8,128)(2,1)} %constant.37.clone.basis_wide) | copy-start | bytes 393220
  55.8 18.3 %copy-start.8 = (bf16[256,256]{1,0:T(8,128)(2,1)S(1)}, bf16[256,256]{1,0:T(8,128)(2,1)}, u32[]{:S(2)}) copy-start(bf16[256,256]{1,0:T(8,128)(2,1)} %constant.35.clone.basis_twice) | copy-start | bytes 393220
  55.8 18.3 %copy-start.9 = (bf16[256,256]{1,0:T(8,128)(2,1)S(1)}, bf16[256,256]{1,0:T(8,128)(2,1)}, u32[]{:S(2)}) copy-start(bf16[256,256]{1,0:T(8,128)(2,1)} %constant.34.clone.side_tall.side_both) | copy-start | bytes 393220
  55.8 18.3 %copy-start.10 = (bf16[256,128]{1,0:T(8,128)(2,1)S(1)}, bf16[256,128]{1,0:T(8,128)(2,1)}, u32[]{:S(2)}) copy-start(bf16[256,128]{1,0:T(8,128)(2,1)} %constant.36.clone.basis_low) | copy-start | bytes 196612
  60.5 1.3 %copy-start.11 = (bf16[2048,512]{1,0:T(8,128)(2,1)}, bf16[2048,512]{1,0:T(8,128)(2,1)S(1)}, u32[]{:S(2)}) copy-start(bf16[2048,512]{1,0:T(8,128)(2,1)S(1)} %shard_map.120) | copy-start | bytes 6291460
  74.2 25.0 %copy-start.12 = (bf16[2048,512]{1,0:T(8,128)(2,1)S(1)}, bf16[2048,512]{1,0:T(8,128)(2,1)}, u32[]{:S(2)}) copy-start(bf16[2048,512]{1,0:T(8,128)(2,1)} %copy-done.11) | copy-start | bytes 6291460
